TPU v7x, 32 devices: a whole 2x2x4 slice. The times are simulated.
32 devices in a mesh: seq: 8 (over y, x, core), fsdp: 4 (over z).
Axes of the slice: x: 2, y: 2, z: 4, core: 2. Of those that a mesh axis runs over, the one named last changes fastest.
Arguments:
- hidden_in: bfloat16 [4, 1024, 2048], P('fsdp', 'seq'), may hold values from -6 to 6
- positions: int32 [4, 1024], P('fsdp'), may hold values from 0 to 1535, as said below
- norm1_gain: bfloat16 [2048], P(('seq', 'fsdp')), may hold values from 0.25 to 1.75
- norm1_shift: bfloat16 [2048], P(('seq', 'fsdp')), may hold values from -3 to 3
- w_qkv: bfloat16 [2048, 6144], P(('seq', 'fsdp')), may hold values from -0.125 to 0.125
- b_qkv: bfloat16 [6144], P(('seq', 'fsdp')), may hold values from -3 to 3
- w_out: bfloat16 [2048, 2048], P(('seq', 'fsdp')), may hold values from -4 to 4
- norm2_gain: bfloat16 [2048], P(('seq', 'fsdp')), may hold values from 0.25 to 1.75
- norm2_shift: bfloat16 [2048], P(('seq', 'fsdp')), may hold values from -3 to 3
- w_gate: bfloat16 [2048, 5632], P(('seq', 'fsdp')), may hold values from -0.125 to 0.125
- w_up: bfloat16 [2048, 5632], P(('seq', 'fsdp')), may hold values from -0.125 to 0.125
- w_down: bfloat16 [5632, 2048], P(('seq', 'fsdp')), may hold values from -0.078125 to 0.078125
- grad_out: bfloat16 [4, 1024, 2048], P('fsdp', 'seq'), may hold values from -6 to 6
Outputs:
- layer_out: bfloat16 [4, 1024, 2048], P('fsdp', 'seq')
- grad_in: bfloat16 [4, 1024, 2048], P('fsdp', 'seq')
- grad_norm1_gain: float32 [2048], P(('seq', 'fsdp'))
- grad_norm1_shift: float32 [2048], P(('seq', 'fsdp'))
- grad_w_qkv: float32 [2048, 6144], P(('seq', 'fsdp'))
- grad_b_qkv: float32 [6144], P(('seq', 'fsdp'))
- grad_w_out: float32 [2048, 2048], P(('seq', 'fsdp'))
- grad_norm2_gain: float32 [2048], P(('seq', 'fsdp'))
- grad_norm2_shift: float32 [2048], P(('seq', 'fsdp'))
- grad_w_gate: float32 [2048, 5632], P(('seq', 'fsdp'))
- grad_w_up: float32 [2048, 5632], P(('seq', 'fsdp'))
- grad_w_down: float32 [5632, 2048], P(('seq', 'fsdp'))
Inputs may be any that keep to these rules, and one draw needn't show every extreme that they name: In every sequence, positions start at 0 and rise strictly by steps of 1 or 2, and the last one is 1535.
All inputs are finite; a program needn't handle non-finite values.
Results may differ from a plain program's by a relative error of at most 0.012.
Values may be sent and summed in bfloat16 or wider, within the bound.
No kernel may reach another device: no remote copies, remote signals or barrier semaphores. Data moves between devices by JAX's collectives and lax.ppermute only.
A program may use at most 512 MiB of HBM per device.

v0:
```python
import jax
import jax.numpy as jnp
from jax import lax
from jax.sharding import PartitionSpec as P

HD = 64
ROT = 16


EPS = 1e-05
NEG = -1e30


def layer_norm(values, gain_row, shift_row):
    row_mean = jnp.mean(values, axis=1, keepdims=True)
    centred = values - row_mean
    inverse = lax.rsqrt(jnp.mean(centred * centred, axis=1, keepdims=True) + EPS)
    normed = centred * inverse
    return (normed * gain_row.astype(jnp.float32) + shift_row.astype(jnp.float32), normed, inverse)


def norm_backward(grad_rows, normed, inverse, gain_row):
    scaled = grad_rows * gain_row.astype(jnp.float32)
    inner_term = (
        scaled
        - jnp.mean(scaled, axis=1, keepdims=True)
        - normed * jnp.mean(scaled * normed, axis=1, keepdims=True)
    )
    return (inner_term * inverse, jnp.sum(grad_rows * normed, axis=0), jnp.sum(grad_rows, axis=0))


def angle_tables(positions_here):
    half_rot = ROT // 2
    frequency = 10000.0 ** (-2.0 * jnp.arange(half_rot, dtype=jnp.float32) / ROT)
    angles = positions_here.astype(jnp.float32)[:, None] * frequency[None, :]
    return (
        jnp.concatenate([jnp.cos(angles), jnp.cos(angles)], 1),
        jnp.concatenate([jnp.sin(angles), jnp.sin(angles)], 1),
    )


def rotate(flat_rows, cosine_table, sine_table, backward):
    row_count = flat_rows.shape[0]
    head_view = flat_rows.reshape(row_count, -1, HD)
    half_rot = ROT // 2
    turning = head_view[:, :, :ROT]
    if backward:
        swapped = jnp.concatenate([turning[:, :, half_rot:], -turning[:, :, :half_rot]], 2)
    else:
        swapped = jnp.concatenate([-turning[:, :, half_rot:], turning[:, :, :half_rot]], 2)
    turned = turning * cosine_table[:, None, :] + swapped * sine_table[:, None, :]
    return jnp.concatenate([turned, head_view[:, :, ROT:]], 2).reshape(row_count, -1)


def block_scores(query_part, key_part, query_place, key_place, score_scale):
    scores = (
        jnp.einsum("qhd,khd->hqk", query_part, key_part, preferred_element_type=jnp.float32)
        * score_scale
    )
    allowed = key_place[None, :] <= query_place[:, None]
    return jnp.where(allowed[None], scores, NEG)


def on_device(
    hidden_in,
    positions,
    norm1_gain,
    norm1_shift,
    w_qkv,
    b_qkv,
    w_out,
    norm2_gain,
    norm2_shift,
    w_gate,
    w_up,
    w_down,
    grad_out,
):
    seq_count = lax.axis_size("seq")
    seq_rank = lax.axis_index("seq")
    tok_rows = hidden_in.shape[1]
    width = hidden_in.shape[2]
    seq_places = positions[0]
    head_rows = seq_places.shape[0]
    local_cols = width // seq_count
    block_rows = min(512, head_rows)
    block_count = head_rows // block_rows
    score_scale = HD ** (-0.5)
    (
        first_gain,
        first_shift,
        qkv_full,
        qkv_bias,
        out_full,
        second_gain,
        second_shift,
        gate_full,
        up_full,
        down_full,
    ) = (
        lax.all_gather(norm1_gain, ("seq", "fsdp"), axis=0, tiled=True),
        lax.all_gather(norm1_shift, ("seq", "fsdp"), axis=0, tiled=True),
        lax.all_gather(w_qkv, ("seq", "fsdp"), axis=0, tiled=True),
        lax.all_gather(b_qkv, ("seq", "fsdp"), axis=0, tiled=True),
        lax.all_gather(w_out, ("seq", "fsdp"), axis=0, tiled=True),
        lax.all_gather(norm2_gain, ("seq", "fsdp"), axis=0, tiled=True),
        lax.all_gather(norm2_shift, ("seq", "fsdp"), axis=0, tiled=True),
        lax.all_gather(w_gate, ("seq", "fsdp"), axis=0, tiled=True),
        lax.all_gather(w_up, ("seq", "fsdp"), axis=0, tiled=True),
        lax.all_gather(w_down, ("seq", "fsdp"), axis=0, tiled=True),
    )
    inputs = hidden_in.reshape(tok_rows, width).astype(jnp.float32)
    first_normed, first_hat, first_inverse = layer_norm(inputs, first_gain, first_shift)
    first_normed = first_normed.astype(jnp.bfloat16)
    projected = jnp.dot(
        first_normed, qkv_full, preferred_element_type=jnp.float32
    ) + qkv_bias.astype(jnp.float32)
    own_place = lax.dynamic_slice_in_dim(seq_places, seq_rank * tok_rows, tok_rows)
    own_cosine, own_sine = angle_tables(own_place)
    queries = rotate(projected[:, :width], own_cosine, own_sine, False).astype(jnp.bfloat16)
    key_rows = rotate(projected[:, width : 2 * width], own_cosine, own_sine, False).astype(
        jnp.bfloat16
    )
    values = projected[:, 2 * width :].astype(jnp.bfloat16)
    head_q, head_k, head_v = (
        lax.all_to_all(queries, "seq", split_axis=1, concat_axis=0, tiled=True),
        lax.all_to_all(key_rows, "seq", split_axis=1, concat_axis=0, tiled=True),
        lax.all_to_all(values, "seq", split_axis=1, concat_axis=0, tiled=True),
    )
    all_keys = head_k.reshape(head_rows, -1, HD)
    all_values = head_v.reshape(head_rows, -1, HD)
    query_heads = head_q.reshape(head_rows, -1, HD)
    attended = []
    log_totals = []
    for block_index in range(block_count):
        keys_len = (block_index + 1) * block_rows
        rows_now = slice(block_index * block_rows, keys_len)
        scores = block_scores(
            query_heads[rows_now],
            all_keys[:keys_len],
            seq_places[rows_now],
            seq_places[:keys_len],
            score_scale,
        )
        row_peak = jnp.max(scores, axis=2, keepdims=True)
        exp_scores = jnp.exp(scores - row_peak)
        summed = jnp.sum(exp_scores, axis=2, keepdims=True)
        soft_weights = (exp_scores / summed).astype(jnp.bfloat16)
        block_out = jnp.einsum(
            "hqk,khd->qhd", soft_weights, all_values[:keys_len], preferred_element_type=jnp.float32
        )
        attended.append(block_out.astype(jnp.bfloat16))
        log_totals.append(row_peak[:, :, 0] + jnp.log(summed[:, :, 0]))
    heads_out = jnp.concatenate(attended, 0).reshape(head_rows, local_cols)
    mixed_rows = lax.all_to_all(heads_out, "seq", split_axis=0, concat_axis=1, tiled=True)
    middle = inputs + jnp.dot(mixed_rows, out_full, preferred_element_type=jnp.float32)
    second_normed, second_hat, second_inverse = layer_norm(middle, second_gain, second_shift)
    second_normed = second_normed.astype(jnp.bfloat16)
    gate_act = jnp.dot(second_normed, gate_full, preferred_element_type=jnp.float32)
    up_act = jnp.dot(second_normed, up_full, preferred_element_type=jnp.float32)
    hidden_mid = (gate_act / (1.0 + jnp.exp(-gate_act)) * up_act).astype(jnp.bfloat16)
    layer_out = (
        middle + jnp.dot(hidden_mid, down_full, preferred_element_type=jnp.float32)
    ).astype(jnp.bfloat16)
    first_gain, qkv_full, out_full, second_gain, gate_full, up_full, down_full = (
        lax.all_gather(norm1_gain, ("seq", "fsdp"), axis=0, tiled=True),
        lax.all_gather(w_qkv, ("seq", "fsdp"), axis=0, tiled=True),
        lax.all_gather(w_out, ("seq", "fsdp"), axis=0, tiled=True),
        lax.all_gather(norm2_gain, ("seq", "fsdp"), axis=0, tiled=True),
        lax.all_gather(w_gate, ("seq", "fsdp"), axis=0, tiled=True),
        lax.all_gather(w_up, ("seq", "fsdp"), axis=0, tiled=True),
        lax.all_gather(w_down, ("seq", "fsdp"), axis=0, tiled=True),
    )
    cotangent_low = grad_out.reshape(tok_rows, width)
    cotangent = cotangent_low.astype(jnp.float32)
    d_hidden = jnp.einsum("td,fd->tf", cotangent_low, down_full, preferred_element_type=jnp.float32)
    gate_sigmoid = 1.0 / (1.0 + jnp.exp(-gate_act))
    d_gate = (d_hidden * up_act * gate_sigmoid * (1.0 + gate_act * (1.0 - gate_sigmoid))).astype(
        jnp.bfloat16
    )
    d_up = (d_hidden * gate_act * gate_sigmoid).astype(jnp.bfloat16)
    d_second = jnp.einsum("tf,df->td", d_gate, gate_full, preferred_element_type=jnp.float32)
    d_second = d_second + jnp.einsum("tf,df->td", d_up, up_full, preferred_element_type=jnp.float32)
    d_from_norm, second_gain_grad, second_shift_grad = norm_backward(
        d_second, second_hat, second_inverse, second_gain
    )
    d_middle = cotangent + d_from_norm
    d_middle_low = d_middle.astype(jnp.bfloat16)
    grad_down = jnp.einsum(
        "tf,td->fd", hidden_mid, cotangent_low, preferred_element_type=jnp.float32
    )
    grad_gate = jnp.einsum("td,tf->df", second_normed, d_gate, preferred_element_type=jnp.float32)
    grad_up = jnp.einsum("td,tf->df", second_normed, d_up, preferred_element_type=jnp.float32)
    grad_out_weight = jnp.einsum(
        "te,td->ed", mixed_rows, d_middle_low, preferred_element_type=jnp.float32
    )
    out_share, second_gain_share, second_shift_share, gate_share, up_share, down_share = (
        lax.psum_scatter(grad_out_weight, ("seq", "fsdp"), scatter_dimension=0, tiled=True),
        lax.psum_scatter(second_gain_grad, ("seq", "fsdp"), scatter_dimension=0, tiled=True),
        lax.psum_scatter(second_shift_grad, ("seq", "fsdp"), scatter_dimension=0, tiled=True),
        lax.psum_scatter(grad_gate, ("seq", "fsdp"), scatter_dimension=0, tiled=True),
        lax.psum_scatter(grad_up, ("seq", "fsdp"), scatter_dimension=0, tiled=True),
        lax.psum_scatter(grad_down, ("seq", "fsdp"), scatter_dimension=0, tiled=True),
    )
    d_mixed = jnp.einsum(
        "td,ed->te", d_middle_low, out_full, preferred_element_type=jnp.float32
    ).astype(jnp.bfloat16)
    grad_heads = lax.all_to_all(d_mixed, "seq", split_axis=1, concat_axis=0, tiled=True).reshape(
        head_rows, -1, HD
    )
    key_grad = jnp.zeros((head_rows, local_cols), jnp.float32)
    value_grad = jnp.zeros((head_rows, local_cols), jnp.float32)
    query_terms = []
    for block_index in range(block_count):
        keys_len = (block_index + 1) * block_rows
        rows_now = slice(block_index * block_rows, keys_len)
        query_part = query_heads[rows_now]
        grad_part = grad_heads[rows_now]
        scores = block_scores(
            query_part,
            all_keys[:keys_len],
            seq_places[rows_now],
            seq_places[:keys_len],
            score_scale,
        )
        probs_now = jnp.exp(scores - log_totals[block_index][:, :, None])
        d_probs = jnp.einsum(
            "qhd,khd->hqk", grad_part, all_values[:keys_len], preferred_element_type=jnp.float32
        )
        centre = jnp.sum(probs_now * d_probs, axis=2, keepdims=True)
        d_scores = (probs_now * (d_probs - centre)).astype(jnp.bfloat16)
        d_values = jnp.einsum(
            "hqk,qhd->khd",
            probs_now.astype(jnp.bfloat16),
            grad_part,
            preferred_element_type=jnp.float32,
        )
        d_keys = (
            jnp.einsum("hqk,qhd->khd", d_scores, query_part, preferred_element_type=jnp.float32)
            * score_scale
        )
        d_queries = (
            jnp.einsum(
                "hqk,khd->qhd", d_scores, all_keys[:keys_len], preferred_element_type=jnp.float32
            )
            * score_scale
        )
        query_terms.append(d_queries.astype(jnp.bfloat16))
        key_grad = key_grad.at[:keys_len].add(d_keys.reshape(keys_len, local_cols))
        value_grad = value_grad.at[:keys_len].add(d_values.reshape(keys_len, local_cols))
    query_grad = jnp.concatenate(query_terms, 0).reshape(head_rows, local_cols)
    back_q, back_k, back_v = (
        lax.all_to_all(query_grad, "seq", split_axis=0, concat_axis=1, tiled=True),
        lax.all_to_all(
            key_grad.astype(jnp.bfloat16), "seq", split_axis=0, concat_axis=1, tiled=True
        ),
        lax.all_to_all(
            value_grad.astype(jnp.bfloat16), "seq", split_axis=0, concat_axis=1, tiled=True
        ),
    )
    d_projected = jnp.concatenate(
        [
            rotate(back_q.astype(jnp.float32), own_cosine, own_sine, True),
            rotate(back_k.astype(jnp.float32), own_cosine, own_sine, True),
            back_v.astype(jnp.float32),
        ],
        1,
    ).astype(jnp.bfloat16)
    grad_qkv_bias = jnp.sum(d_projected.astype(jnp.float32), axis=0)
    d_first = jnp.einsum("te,de->td", d_projected, qkv_full, preferred_element_type=jnp.float32)
    d_from_first, first_gain_grad, first_shift_grad = norm_backward(
        d_first, first_hat, first_inverse, first_gain
    )
    grad_in = (d_middle + d_from_first).astype(jnp.bfloat16).reshape(1, tok_rows, width)
    grad_qkv_weight = jnp.einsum(
        "td,te->de", first_normed, d_projected, preferred_element_type=jnp.float32
    )
    first_gain_share, first_shift_share, qkv_share, bias_share = (
        lax.psum_scatter(first_gain_grad, ("seq", "fsdp"), scatter_dimension=0, tiled=True),
        lax.psum_scatter(first_shift_grad, ("seq", "fsdp"), scatter_dimension=0, tiled=True),
        lax.psum_scatter(grad_qkv_weight, ("seq", "fsdp"), scatter_dimension=0, tiled=True),
        lax.psum_scatter(grad_qkv_bias, ("seq", "fsdp"), scatter_dimension=0, tiled=True),
    )
    return (
        layer_out.reshape(1, tok_rows, width),
        grad_in,
        first_gain_share,
        first_shift_share,
        qkv_share,
        bias_share,
        out_share,
        second_gain_share,
        second_shift_share,
        gate_share,
        up_share,
        down_share,
    )


def solution(mesh):
    placed = (
        P("fsdp", "seq", None),
        P("fsdp", None),
        P(("seq", "fsdp")),
        P(("seq", "fsdp")),
        P(("seq", "fsdp"), None),
        P(("seq", "fsdp")),
        P(("seq", "fsdp"), None),
        P(("seq", "fsdp")),
        P(("seq", "fsdp")),
        P(("seq", "fsdp"), None),
        P(("seq", "fsdp"), None),
        P(("seq", "fsdp"), None),
        P("fsdp", "seq", None),
    )
    return jax.shard_map(
        on_device,
        mesh=mesh,
        in_specs=placed,
        out_specs=(
            P("fsdp", "seq", None),
            P("fsdp", "seq", None),
            P(("seq", "fsdp")),
            P(("seq", "fsdp")),
            P(("seq", "fsdp"), None),
            P(("seq", "fsdp")),
            P(("seq", "fsdp"), None),
            P(("seq", "fsdp")),
            P(("seq", "fsdp")),
            P(("seq", "fsdp"), None),
            P(("seq", "fsdp"), None),
            P(("seq", "fsdp"), None),
        ),
        check_vma=False,
    )
```

profile of v0, /device:TPU:0, one launch (start us, length us, event | category | flops | bytes accessed | tf_op | source)
XLA Modules:
  0.0 4477.0 jit_solution(10988822912044726973)
XLA Ops:
  14.8 43.6 all-reduce.13
  61.4 108.4 %all-gather.6.cloned.1.call-done = bf16[2048,6144]{1,0:T(8,128)(2,1)} async-done(((bf16[64,6144]{1,0:T(8,128)(2,1)}), bf16[2048,6144]{1,0:T(8,128)(2,1)}) %all-gather.6.cloned.1.call-update) | async-done | bytes 25165840 | tf_op jit(solution)/shard_map/all_gather | solution.py:103
  169.8 10.1 convolution_add_fusion
  182.3 3.5 all-to-all-start
  190.2 5.2 all-to-all-done
  195.5 3.5 all-to-all-start.2
  200.6 12.8 all-to-all-done.2
  213.4 3.7 all-to-all-start.1
  222.9 3.9 all-to-all-done.1
  239.3 3.5 all-to-all-start.3
  243.1 12.0 all-gather.8.cloned.1.call-done
  255.1 4.7 fusion.66
  260.4 139.4 %all-gather.12.cloned.1.call-done = bf16[2048,5632]{1,0:T(8,128)(2,1)} async-done(((bf16[64,5632]{1,0:T(8,128)(2,1)}), bf16[2048,5632]{1,0:T(8,128)(2,1)}) %all-gather.12.cloned.1.call-update) | async-done | bytes 23068688 | tf_op jit(solution)/shard_map/all_gather | solution.py:109
  399.9 12.3 fusion.68
  412.2 133.2 %all-gather.10.cloned.1.call-done = bf16[2048,5632]{1,0:T(8,128)(2,1)} async-done(((bf16[64,5632]{1,0:T(8,128)(2,1)}), bf16[2048,5632]{1,0:T(8,128)(2,1)}) %all-gather.10.cloned.1.call-update) | async-done | bytes 23068688 | tf_op jit(solution)/shard_map/all_gather | solution.py:108
  545.4 12.3 fusion.67
  557.7 133.2 %all-gather.14.cloned.1.call-done = bf16[5632,2048]{1,0:T(8,128)(2,1)} async-done(((bf16[176,2048]{1,0:T(8,128)(2,1)}), bf16[5632,2048]{1,0:T(8,128)(2,1)}) %all-gather.14.cloned.1.call-update) | async-done | bytes 23068688 | tf_op jit(solution)/shard_map/all_gather | solution.py:110
  690.9 15.6 multiply_convert_fusion.2
  706.5 13.4 fusion.69
  719.9 14.2 multiply_reduce_fusion.2
  736.1 8.1 fusion.53
  744.3 6.3 convolution_convert_fusion
  751.4 3.7 all-to-all-start.4
  755.2 11.6 all-to-all-done.4
  767.5 3.3 multiply_reduce_fusion.1
  775.3 4.7 multiply_reduce_fusion
  780.0 4.5 multiply_convert_fusion
  789.9 3.7 fusion.26
  795.5 3.5 all-to-all-start.6
  799.0 3.0 fusion.11
  802.0 4.9 fusion.2
  806.9 3.7 all-to-all-done.6
  810.5 3.5 all-to-all-start.5
  816.1 9.1 all-to-all-done.5
  825.2 3.5 all-to-all-start.7
  830.8 9.2 all-to-all-done.7
  840.0 21.7 fusion.56
  863.2 18.0 fusion.41
  882.8 18.1 fusion.71
  902.3 18.2 fusion.70
  922.2 11.7 fusion.10
  934.5 13.8 fusion.37
  948.3 41.6 all-reduce.12
  994.2 113.5 %reduce-scatter.8.cloned.1.call-done = f32[64,2048]{1,0:T(8,128)} async-done(((f32[2048,2048]{1,0:T(8,128)}), f32[64,2048]{1,0:T(8,128)}) %reduce-scatter.8.cloned.1.call-update) | async-done | bytes 524304 | tf_op jit(solution)/shard_map/reduce_scatter | solution.py:198
  1107.7 436.6 %reduce-scatter.6.cloned.1.call-done = f32[64,6144]{1,0:T(8,128)} async-done(((f32[2048,6144]{1,0:T(8,128)}), f32[64,6144]{1,0:T(8,128)}) %reduce-scatter.6.cloned.1.call-update) | async-done | bytes 1572880 | tf_op jit(solution)/shard_map/reduce_scatter | solution.py:281
  1544.3 974.3 %reduce-scatter.14.cloned.1.call-done = f32[176,2048]{1,0:T(8,128)} async-done(((f32[5632,2048]{1,0:T(8,128)}), f32[176,2048]{1,0:T(8,128)}) %reduce-scatter.14.cloned.1.call-update) | async-done | bytes 1441808 | tf_op jit(solution)/shard_map/reduce_scatter | solution.py:203
  2518.5 975.7 %reduce-scatter.12.cloned.1.call-done = f32[64,5632]{1,0:T(8,128)} async-done(((f32[2048,5632]{1,0:T(8,128)}), f32[64,5632]{1,0:T(8,128)}) %reduce-scatter.12.cloned.1.call-update) | async-done | bytes 1441808 | tf_op jit(solution)/shard_map/reduce_scatter | solution.py:202
  3494.2 975.5 %reduce-scatter.10.cloned.1.call-done = f32[64,5632]{1,0:T(8,128)} async-done(((f32[2048,5632]{1,0:T(8,128)}), f32[64,5632]{1,0:T(8,128)}) %reduce-scatter.10.cloned.1.call-update) | async-done | bytes 1441808 | tf_op jit(solution)/shard_map/reduce_scatter | solution.py:201
  (252 shorter events, 67.6 us)
Async XLA Ops:
  7.2 53.9 %copy-start.6 = (bf16[1,128,2048]{2,1,0:T(8,128)(2,1)S(1)}, bf16[1,128,2048]{2,1,0:T(8,128)(2,1)}, u32[]{:S(2)}) copy-start(bf16[1,128,2048]{2,1,0:T(8,128)(2,1)} %param.25) | copy-start | bytes 1572868
  7.2 162.6 %all-gather.6.cloned.1.call-start = ((), (), s32[]{:S(2)}) async-start(), calls=%async_computation.13 | async-start | bytes 25952256 | tf_op jit(solution)/shard_map/all_gather | solution.py:103
  7.9 247.2 %all-gather.8.cloned.1.call-start = ((), (), s32[]{:S(2)}) async-start(), calls=%async_computation.14 | async-start | bytes 8650752 | tf_op jit(solution)/shard_map/all_gather | solution.py:105
  8.7 391.2 %all-gather.12.cloned.1.call-start = ((), (), s32[]{:S(2)}) async-start(), calls=%async_computation.16 | async-start | bytes 23789568 | tf_op jit(solution)/shard_map/all_gather | solution.py:109
  9.4 536.0 %all-gather.10.cloned.1.call-start = ((), (), s32[]{:S(2)}) async-start(), calls=%async_computation.15 | async-start | bytes 23789568 | tf_op jit(solution)/shard_map/all_gather | solution.py:108
  10.0 680.9 %all-gather.14.cloned.1.call-start = ((), (), s32[]{:S(2)}) async-start(), calls=%async_computation.17 | async-start | bytes 23789568 | tf_op jit(solution)/shard_map/all_gather | solution.py:110
  61.1 118.8 %copy-start.45 = (f32[128]{0:T(128)}, f32[128]{0:T(128)S(1)}, u32[]{:S(2)}) copy-start(f32[128]{0:T(128)S(1)} %broadcast_multiply_fusion.5) | copy-start | bytes 1540
  61.4 118.5 %copy-start.53 = (f32[128]{0:T(128)}, f32[128]{0:T(128)S(1)}, u32[]{:S(2)}) copy-start(f32[128]{0:T(128)S(1)} %add_rsqrt_fusion.1) | copy-start | bytes 1540
  182.3 13.2 all-to-all-start
  195.5 17.9 all-to-all-start.2
  213.4 13.5 all-to-all-start.1
  222.6 12.9 copy-start.32
  222.9 11.6 copy-start.36
  239.3 15.8 all-to-all-start.3
  242.8 864.9 %reduce-scatter.8.cloned.1.call-start = ((), (), s32[]{:S(2)}) async-start(), calls=%async_computation.19 | async-start | bytes 17301504 | tf_op jit(solution)/shard_map/reduce_scatter | solution.py:198
  243.1 17.0 copy-start.39
  259.8 474.3 %copy-start.4 = (f32[128,2048]{1,0:T(8,128)}, f32[128,2048]{1,0:T(8,128)S(1)}, u32[]{:S(2)}) copy-start(f32[128,2048]{1,0:T(8,128)S(1)} %get-tuple-element.120) | copy-start | bytes 3145732
  259.9 152.3 %copy-start.55 = (f32[128]{0:T(128)}, f32[128]{0:T(128)S(1)}, u32[]{:S(2)}) copy-start(f32[128]{0:T(128)S(1)} %broadcast_multiply_fusion.4) | copy-start | bytes 1540
  260.1 152.1 %copy-start.57 = (f32[128]{0:T(128)}, f32[128]{0:T(128)S(1)}, u32[]{:S(2)}) copy-start(f32[128]{0:T(128)S(1)} %add_rsqrt_fusion) | copy-start | bytes 1540
  260.4 285.0 %copy-start.10 = (bf16[128,2048]{1,0:T(8,128)(2,1)}, bf16[128,2048]{1,0:T(8,128)(2,1)S(1)}, u32[]{:S(2)}) copy-start(bf16[128,2048]{1,0:T(8,128)(2,1)S(1)} %add_convert_fusion.1) | copy-start | bytes 1572868
  706.4 13.4 copy-start.12
  706.4 13.4 copy-start.14
  706.4 13.4 copy-start.40
  706.5 13.4 copy-start.56
  706.5 13.4 copy-start.58
  736.1 8.2 copy-start.8
  744.2 10.8 copy-start.42
  744.3 10.8 copy-start.50
  744.3 10.9 copy-start.44
  744.3 10.9 copy-start.52
  750.6 16.9 copy-start.37
  751.4 15.4 all-to-all-start.4
  795.5 15.1 all-to-all-start.6
  810.5 14.6 all-to-all-start.5
  825.2 14.8 all-to-all-start.7
  828.7 715.6 %reduce-scatter.6.cloned.1.call-start = ((), (), s32[]{:S(2)}) async-start(), calls=%async_computation.18 | async-start | bytes 51904512 | tf_op jit(solution)/shard_map/reduce_scatter | solution.py:281
  830.7 31.0 copy-start.18
  830.8 30.9 copy-start.20
  861.7 1656.8 %reduce-scatter.14.cloned.1.call-start = ((), (), s32[]{:S(2)}) async-start(), calls=%async_computation.22 | async-start | bytes 47579136 | tf_op jit(solution)/shard_map/reduce_scatter | solution.py:203
  881.3 2613.0 %reduce-scatter.12.cloned.1.call-start = ((), (), s32[]{:S(2)}) async-start(), calls=%async_computation.21 | async-start | bytes 47579136 | tf_op jit(solution)/shard_map/reduce_scatter | solution.py:202
  901.0 3568.8 %reduce-scatter.10.cloned.1.call-start = ((), (), s32[]{:S(2)}) async-start(), calls=%async_computation.20 | async-start | bytes 47579136 | tf_op jit(solution)/shard_map/reduce_scatter | solution.py:201
  922.2 11.7 copy-start.19
  922.2 11.7 copy-start.21
  922.2 12.2 copy-start.46
  922.2 12.2 copy-start.54
  934.5 13.8 copy-start.47
  934.5 13.8 copy-start.48
  934.5 58.4 %copy-start.9 = (f32[128,2048]{1,0:T(8,128)S(1)}, f32[128,2048]{1,0:T(8,128)}, u32[]{:S(2)}) copy-start(f32[128,2048]{1,0:T(8,128)} %copy-done.8) | copy-start | bytes 3145732
  (31 other events, 88.1 us)
Sparse Core Ops, SparseCore 0:
  10.9 158.8 all-gather.5
  172.7 82.3 all-gather.7
  257.9 141.8 all-gather.11
  402.5 142.7 all-gather.9
  548.0 142.7 all-gather.13
  744.4 363.2 reduce-scatter.7
  1114.7 429.5 reduce-scatter.5
  1547.1 971.3 reduce-scatter.13
  2521.4 972.7 reduce-scatter.11
  3497.0 972.7 reduce-scatter.9
where the time goes:
time: 4480 us
  waiting for transfers between devices  4060 us (91%)
  matrix products  228 us (5%)
  blocking collectives  85.2 us (2%)
    reduce_scatter x1, waiting for transfers between devices, on_device(): lax.psum_scatter(grad_up, ('seq', 'fsdp'), scatter_dimension=0, tiled=True)  976 us
    reduce_scatter x1, waiting for transfers between devices, on_device(): lax.psum_scatter(grad_gate, ('seq', 'fsdp'), scatter_dimension=0, tiled=T...  975 us
    reduce_scatter x1, waiting for transfers between devices, on_device(): lax.psum_scatter(grad_down, ('seq', 'fsdp'), scatter_dimension=0, tiled=T...  974 us
    reduce_scatter x1, waiting for transfers between devices, on_device(): lax.psum_scatter(grad_qkv_weight, ('seq', 'fsdp'), scatter_dimension=0, t...  437 us
    all_gather x1, waiting for transfers between devices, on_device(): lax.all_gather(w_up, ('seq', 'fsdp'), axis=0, tiled=True)  139 us
    all_gather x1, waiting for transfers between devices, on_device(): lax.all_gather(w_down, ('seq', 'fsdp'), axis=0, tiled=True)  133 us
    all_gather x1, waiting for transfers between devices, on_device(): lax.all_gather(w_gate, ('seq', 'fsdp'), axis=0, tiled=True)  133 us
    reduce_scatter x1, waiting for transfers between devices, on_device(): lax.psum_scatter(grad_out_weight, ('seq', 'fsdp'), scatter_dimension=0, t...  114 us
  transfers between devices with their start and end apart: 18, of which 17 were waited for; matrix products, arithmetic and copies ran while one was open for 5% of the time, Pallas kernels for 0%

commit v1 on v0

v1 whole, which is shorter than its diff:
```python
import jax
import jax.numpy as jnp
from jax import lax
from jax.sharding import PartitionSpec as P

HD = 64
ROT = 16

EPS = 1e-05
NEG = -1e30

BF = jnp.bfloat16
F4 = jnp.float32


def dot(a, b, out=F4):
    return jnp.dot(a, b, preferred_element_type=F4).astype(out)


def dot_nt(a, b):
    return lax.dot_general(a, b, (((1,), (1,)), ((), ())), preferred_element_type=F4)


def dot_tn(a, b):
    return lax.dot_general(a, b, (((0,), (0,)), ((), ())), preferred_element_type=F4)


def layer_norm(values, gain_row, shift_row):
    row_mean = jnp.mean(values, axis=1, keepdims=True)
    centred = values - row_mean
    inverse = lax.rsqrt(jnp.mean(centred * centred, axis=1, keepdims=True) + EPS)
    normed = centred * inverse
    return (normed * gain_row.astype(F4) + shift_row.astype(F4), normed, inverse)


def norm_backward(grad_rows, normed, inverse, gain_row):
    scaled = grad_rows * gain_row.astype(F4)
    inner_term = (
        scaled
        - jnp.mean(scaled, axis=1, keepdims=True)
        - normed * jnp.mean(scaled * normed, axis=1, keepdims=True)
    )
    return (inner_term * inverse, jnp.sum(grad_rows * normed, axis=0), jnp.sum(grad_rows, axis=0))


def angle_tables(places):
    half_rot = ROT // 2
    frequency = 10000.0 ** (-2.0 * jnp.arange(half_rot, dtype=F4) / ROT)
    angles = places.astype(F4)[:, None] * frequency[None, :]
    return (
        jnp.concatenate([jnp.cos(angles), jnp.cos(angles)], 1),
        jnp.concatenate([jnp.sin(angles), jnp.sin(angles)], 1),
    )


def rotate(flat_rows, cosine_table, sine_table, backward):
    row_count = flat_rows.shape[0]
    head_view = flat_rows.reshape(row_count, -1, HD)
    half_rot = ROT // 2
    turning = head_view[:, :, :ROT]
    if backward:
        swapped = jnp.concatenate([turning[:, :, half_rot:], -turning[:, :, :half_rot]], 2)
    else:
        swapped = jnp.concatenate([-turning[:, :, half_rot:], turning[:, :, :half_rot]], 2)
    turned = turning * cosine_table[:, None, :] + swapped * sine_table[:, None, :]
    return jnp.concatenate([turned, head_view[:, :, ROT:]], 2).reshape(row_count, -1)


def block_scores(query_part, key_part, query_place, key_place, score_scale):
    scores = (
        jnp.einsum("qhd,khd->hqk", query_part, key_part, preferred_element_type=F4) * score_scale
    )
    allowed = key_place[None, :] <= query_place[:, None]
    return jnp.where(allowed[None], scores, NEG)


def attend(query_heads, all_keys, all_values, places, score_scale):
    rows = places.shape[0]
    block_rows = min(512, rows)
    attended, log_totals = [], []
    for block_index in range(rows // block_rows):
        keys_len = (block_index + 1) * block_rows
        rows_now = slice(block_index * block_rows, keys_len)
        scores = block_scores(
            query_heads[rows_now], all_keys[:keys_len], places[rows_now], places[:keys_len], score_scale
        )
        row_peak = jnp.max(scores, axis=2, keepdims=True)
        exp_scores = jnp.exp(scores - row_peak)
        summed = jnp.sum(exp_scores, axis=2, keepdims=True)
        soft_weights = (exp_scores / summed).astype(BF)
        block_out = jnp.einsum(
            "hqk,khd->qhd", soft_weights, all_values[:keys_len], preferred_element_type=F4
        )
        attended.append(block_out.astype(BF))
        log_totals.append(row_peak[:, :, 0] + jnp.log(summed[:, :, 0]))
    return jnp.concatenate(attended, 0).reshape(rows, -1), log_totals


def attend_backward(query_heads, all_keys, all_values, grad_heads, log_totals, places, score_scale):
    rows = places.shape[0]
    cols = query_heads.shape[1] * HD
    block_rows = min(512, rows)
    key_grad = jnp.zeros((rows, cols), F4)
    value_grad = jnp.zeros((rows, cols), F4)
    query_terms = []
    for block_index in range(rows // block_rows):
        keys_len = (block_index + 1) * block_rows
        rows_now = slice(block_index * block_rows, keys_len)
        query_part = query_heads[rows_now]
        grad_part = grad_heads[rows_now]
        scores = block_scores(
            query_part, all_keys[:keys_len], places[rows_now], places[:keys_len], score_scale
        )
        probs_now = jnp.exp(scores - log_totals[block_index][:, :, None])
        d_probs = jnp.einsum(
            "qhd,khd->hqk", grad_part, all_values[:keys_len], preferred_element_type=F4
        )
        centre = jnp.sum(probs_now * d_probs, axis=2, keepdims=True)
        d_scores = (probs_now * (d_probs - centre)).astype(BF)
        d_values = jnp.einsum(
            "hqk,qhd->khd", probs_now.astype(BF), grad_part, preferred_element_type=F4
        )
        d_keys = (
            jnp.einsum("hqk,qhd->khd", d_scores, query_part, preferred_element_type=F4) * score_scale
        )
        d_queries = (
            jnp.einsum("hqk,khd->qhd", d_scores, all_keys[:keys_len], preferred_element_type=F4)
            * score_scale
        )
        query_terms.append(d_queries.astype(BF))
        key_grad = key_grad.at[:keys_len].add(d_keys.reshape(keys_len, cols))
        value_grad = value_grad.at[:keys_len].add(d_values.reshape(keys_len, cols))
    query_grad = jnp.concatenate(query_terms, 0).reshape(rows, cols)
    return query_grad, key_grad.astype(BF), value_grad.astype(BF)


class Links:
    def __init__(self):
        self.ns = lax.axis_size("seq")
        self.nz = lax.axis_size("fsdp")
        self.s = lax.axis_index("seq")
        self.z = lax.axis_index("fsdp")
        self.core = self.s % 2
        self.fast_plane = self.ns == 8
        self.fast_line = self.nz == 4
        self.order = [0, 2, 4, 6, 1, 3, 5, 7]

    def flip(self, values, bit):
        return lax.ppermute(values, "seq", [(i, i ^ bit) for i in range(self.ns)])

    def swap_core(self, values):
        return self.flip(values, 1)

    def hop(self, values, pairs):
        return lax.ppermute(values, "fsdp", pairs)

    def plane_gather(self, own):
        if not self.fast_plane:
            return lax.all_gather(own, "seq", axis=0, tiled=True)
        half = own.shape[0] // 2
        own_other = self.swap_core(own)
        along_x = self.flip(own, 2)
        along_y = self.flip(own, 4)
        far_a = self.flip(along_x[:half], 4)
        far_b = self.flip(along_y[half:], 2)
        rest = [self.swap_core(part) for part in (along_x, along_y, far_a, far_b)]
        return jnp.concatenate([own, along_x, along_y, far_a, far_b, own_other] + rest, 0)

    def plane_reduce(self, keep, send):
        if not self.fast_plane:
            return lax.psum_scatter(
                jnp.concatenate([keep, send], 0).astype(BF), "seq", scatter_dimension=0, tiled=True
            ).astype(F4)
        rows = keep.shape[0] // 4
        half = rows // 2
        pair = keep + self.swap_core(send.astype(BF)).astype(F4)
        own, to_x, to_y, far = (pair[i * rows : (i + 1) * rows] for i in range(4))
        far = far.astype(BF)
        via_x = self.flip(far[:half], 2)
        via_y = self.flip(far[half:], 4)
        to_y = jnp.concatenate([to_y[:half] + via_x.astype(F4), to_y[half:]], 0).astype(BF)
        to_x = jnp.concatenate([to_x[:half], to_x[half:] + via_y.astype(F4)], 0).astype(BF)
        from_x = self.flip(to_x, 2)
        from_y = self.flip(to_y, 4)
        return own + from_x.astype(F4) + from_y.astype(F4)

    def plane_sorted(self, rows_in):
        if not self.fast_plane:
            return rows_in
        chunk = rows_in.shape[0] // self.ns
        at = jnp.array([self.order.index(j) for j in range(8)], jnp.int32)
        parts = [
            lax.dynamic_slice_in_dim(rows_in, at[self.s ^ j] * chunk, chunk, 0) for j in range(8)
        ]
        return jnp.concatenate(parts, 0)

    def plane_unsorted(self, rows_in):
        if not self.fast_plane:
            return rows_in
        chunk = rows_in.shape[0] // self.ns
        parts = [
            lax.dynamic_slice_in_dim(rows_in, (self.s ^ k) * chunk, chunk, 0) for k in self.order
        ]
        return jnp.concatenate(parts, 0)

    def line_gather(self, own):
        if not self.fast_line:
            mine = lax.all_gather(own, "fsdp", axis=0, tiled=True)
            return jnp.concatenate([mine, self.swap_core(mine)], 0)
        up1 = self.hop(own, [(0, 1), (1, 2), (2, 3)])
        down1 = self.hop(own, [(3, 2), (2, 1), (1, 0)])
        up2 = self.hop(up1, [(1, 2), (2, 3)])
        down2 = self.hop(down1, [(2, 1), (1, 0)])
        up3 = self.hop(up2, [(2, 3)])
        down3 = self.hop(down2, [(1, 0)])
        parts = [
            own,
            jnp.where(self.z >= 1, up1, down3),
            jnp.where(self.z >= 2, up2, down2),
            jnp.where(self.z >= 3, up3, down1),
        ]
        return jnp.concatenate(parts + [self.swap_core(part) for part in parts], 0)

    def line_reduce(self, keep, send):
        pair = keep + self.swap_core(send.astype(BF)).astype(F4)
        if not self.fast_line:
            return lax.psum_scatter(pair.astype(BF), "fsdp", scatter_dimension=0, tiled=True).astype(F4)
        rows = pair.shape[0] // 4
        own, one, two, three = (pair[i * rows : (i + 1) * rows] for i in range(4))
        up = self.hop(one.astype(BF), [(0, 1)])
        down = self.hop(three.astype(BF), [(3, 2)])
        two = (two + up.astype(F4) + down.astype(F4)).astype(BF)
        up = self.hop(two, [(0, 1), (1, 2)])
        down = self.hop(two, [(3, 2), (2, 1)])
        three = three + up.astype(F4)
        one = one + down.astype(F4)
        up = self.hop(three.astype(BF), [(0, 1), (1, 2), (2, 3)])
        down = self.hop(one.astype(BF), [(3, 2), (2, 1), (1, 0)])
        return own + up.astype(F4) + down.astype(F4)

    def chip_groups(self):
        return [list(range(c, self.ns, 2)) for c in range(2)]

    def chips_gather(self, own):
        return lax.all_gather(own, "seq", axis=0, tiled=True, axis_index_groups=self.chip_groups())

    def chips_reduce(self, rows_in):
        return lax.psum_scatter(
            rows_in, "seq", scatter_dimension=0, tiled=True, axis_index_groups=self.chip_groups()
        )

    def bits(self):
        found = []
        bit = self.ns // 2
        while bit:
            found.append(("seq", self.ns, self.s, bit))
            bit //= 2
        bit = self.nz // 2
        while bit:
            found.append(("fsdp", self.nz, self.z, bit))
            bit //= 2
        return found

    def short_gather(self, own):
        held = own[None, :]
        for axis, size, place, bit in reversed(self.bits()):
            other = lax.ppermute(held, axis, [(i, i ^ bit) for i in range(size)])
            high = (place & bit) != 0
            first = jnp.where(high, other, held)
            second = jnp.where(high, held, other)
            held = jnp.concatenate([first, second], 0)
        return held

    def short_reduce(self, held):
        for axis, size, place, bit in self.bits():
            half = held.shape[0] // 2
            high = (place & bit) != 0
            keep = jnp.where(high, held[half:], held[:half])
            send = jnp.where(high, held[:half], held[half:])
            held = keep + lax.ppermute(send, axis, [(i, i ^ bit) for i in range(size)])
        return held[0]


def on_device(
    hidden_in,
    positions,
    norm1_gain,
    norm1_shift,
    w_qkv,
    b_qkv,
    w_out,
    norm2_gain,
    norm2_shift,
    w_gate,
    w_up,
    w_down,
    grad_out,
):
    links = Links()
    ns, nz = links.ns, links.nz
    devices = ns * nz
    chips = ns // 2
    tok_rows = hidden_in.shape[1]
    width = hidden_in.shape[2]
    ff_rows = w_down.shape[0]
    ff_cols = ff_rows * chips
    shard_rows = w_qkv.shape[0]
    seq_places = positions[0]
    length = seq_places.shape[0]
    cols = width // ns
    score_scale = HD ** (-0.5)
    core = links.core

    qkv_blocks = w_qkv.reshape(shard_rows, 3, ns, cols).transpose(2, 0, 1, 3)
    qkv_blocks = qkv_blocks.reshape(ns, shard_rows, 3 * cols)
    qkv_blocks = lax.all_to_all(qkv_blocks, "seq", split_axis=0, concat_axis=0, tiled=True)
    qkv_here = lax.all_gather(qkv_blocks, "fsdp", axis=0, tiled=False)
    qkv_here = qkv_here.transpose(1, 0, 2, 3).reshape(width, 3 * cols)
    out_here = lax.all_gather(w_out, "fsdp", axis=0, tiled=True)

    short = jnp.concatenate([norm1_gain, norm1_shift, norm2_gain, norm2_shift, b_qkv])
    short_all = links.short_gather(short)
    n = shard_rows
    first_gain = short_all[:, :n].reshape(-1)
    first_shift = short_all[:, n : 2 * n].reshape(-1)
    second_gain = short_all[:, 2 * n : 3 * n].reshape(-1)
    second_shift = short_all[:, 3 * n : 4 * n].reshape(-1)
    bias_all = short_all[:, 4 * n :].reshape(3, ns, cols)
    bias_here = lax.dynamic_index_in_dim(bias_all, links.s, 1, keepdims=False).reshape(3 * cols)

    def ff_blocks(weight):
        return weight.reshape(shard_rows, chips, 2, nz, ff_rows).transpose(3, 2, 0, 1, 4)

    gate_up = jnp.stack([ff_blocks(w_gate), ff_blocks(w_up)], 2)
    gate_up = gate_up.reshape(nz, 2, 2, shard_rows, ff_cols)
    gate_up = lax.all_to_all(gate_up, "fsdp", split_axis=0, concat_axis=0, tiled=True)
    ff_keep = jnp.where(core == 0, gate_up[:, 0], gate_up[:, 1])
    ff_send = jnp.where(core == 0, gate_up[:, 1], gate_up[:, 0])
    ff_other = links.swap_core(ff_send)
    ff_first = jnp.where(core == 0, ff_keep, ff_other)
    ff_second = jnp.where(core == 0, ff_other, ff_keep)
    down_here = links.chips_gather(w_down)

    def ff_weight(index):
        rows = jnp.stack([ff_first[:, index], ff_second[:, index]], 0)
        return links.chips_gather(rows.reshape(2 * nz * shard_rows, ff_cols))

    gate_here = ff_weight(0)
    up_here = ff_weight(1)

    inputs = hidden_in.reshape(tok_rows, width).astype(F4)
    first_normed, first_hat, first_inverse = layer_norm(inputs, first_gain, first_shift)
    normed_rows = links.plane_gather(first_normed.astype(BF))
    cotangent_low = grad_out.reshape(tok_rows, width)
    cotangent_rows = links.line_gather(cotangent_low)
    projected = dot(normed_rows, qkv_here) + bias_here.astype(F4)
    projected = links.plane_sorted(projected)
    cosine, sine = angle_tables(seq_places)
    query_heads = rotate(projected[:, :cols], cosine, sine, False).astype(BF).reshape(length, -1, HD)
    all_keys = (
        rotate(projected[:, cols : 2 * cols], cosine, sine, False).astype(BF).reshape(length, -1, HD)
    )
    all_values = projected[:, 2 * cols :].astype(BF).reshape(length, -1, HD)
    heads_out, log_totals = attend(query_heads, all_keys, all_values, seq_places, score_scale)
    mixed = links.plane_unsorted(heads_out)
    half = length // 2
    out_send = dot(mixed[half:], out_here)
    out_keep = dot(mixed[:half], out_here)
    middle = inputs + links.plane_reduce(out_keep, out_send)

    second_normed, second_hat, second_inverse = layer_norm(middle, second_gain, second_shift)
    second_rows = links.line_gather(second_normed.astype(BF))
    d_hidden = dot_nt(cotangent_rows, down_here)
    gate_act = dot(second_rows, gate_here)
    up_act = dot(second_rows, up_here)
    gate_sigmoid = 1.0 / (1.0 + jnp.exp(-gate_act))
    hidden_mid = (gate_act / (1.0 + jnp.exp(-gate_act)) * up_act).astype(BF)
    d_gate = (d_hidden * up_act * gate_sigmoid * (1.0 + gate_act * (1.0 - gate_sigmoid))).astype(BF)
    d_up = (d_hidden * gate_act * gate_sigmoid).astype(BF)
    tokens_half = second_rows.shape[0] // 2

    def second_terms(rows):
        return dot_nt(d_gate[rows], gate_here) + dot_nt(d_up[rows], up_here)

    second_send = second_terms(slice(tokens_half, None))
    second_keep = second_terms(slice(0, tokens_half))
    d_second = links.line_reduce(second_keep, second_send)
    d_from_norm, second_gain_grad, second_shift_grad = norm_backward(
        d_second, second_hat, second_inverse, second_gain
    )
    d_middle = cotangent_low.astype(F4) + d_from_norm
    d_middle_rows = links.plane_gather(d_middle.astype(BF))

    down_share = links.chips_reduce(dot_tn(hidden_mid, cotangent_rows).astype(BF))
    gate_sum = links.chips_reduce(dot_tn(second_rows, d_gate).astype(BF))
    up_sum = links.chips_reduce(dot_tn(second_rows, d_up).astype(BF))
    down_send = dot(hidden_mid[tokens_half:], down_here)
    down_keep = dot(hidden_mid[:tokens_half], down_here)
    layer_out = (middle + links.line_reduce(down_keep, down_send)).astype(BF)

    grad_mixed = dot_nt(d_middle_rows, out_here).astype(BF)
    grad_heads = links.plane_sorted(grad_mixed).reshape(length, -1, HD)
    out_share = lax.psum_scatter(
        dot_tn(mixed, d_middle_rows).astype(BF), "fsdp", scatter_dimension=0, tiled=True
    )
    query_grad, key_grad, value_grad = attend_backward(
        query_heads, all_keys, all_values, grad_heads, log_totals, seq_places, score_scale
    )
    d_projected = jnp.concatenate(
        [
            rotate(query_grad.astype(F4), cosine, sine, True),
            rotate(key_grad.astype(F4), cosine, sine, True),
            value_grad.astype(F4),
        ],
        1,
    ).astype(BF)
    bias_grad = jnp.sum(d_projected.astype(F4), axis=0).reshape(3, 1, cols)
    d_projected = links.plane_unsorted(d_projected)
    qkv_grad = dot_tn(normed_rows, d_projected).astype(BF)
    qkv_grad = qkv_grad.reshape(ns, nz, shard_rows, 3 * cols).transpose(1, 0, 2, 3)
    qkv_sum = lax.psum_scatter(qkv_grad, "fsdp", scatter_dimension=0, tiled=True)
    qkv_sum = qkv_sum.reshape(ns, shard_rows, 3 * cols)
    qkv_sum = lax.all_to_all(qkv_sum, "seq", split_axis=0, concat_axis=0, tiled=True)
    qkv_share = qkv_sum.reshape(ns, shard_rows, 3, cols).transpose(1, 2, 0, 3)
    qkv_share = qkv_share.reshape(shard_rows, 3 * width).astype(F4)
    first_send = dot_nt(d_projected[half:], qkv_here)
    first_keep = dot_nt(d_projected[:half], qkv_here)
    d_first = links.plane_reduce(first_keep, first_send)
    d_from_first, first_gain_grad, first_shift_grad = norm_backward(
        d_first, first_hat, first_inverse, first_gain
    )
    grad_in = (d_middle + d_from_first).astype(BF).reshape(1, tok_rows, width)

    ff_sums = jnp.stack([gate_sum, up_sum], 0).reshape(2, 2, nz, shard_rows, ff_cols)
    sums_keep = jnp.where(core == 0, ff_sums[:, 0], ff_sums[:, 1])
    sums_send = jnp.where(core == 0, ff_sums[:, 1], ff_sums[:, 0])
    sums_other = links.swap_core(sums_send)
    sums_first = jnp.where(core == 0, sums_keep, sums_other)
    sums_second = jnp.where(core == 0, sums_other, sums_keep)
    ff_sums = jnp.stack([sums_first, sums_second], 0).transpose(2, 0, 1, 3, 4)
    ff_sums = lax.all_to_all(ff_sums, "fsdp", split_axis=0, concat_axis=0, tiled=True)

    def ff_share(index):
        blocks = ff_sums[:, :, index].reshape(nz, 2, shard_rows, chips, ff_rows)
        return blocks.transpose(2, 3, 1, 0, 4).reshape(shard_rows, devices * ff_rows).astype(F4)

    placed = lax.dynamic_update_slice(
        jnp.zeros((3, ns, cols), F4), bias_grad, (0, links.s, 0)
    ).reshape(devices, -1)
    short_terms = jnp.concatenate(
        [
            first_gain_grad.reshape(devices, n),
            first_shift_grad.reshape(devices, n),
            second_gain_grad.reshape(devices, n),
            second_shift_grad.reshape(devices, n),
            placed,
        ],
        1,
    )
    short_sums = links.short_reduce(short_terms)
    return (
        layer_out.reshape(1, tok_rows, width),
        grad_in,
        short_sums[:n],
        short_sums[n : 2 * n],
        qkv_share,
        short_sums[4 * n :],
        out_share.astype(F4),
        short_sums[2 * n : 3 * n],
        short_sums[3 * n : 4 * n],
        ff_share(0),
        ff_share(1),
        down_share.astype(F4),
    )


def solution(mesh):
    both = ("seq", "fsdp")
    rows = P("fsdp", "seq", None)
    vector = P(both)
    matrix = P(both, None)
    return jax.shard_map(
        on_device,
        mesh=mesh,
        in_specs=(
            rows,
            P("fsdp", None),
            vector,
            vector,
            matrix,
            vector,
            matrix,
            vector,
            vector,
            matrix,
            matrix,
            matrix,
            rows,
        ),
        out_specs=(
            rows,
            rows,
            vector,
            vector,
            matrix,
            vector,
            matrix,
            vector,
            vector,
            matrix,
            matrix,
            matrix,
        ),
        check_vma=False,
    )
```

time: 4480 us -> 675 us (0.15)
  waiting for transfers between devices: 4060 us -> 251 us
  matrix products: 228 us -> 110 us
  starting transfers between devices: 29.5 us -> 123 us
  blocking collectives: 85.2 us -> 17.6 us
  local copies, waits for them, and re-layouts: 35 us -> 90.8 us
    reduce_scatter x5, waiting for transfers between devices: 3480 us -> 0.03 us  [the longest x3 0.02 us: chips_reduce(): lax.psum_scatter(rows_in, 'seq', scatter_dimension=0, tiled=True, axis_in...]
    all_gather x5, waiting for transfers between devices: 526 us -> 0.04 us  [the longest x1 0.02 us: on_device(): out_here = lax.all_gather(w_out, 'fsdp', axis=0, tiled=True)]
    ppermute x0 -> x74, waiting for transfers between devices: none -> 231 us  [the longest x5 65.8 us: short_reduce(): held = keep + lax.ppermute(send, axis, [(i, i ^ bit) for i in range(size)])]
    dot_general x27 -> x32, matrix products: 228 us -> 110 us  [the longest x8 35.8 us: dot_nt(): lax.dot_general(a, b, (((1,), (1,)), ((), ())), preferred_element_type=F4)]
    ppermute x0 -> x74, starting transfers between devices: none -> 104 us  [the longest x24 66.8 us: hop(): return lax.ppermute(values, 'fsdp', pairs)]
    unnamed x2 -> x0, blocking collectives: 85.2 us -> none
  transfers between devices with their start and end apart: 18 -> 87, of which waited for: 17 -> 32; matrix products, arithmetic and copies ran while one was open for 5% -> 33% of each run, Pallas kernels for 0% -> 0%
where the time goes in v1:
time: 675 us; the launch traced here: 666 us
  waiting for transfers between devices  251 us (37%)
  starting transfers between devices  123 us (18%)
  matrix products  110 us (16%)
  local copies, waits for them, and re-layouts  90.8 us (13%)
  other arithmetic  51.3 us (8%)
  between operations  21.9 us (3%)
  blocking collectives  17.6 us (3%)
    ppermute x24, starting transfers between devices, hop(): return lax.ppermute(values, 'fsdp', pairs)  66.8 us
    ppermute x5, waiting for transfers between devices, short_reduce(): held = keep + lax.ppermute(send, axis, [(i, i ^ bit) for i in range(size)])  65.8 us
    ppermute x24, waiting for transfers between devices, hop(): return lax.ppermute(values, 'fsdp', pairs)  63.3 us
    ppermute x40, waiting for transfers between devices, flip(): return lax.ppermute(values, 'seq', [(i, i ^ bit) for i in range(self.ns)])  52.1 us
    ppermute x5, waiting for transfers between devices, short_gather(): other = lax.ppermute(held, axis, [(i, i ^ bit) for i in range(size)])  50 us
    dot_general x8, matrix products, dot_nt(): lax.dot_general(a, b, (((1,), (1,)), ((), ())), preferred_element_type=F4)  35.8 us
    unnamed x200, local copies, waits for them, and re-layouts  33.4 us
    dot_general x7, matrix products, dot(): return jnp.dot(a, b, preferred_element_type=F4).astype(out)  31.3 us
  transfers between devices with their start and end apart: 87, of which 32 were waited for; matrix products, arithmetic and copies ran while one was open for 33% of the time, Pallas kernels for 0%

profile of v1, /device:TPU:0, one launch (start us, length us, event | category | flops | bytes accessed | tf_op | source)
XLA Modules:
  0.0 665.7 jit_solution(14523808142304439797)
XLA Ops:
  9.9 17.6 %all_to_all.20 = bf16[8,64,768]{2,1,0:T(8,128)(2,1)} all-to-all(bf16[8,64,768]{2,1,0:T(8,128)(2,1)S(1)} %reshape.487), channel_id=1, replica_groups=mesh['seq'=8,'fsdp'=4] {'seq'}, dimensions={0} | all-to-all | bytes 1572864 | tf_op jit(solution)/shard_map/all_to_all | solution.py:316
  30.9 4.4 reshape.495
  38.1 4.9 all-to-all-start.1
  45.8 48.6 %collective-permute-done = bf16[1,448]{1,0:T(2,128)(2,1)S(1)} collective-permute-done((bf16[1,448]{1,0:T(2,128)(2,1)S(1)}, bf16[1,448]{1,0:T(2,128)(2,1)S(1)}, u32[]{:S(2)}, u32[]{:S(2)}) %collective-permute-start) | collective-permute-done | bytes 928 | tf_op jit(solution)/shard_map/ppermute | solution.py:267
  94.4 4.8 collective-permute-start.1
  99.2 19.4 %all-to-all-done.1 = bf16[4,2,2,64,704]{4,3,1,2,0:T(8,128)(2,1)S(1)} async-done(((bf16[4,2,2,64,704]{4,3,1,2,0:T(8,128)(2,1)}), bf16[4,2,2,64,704]{4,3,1,2,0:T(8,128)(2,1)S(1)}, u32[]{:S(2)}, u32[]{:S(2)}) %all-to-all-start.1) | async-done | bytes 1441824 | tf_op jit(solution)/shard_map/all_to_all | solution.py:336
  140.1 9.4 %collective-permute-done.6 = bf16[128,2048]{1,0:T(8,128)(2,1)S(1)} collective-permute-done((bf16[128,2048]{1,0:T(8,128)(2,1)S(1)}, bf16[128,2048]{1,0:T(8,128)(2,1)S(1)}, u32[]{:S(2)}, u32[]{:S(2)}) %collective-permute-start.6) | collective-permute-done | bytes 524320 | tf_op jit(solution)/shard_map/ppermute | solution.py:149
  166.8 3.4 convolution_add_fusion
  199.7 4.8 collective-permute-start.37
  207.6 6.9 %collective-permute-done.38 = bf16[128,2048]{1,0:T(8,128)(2,1)S(1)} collective-permute-done((bf16[128,2048]{1,0:T(8,128)(2,1)}, bf16[128,2048]{1,0:T(8,128)(2,1)S(1)}, u32[]{:S(2)}, u32[]{:S(2)}) %collective-permute-start.38) | collective-permute-done | bytes 524320 | tf_op jit(solution)/shard_map/ppermute | solution.py:155
  231.7 9.6 %collective-permute-done.18 = bf16[128,2048]{1,0:T(8,128)(2,1)} collective-permute-done((bf16[128,2048]{1,0:T(8,128)(2,1)}, bf16[128,2048]{1,0:T(8,128)(2,1)}, u32[]{:S(2)}, u32[]{:S(2)}) %collective-permute-start.18) | collective-permute-done | bytes 524320 | tf_op jit(solution)/shard_map/ppermute | solution.py:149
  249.2 7.1 %collective-permute-start.19 = (bf16[128,2048]{1,0:T(8,128)(2,1)S(1)}, bf16[128,2048]{1,0:T(8,128)(2,1)S(1)}, u32[]{:S(2)}, u32[]{:S(2)}) collective-permute-start(bf16[128,2048]{1,0:T(8,128)(2,1)S(1)} %get-tuple-element.138), channel_id=1, source_target_pairs={{0,1},{1,2},{2,3},{4,5},{5,6},{6,7},{8,9},{9,10},{10,11},{12,13},{... | collective-permute-start | bytes 1572872 | tf_op jit(solution)/shard_map/ppermute | solution.py:155
  256.3 3.2 collective-permute-done.20
  262.3 5.4 collective-permute-done.19
  268.4 3.7 collective-permute-done.21
  274.4 12.2 %collective-permute-done.22 = bf16[128,2048]{1,0:T(8,128)(2,1)S(1)} collective-permute-done((bf16[128,2048]{1,0:T(8,128)(2,1)S(1)}, bf16[128,2048]{1,0:T(8,128)(2,1)S(1)}, u32[]{:S(2)}, u32[]{:S(2)}) %collective-permute-start.22) | collective-permute-done | bytes 524320 | tf_op jit(solution)/shard_map/ppermute | solution.py:155
  293.5 8.0 %fusion.156 = f32[1024,704]{0,1:T(8,128)} fusion(bf16[1024,2048]{1,0:T(8,128)(2,1)} %constant_dynamic-update-slice_fusion.10, bf16[2048,704]{1,0:T(8,128)(2,1)} %all-gather.11.cloned.1.call-done), kind=kOutput, calls=%fused_computation.408 | convolution fusion | flops 2952790016 | bytes 9961472 | tf_op jit(solution)/shard_map/dot_general | solution.py:17
  301.4 8.0 %fusion.155 = f32[1024,704]{0,1:T(8,128)} fusion(bf16[1024,2048]{1,0:T(8,128)(2,1)} %constant_dynamic-update-slice_fusion.10, bf16[2048,704]{1,0:T(8,128)(2,1)} %all-gather.9.cloned.1.call-done), kind=kOutput, calls=%fused_computation.407 | convolution fusion | flops 2952790016 | bytes 9961472 | tf_op jit(solution)/shard_map/dot_general | solution.py:17
  309.4 10.5 %multiply_convert_fusion.2 = (bf16[1024,704]{0,1:T(8,128)(2,1)S(1)}, bf16[1024,704]{0,1:T(8,128)(2,1)}, bf16[1024,704]{0,1:T(8,128)(2,1)}) fusion(f32[1024,704]{0,1:T(8,128)} %fusion.155, f32[1024,704]{0,1:T(8,128)} %fusion.156, bf16[1024,2048]{1,0:T(8,128)(2,1)} %copy-done.41, bf16[704,2048]{1,0:T(8,128)(2,1)} %all-gather.13.cloned.1.call-done), kind=kOutput, calls=%fused_computation.33 | convolution fusion | flops 2964324352 | bytes 17170432 | tf_op jit(solution)/shard_map/dot_general | solution.py:21
  321.0 6.7 %convolution_convert_fusion.1 = bf16[2048,704]{0,1:T(8,128)(2,1)} fusion(bf16[1024,704]{0,1:T(8,128)(2,1)S(1)} %get-tuple-element.143, bf16[1024,2048]{1,0:T(8,128)(2,1)} %constant_dynamic-update-slice_fusion.10), kind=kOutput, calls=%fused_computation.24 | convolution fusion | flops 2954231808 | bytes 8519680 | tf_op jit(solution)/shard_map/dot_general | solution.py:25
  328.2 5.4 convolution_convert_fusion.6
  336.4 3.2 add_convert_fusion
  339.7 6.7 %convolution_convert_fusion.2 = bf16[2048,704]{0,1:T(8,128)(2,1)} fusion(bf16[1024,704]{0,1:T(8,128)(2,1)S(1)} %copy-done.74, bf16[1024,2048]{1,0:T(8,128)(2,1)} %constant_dynamic-update-slice_fusion.10), kind=kOutput, calls=%fused_computation.25 | convolution fusion | flops 2954231808 | bytes 8519680 | tf_op jit(solution)/shard_map/dot_general | solution.py:25
  346.5 4.1 fusion.75
  350.6 3.7 convert_add_fusion.2
  356.7 3.6 convert_add_fusion.1
  362.7 5.6 collective-permute-done.31
  369.1 5.0 collective-permute-start.33
  374.2 5.3 collective-permute-done.48
  380.4 10.3 %collective-permute-start.50 = (bf16[128,2048]{1,0:T(8,128)(2,1)S(1)}, bf16[128,2048]{1,0:T(8,128)(2,1)S(1)}, u32[]{:S(2)}, u32[]{:S(2)}) collective-permute-start(bf16[128,2048]{1,0:T(8,128)(2,1)S(1)} %fusion.40), channel_id=1, source_target_pairs={{0,1},{1,2},{4,5},{5,6},{8,9},{9,10},{12,13},{13,14},{16,17},{17,1... | collective-permute-start | bytes 1572872 | tf_op jit(solution)/shard_map/ppermute | solution.py:155
  391.1 9.8 %collective-permute-start.34 = (bf16[128,2048]{1,0:T(8,128)(2,1)S(1)}, bf16[128,2048]{1,0:T(8,128)(2,1)S(1)}, u32[]{:S(2)}, u32[]{:S(2)}) collective-permute-start(bf16[128,2048]{1,0:T(8,128)(2,1)S(1)} %get-tuple-element.152), channel_id=1, source_target_pairs={{0,1},{1,2},{2,3},{4,5},{5,6},{6,7},{8,9},{9,10},{10,11},{12,13},{... | collective-permute-start | bytes 1572872 | tf_op jit(solution)/shard_map/ppermute | solution.py:155
  402.8 10.2 %collective-permute-start.51 = (bf16[128,2048]{1,0:T(8,128)(2,1)S(1)}, bf16[128,2048]{1,0:T(8,128)(2,1)S(1)}, u32[]{:S(2)}, u32[]{:S(2)}) collective-permute-start(bf16[128,2048]{1,0:T(8,128)(2,1)S(1)} %get-tuple-element.148), channel_id=1, source_target_pairs={{0,1},{1,2},{2,3},{4,5},{5,6},{6,7},{8,9},{9,10},{10,11},{12,13},{... | collective-permute-start | bytes 1572872 | tf_op jit(solution)/shard_map/ppermute | solution.py:155
  415.0 7.1 %collective-permute-done.36 = bf16[128,2048]{1,0:T(8,128)(2,1)S(1)} collective-permute-done((bf16[128,2048]{1,0:T(8,128)(2,1)S(1)}, bf16[128,2048]{1,0:T(8,128)(2,1)S(1)}, u32[]{:S(2)}, u32[]{:S(2)}) %collective-permute-start.36) | collective-permute-done | bytes 524320 | tf_op jit(solution)/shard_map/ppermute | solution.py:155
  424.1 8.9 %collective-permute-done.53 = bf16[128,2048]{1,0:T(8,128)(2,1)S(1)} collective-permute-done((bf16[128,2048]{1,0:T(8,128)(2,1)S(1)}, bf16[128,2048]{1,0:T(8,128)(2,1)S(1)}, u32[]{:S(2)}, u32[]{:S(2)}) %collective-permute-start.53) | collective-permute-done | bytes 524320 | tf_op jit(solution)/shard_map/ppermute | solution.py:155
  440.6 4.5 convolution_convert_fusion.3
  445.2 6.4 collective-permute-done.55
  456.5 7.0 %collective-permute-done.57 = bf16[64,2048]{1,0:T(8,128)(2,1)S(1)} collective-permute-done((bf16[64,2048]{1,0:T(8,128)(2,1)S(1)}, bf16[64,2048]{1,0:T(8,128)(2,1)S(1)}, u32[]{:S(2)}, u32[]{:S(2)}) %collective-permute-start.57) | collective-permute-done | bytes 262176 | tf_op jit(solution)/shard_map/ppermute | solution.py:149
  471.0 3.5 convolution_convert_fusion.8
  475.5 3.3 multiply_reduce_fusion.1
  498.6 5.2 convolution_convert_fusion.5
  504.3 4.2 convolution_convert_fusion
  510.5 3.8 fusion.154
  516.5 6.2 collective-permute-done.66
  548.5 8.8 %all-to-all-start.3 = ((bf16[4,2,2,64,704]{4,3,2,1,0:T(8,128)(2,1)}), bf16[4,2,2,64,704]{4,3,2,1,0:T(8,128)(2,1)S(1)}, u32[]{:S(2)}, u32[]{:S(2)}) async-start(bf16[4,2,2,64,704]{4,3,2,1,0:T(8,128)(2,1)} %copy.177), calls=%async_computation.7 | async-start | bytes 3145728 | tf_op jit(solution)/shard_map/all_to_all | solution.py:441
  563.4 62.7 %collective-permute-done.71 = f32[2,448]{1,0:T(2,128)S(1)} collective-permute-done((f32[2,448]{1,0:T(2,128)S(1)}, f32[2,448]{1,0:T(2,128)S(1)}, u32[]{:S(2)}, u32[]{:S(2)}) %collective-permute-start.71) | collective-permute-done | bytes 3616 | tf_op jit(solution)/shard_map/ppermute | solution.py:280
  628.7 3.9 all-to-all-start.2
  641.5 4.0 reshape.522
  651.3 4.0 reshape.521
  (544 shorter events, 229.0 us)
Async XLA Ops:
  7.2 156.4 %all-gather.15.cloned.1.call-start = ((), (), s32[]{:S(2)}) async-start(), calls=%async_computation.18 | async-start | bytes 3932160 | tf_op jit(solution)/shard_map/all_gather | solution.py:317
  38.1 80.4 %all-to-all-start.1 = ((bf16[4,2,2,64,704]{4,3,1,2,0:T(8,128)(2,1)}), bf16[4,2,2,64,704]{4,3,1,2,0:T(8,128)(2,1)S(1)}, u32[]{:S(2)}, u32[]{:S(2)}) async-start(bf16[4,2,2,64,704]{4,3,1,2,0:T(8,128)(2,1)} %copy.155), calls=%async_computation.1 | async-start | bytes 3145728 | tf_op jit(solution)/shard_map/all_to_all | solution.py:336
  43.0 152.7 %all-gather.7.cloned.1.call-start = ((), (), s32[]{:S(2)}) async-start(), calls=%async_computation.9 | async-start | bytes 1310720 | tf_op jit(solution)/shard_map/all_gather | solution.py:319
  43.2 51.2 %collective-permute-start = (bf16[1,448]{1,0:T(2,128)(2,1)S(1)}, bf16[1,448]{1,0:T(2,128)(2,1)S(1)}, u32[]{:S(2)}, u32[]{:S(2)}) collective-permute-start(bf16[1,448]{1,0:T(2,128)(2,1)S(1)} %broadcast_in_dim.36), channel_id=1, source_target_pairs={{0,1},{1,0},{2,3},{3,2},{4,5},{5,4},{6,7},{7,6},{8,9},{9,8},{10,11... | collective-permute-start | bytes 2696 | tf_op jit(solution)/shard_map/ppermute | solution.py:267
  45.3 248.2 %all-gather.11.cloned.1.call-start = ((), (), s32[]{:S(2)}) async-start(), calls=%async_computation.11 | async-start | bytes 3932160 | tf_op jit(solution)/shard_map/all_gather | solution.py:245
  94.4 25.5 %collective-permute-start.1 = (bf16[2,448]{1,0:T(2,128)(2,1)S(1)}, bf16[2,448]{1,0:T(2,128)(2,1)S(1)}, u32[]{:S(2)}, u32[]{:S(2)}) collective-permute-start(bf16[2,448]{1,0:T(2,128)(2,1)S(1)} %pad_maximum_fusion.24), channel_id=1, source_target_pairs={{0,2},{1,3},{2,0},{3,1},{4,6},{5,7},{6,4},{7,5},{8,10},{9,11},{10,... | collective-permute-start | bytes 5384 | tf_op jit(solution)/shard_map/ppermute | solution.py:267
  125.7 175.7 %all-gather.9.cloned.1.call-start = ((), (), s32[]{:S(2)}) async-start(), calls=%async_computation.10 | async-start | bytes 3932160 | tf_op jit(solution)/shard_map/all_gather | solution.py:245
  139.9 18.7 %collective-permute-start.9 = (bf16[128,2048]{1,0:T(8,128)(2,1)S(1)}, bf16[128,2048]{1,0:T(8,128)(2,1)S(1)}, u32[]{:S(2)}, u32[]{:S(2)}) collective-permute-start(bf16[128,2048]{1,0:T(8,128)(2,1)S(1)} %get-tuple-element.142), channel_id=1, source_target_pairs={{0,4},{4,0},{8,12},{12,8},{16,20},{20,16},{24,28},{28,24},{1,5},{5... | collective-permute-start | bytes 1572872 | tf_op jit(solution)/shard_map/ppermute | solution.py:149
  163.6 145.9 %all-gather.13.cloned.1.call-start = ((), (), s32[]{:S(2)}) async-start(), calls=%async_computation.12 | async-start | bytes 3604480 | tf_op jit(solution)/shard_map/all_gather | solution.py:245
  198.4 16.1 %collective-permute-start.38 = (bf16[128,2048]{1,0:T(8,128)(2,1)}, bf16[128,2048]{1,0:T(8,128)(2,1)S(1)}, u32[]{:S(2)}, u32[]{:S(2)}) collective-permute-start(bf16[128,2048]{1,0:T(8,128)(2,1)} %bitcast.34), channel_id=1, source_target_pairs={{3,2},{2,1},{1,0},{7,6},{6,5},{5,4},{11,10},{10,9},{9,8},{15,14},{... | collective-permute-start | bytes 1572872 | tf_op jit(solution)/shard_map/ppermute | solution.py:155
  199.7 16.1 %collective-permute-start.37 = (bf16[128,2048]{1,0:T(8,128)(2,1)}, bf16[128,2048]{1,0:T(8,128)(2,1)S(1)}, u32[]{:S(2)}, u32[]{:S(2)}) collective-permute-start(bf16[128,2048]{1,0:T(8,128)(2,1)} %bitcast.34), channel_id=1, source_target_pairs={{0,1},{1,2},{2,3},{4,5},{5,6},{6,7},{8,9},{9,10},{10,11},{12,13},{... | collective-permute-start | bytes 1572872 | tf_op jit(solution)/shard_map/ppermute | solution.py:155
  214.5 15.2 %collective-permute-start.39 = (bf16[128,2048]{1,0:T(8,128)(2,1)S(1)}, bf16[128,2048]{1,0:T(8,128)(2,1)}, u32[]{:S(2)}, u32[]{:S(2)}) collective-permute-start(bf16[128,2048]{1,0:T(8,128)(2,1)S(1)} %collective-permute-done.38), channel_id=1, source_target_pairs={{2,1},{1,0},{6,5},{5,4},{10,9},{9,8},{14,13},{13,12},{18,17},{17,1... | collective-permute-start | bytes 1572872 | tf_op jit(solution)/shard_map/ppermute | solution.py:155
  215.8 15.2 %collective-permute-start.41 = (bf16[128,2048]{1,0:T(8,128)(2,1)S(1)}, bf16[128,2048]{1,0:T(8,128)(2,1)}, u32[]{:S(2)}, u32[]{:S(2)}) collective-permute-start(bf16[128,2048]{1,0:T(8,128)(2,1)S(1)} %collective-permute-done.37), channel_id=1, source_target_pairs={{1,2},{2,3},{5,6},{6,7},{9,10},{10,11},{13,14},{14,15},{17,18},{18... | collective-permute-start | bytes 1572872 | tf_op jit(solution)/shard_map/ppermute | solution.py:155
  220.5 20.8 %collective-permute-start.18 = (bf16[128,2048]{1,0:T(8,128)(2,1)}, bf16[128,2048]{1,0:T(8,128)(2,1)}, u32[]{:S(2)}, u32[]{:S(2)}) collective-permute-start(bf16[128,2048]{1,0:T(8,128)(2,1)} %pad_maximum_fusion.8), channel_id=1, source_target_pairs={{0,16},{4,20},{8,24},{12,28},{16,0},{20,4},{24,8},{28,12},{1,17},{... | collective-permute-start | bytes 1572872 | tf_op jit(solution)/shard_map/ppermute | solution.py:149
  222.5 20.0 %collective-permute-start.16 = (bf16[128,2048]{1,0:T(8,128)(2,1)}, bf16[128,2048]{1,0:T(8,128)(2,1)}, u32[]{:S(2)}, u32[]{:S(2)}) collective-permute-start(bf16[128,2048]{1,0:T(8,128)(2,1)} %pad_maximum_fusion.7), channel_id=1, source_target_pairs={{0,8},{4,12},{8,0},{12,4},{16,24},{20,28},{24,16},{28,20},{1,9},{5... | collective-permute-start | bytes 1572872 | tf_op jit(solution)/shard_map/ppermute | solution.py:149
  222.8 38.2 %collective-permute-start.43 = (bf16[128,2048]{1,0:T(8,128)(2,1)}, bf16[128,2048]{1,0:T(8,128)(2,1)}, u32[]{:S(2)}, u32[]{:S(2)}) collective-permute-start(bf16[128,2048]{1,0:T(8,128)(2,1)} %bitcast.34), channel_id=1, source_target_pairs={{0,4},{4,0},{8,12},{12,8},{16,20},{20,16},{24,28},{28,24},{1,5},{5... | collective-permute-start | bytes 1572872 | tf_op jit(solution)/shard_map/ppermute | solution.py:149
  222.9 304.7 %reduce-scatter.12.cloned.1.call-start = ((), (), s32[]{:S(2)}) async-start(), calls=%async_computation.16 | async-start | bytes 3604480 | tf_op jit(solution)/shard_map/reduce_scatter | solution.py:248
  229.7 17.5 %collective-permute-start.40 = (bf16[128,2048]{1,0:T(8,128)(2,1)}, bf16[128,2048]{1,0:T(8,128)(2,1)S(1)}, u32[]{:S(2)}, u32[]{:S(2)}) collective-permute-start(bf16[128,2048]{1,0:T(8,128)(2,1)} %collective-permute-done.39), channel_id=1, source_target_pairs={{1,0},{5,4},{9,8},{13,12},{17,16},{21,20},{25,24},{29,28}} | collective-permute-start | bytes 1572872 | tf_op jit(solution)/shard_map/ppermute | solution.py:155
  231.0 18.2 %collective-permute-start.42 = (bf16[128,2048]{1,0:T(8,128)(2,1)}, bf16[128,2048]{1,0:T(8,128)(2,1)S(1)}, u32[]{:S(2)}, u32[]{:S(2)}) collective-permute-start(bf16[128,2048]{1,0:T(8,128)(2,1)} %collective-permute-done.41), channel_id=1, source_target_pairs={{2,3},{6,7},{10,11},{14,15},{18,19},{22,23},{26,27},{30,31}} | collective-permute-start | bytes 1572872 | tf_op jit(solution)/shard_map/ppermute | solution.py:155
  248.6 24.8 %collective-permute-start.45 = (bf16[128,2048]{1,0:T(8,128)(2,1)S(1)}, bf16[128,2048]{1,0:T(8,128)(2,1)S(1)}, u32[]{:S(2)}, u32[]{:S(2)}) collective-permute-start(bf16[128,2048]{1,0:T(8,128)(2,1)S(1)} %get-tuple-element.126), channel_id=1, source_target_pairs={{0,4},{4,0},{8,12},{12,8},{16,20},{20,16},{24,28},{28,24},{1,5},{5... | collective-permute-start | bytes 1572872 | tf_op jit(solution)/shard_map/ppermute | solution.py:149
  248.7 24.7 %collective-permute-start.44 = (bf16[128,2048]{1,0:T(8,128)(2,1)S(1)}, bf16[128,2048]{1,0:T(8,128)(2,1)S(1)}, u32[]{:S(2)}, u32[]{:S(2)}) collective-permute-start(bf16[128,2048]{1,0:T(8,128)(2,1)S(1)} %get-tuple-element.128), channel_id=1, source_target_pairs={{0,4},{4,0},{8,12},{12,8},{16,20},{20,16},{24,28},{28,24},{1,5},{5... | collective-permute-start | bytes 1572872 | tf_op jit(solution)/shard_map/ppermute | solution.py:149
  249.2 18.5 %collective-permute-start.19 = (bf16[128,2048]{1,0:T(8,128)(2,1)S(1)}, bf16[128,2048]{1,0:T(8,128)(2,1)S(1)}, u32[]{:S(2)}, u32[]{:S(2)}) collective-permute-start(bf16[128,2048]{1,0:T(8,128)(2,1)S(1)} %get-tuple-element.138), channel_id=1, source_target_pairs={{0,1},{1,2},{2,3},{4,5},{5,6},{6,7},{8,9},{9,10},{10,11},{12,13},{... | collective-permute-start | bytes 1572872 | tf_op jit(solution)/shard_map/ppermute | solution.py:155
  272.1 14.5 %collective-permute-start.22 = (bf16[128,2048]{1,0:T(8,128)(2,1)S(1)}, bf16[128,2048]{1,0:T(8,128)(2,1)S(1)}, u32[]{:S(2)}, u32[]{:S(2)}) collective-permute-start(bf16[128,2048]{1,0:T(8,128)(2,1)S(1)} %collective-permute-done.21), channel_id=1, source_target_pairs={{1,0},{5,4},{9,8},{13,12},{17,16},{21,20},{25,24},{29,28}} | collective-permute-start | bytes 1572872 | tf_op jit(solution)/shard_map/ppermute | solution.py:155
  273.6 16.5 %collective-permute-start.25 = (bf16[128,2048]{1,0:T(8,128)(2,1)S(1)}, bf16[128,2048]{1,0:T(8,128)(2,1)S(1)}, u32[]{:S(2)}, u32[]{:S(2)}) collective-permute-start(bf16[128,2048]{1,0:T(8,128)(2,1)S(1)} %get-tuple-element.138), channel_id=1, source_target_pairs={{0,4},{4,0},{8,12},{12,8},{16,20},{20,16},{24,28},{28,24},{1,5},{5... | collective-permute-start | bytes 1572872 | tf_op jit(solution)/shard_map/ppermute | solution.py:149
  273.7 15.4 %collective-permute-start.24 = (bf16[128,2048]{1,0:T(8,128)(2,1)S(1)}, bf16[128,2048]{1,0:T(8,128)(2,1)S(1)}, u32[]{:S(2)}, u32[]{:S(2)}) collective-permute-start(bf16[128,2048]{1,0:T(8,128)(2,1)S(1)} %collective-permute-done.23), channel_id=1, source_target_pairs={{2,3},{6,7},{10,11},{14,15},{18,19},{22,23},{26,27},{30,31}} | collective-permute-start | bytes 1572872 | tf_op jit(solution)/shard_map/ppermute | solution.py:155
  327.7 201.3 %reduce-scatter.10.cloned.1.call-start = ((), (), s32[]{:S(2)}) async-start(), calls=%async_computation.15 | async-start | bytes 3604480 | tf_op jit(solution)/shard_map/reduce_scatter | solution.py:248
  333.6 17.0 %collective-permute-start.30 = (bf16[512,2048]{1,0:T(8,128)(2,1)}, bf16[512,2048]{1,0:T(8,128)(2,1)}, u32[]{:S(2)}, u32[]{:S(2)}) collective-permute-start(bf16[512,2048]{1,0:T(8,128)(2,1)} %convolution_convert_fusion.6), channel_id=1, source_target_pairs={{0,4},{4,0},{8,12},{12,8},{16,20},{20,16},{24,28},{28,24},{1,5},{5... | collective-permute-start | bytes 6291464 | tf_op jit(solution)/shard_map/ppermute | solution.py:149
  339.6 17.0 %collective-permute-start.47 = (bf16[512,2048]{1,0:T(8,128)(2,1)}, bf16[512,2048]{1,0:T(8,128)(2,1)}, u32[]{:S(2)}, u32[]{:S(2)}) collective-permute-start(bf16[512,2048]{1,0:T(8,128)(2,1)} %add_convert_fusion), channel_id=1, source_target_pairs={{0,4},{4,0},{8,12},{12,8},{16,20},{20,16},{24,28},{28,24},{1,5},{5... | collective-permute-start | bytes 6291464 | tf_op jit(solution)/shard_map/ppermute | solution.py:149
  346.4 185.4 %reduce-scatter.14.cloned.1.call-start = ((), (), s32[]{:S(2)}) async-start(), calls=%async_computation.17 | async-start | bytes 3604480 | tf_op jit(solution)/shard_map/reduce_scatter | solution.py:248
  354.5 13.7 %collective-permute-start.31 = (bf16[128,2048]{1,0:T(8,128)(2,1)S(1)}, bf16[128,2048]{1,0:T(8,128)(2,1)S(1)}, u32[]{:S(2)}, u32[]{:S(2)}) collective-permute-start(bf16[128,2048]{1,0:T(8,128)(2,1)S(1)} %get-tuple-element.154), channel_id=1, source_target_pairs={{0,1},{4,5},{8,9},{12,13},{16,17},{20,21},{24,25},{28,29}} | collective-permute-start | bytes 1572872 | tf_op jit(solution)/shard_map/ppermute | solution.py:155
  360.4 19.0 %collective-permute-start.48 = (bf16[128,2048]{1,0:T(8,128)(2,1)S(1)}, bf16[128,2048]{1,0:T(8,128)(2,1)S(1)}, u32[]{:S(2)}, u32[]{:S(2)}) collective-permute-start(bf16[128,2048]{1,0:T(8,128)(2,1)S(1)} %get-tuple-element.150), channel_id=1, source_target_pairs={{0,1},{4,5},{8,9},{12,13},{16,17},{20,21},{24,25},{28,29}} | collective-permute-start | bytes 1572872 | tf_op jit(solution)/shard_map/ppermute | solution.py:155
  362.0 17.5 %collective-permute-start.49 = (bf16[128,2048]{1,0:T(8,128)(2,1)S(1)}, bf16[128,2048]{1,0:T(8,128)(2,1)S(1)}, u32[]{:S(2)}, u32[]{:S(2)}) collective-permute-start(bf16[128,2048]{1,0:T(8,128)(2,1)S(1)} %get-tuple-element.151), channel_id=1, source_target_pairs={{3,2},{7,6},{11,10},{15,14},{19,18},{23,22},{27,26},{31,30}} | collective-permute-start | bytes 1572872 | tf_op jit(solution)/shard_map/ppermute | solution.py:155
  368.4 22.3 %collective-permute-start.35 = (bf16[128,2048]{1,0:T(8,128)(2,1)S(1)}, bf16[128,2048]{1,0:T(8,128)(2,1)S(1)}, u32[]{:S(2)}, u32[]{:S(2)}) collective-permute-start(bf16[128,2048]{1,0:T(8,128)(2,1)S(1)} %fusion.43), channel_id=1, source_target_pairs={{3,2},{2,1},{7,6},{6,5},{11,10},{10,9},{15,14},{14,13},{19,18},{18... | collective-permute-start | bytes 1572872 | tf_op jit(solution)/shard_map/ppermute | solution.py:155
  369.1 21.6 %collective-permute-start.33 = (bf16[128,2048]{1,0:T(8,128)(2,1)S(1)}, bf16[128,2048]{1,0:T(8,128)(2,1)S(1)}, u32[]{:S(2)}, u32[]{:S(2)}) collective-permute-start(bf16[128,2048]{1,0:T(8,128)(2,1)S(1)} %fusion.43), channel_id=1, source_target_pairs={{0,1},{1,2},{4,5},{5,6},{8,9},{9,10},{12,13},{13,14},{16,17},{17,1... | collective-permute-start | bytes 1572872 | tf_op jit(solution)/shard_map/ppermute | solution.py:155
  379.7 22.6 %collective-permute-start.52 = (bf16[128,2048]{1,0:T(8,128)(2,1)S(1)}, bf16[128,2048]{1,0:T(8,128)(2,1)S(1)}, u32[]{:S(2)}, u32[]{:S(2)}) collective-permute-start(bf16[128,2048]{1,0:T(8,128)(2,1)S(1)} %fusion.40), channel_id=1, source_target_pairs={{3,2},{2,1},{7,6},{6,5},{11,10},{10,9},{15,14},{14,13},{19,18},{18... | collective-permute-start | bytes 1572872 | tf_op jit(solution)/shard_map/ppermute | solution.py:155
  380.4 22.1 %collective-permute-start.50 = (bf16[128,2048]{1,0:T(8,128)(2,1)S(1)}, bf16[128,2048]{1,0:T(8,128)(2,1)S(1)}, u32[]{:S(2)}, u32[]{:S(2)}) collective-permute-start(bf16[128,2048]{1,0:T(8,128)(2,1)S(1)} %fusion.40), channel_id=1, source_target_pairs={{0,1},{1,2},{4,5},{5,6},{8,9},{9,10},{12,13},{13,14},{16,17},{17,1... | collective-permute-start | bytes 1572872 | tf_op jit(solution)/shard_map/ppermute | solution.py:155
  391.1 23.9 %collective-permute-start.34 = (bf16[128,2048]{1,0:T(8,128)(2,1)S(1)}, bf16[128,2048]{1,0:T(8,128)(2,1)S(1)}, u32[]{:S(2)}, u32[]{:S(2)}) collective-permute-start(bf16[128,2048]{1,0:T(8,128)(2,1)S(1)} %get-tuple-element.152), channel_id=1, source_target_pairs={{0,1},{1,2},{2,3},{4,5},{5,6},{6,7},{8,9},{9,10},{10,11},{12,13},{... | collective-permute-start | bytes 1572872 | tf_op jit(solution)/shard_map/ppermute | solution.py:155
  401.0 21.1 %collective-permute-start.36 = (bf16[128,2048]{1,0:T(8,128)(2,1)S(1)}, bf16[128,2048]{1,0:T(8,128)(2,1)S(1)}, u32[]{:S(2)}, u32[]{:S(2)}) collective-permute-start(bf16[128,2048]{1,0:T(8,128)(2,1)S(1)} %get-tuple-element.153), channel_id=1, source_target_pairs={{3,2},{2,1},{1,0},{7,6},{6,5},{5,4},{11,10},{10,9},{9,8},{15,14},{... | collective-permute-start | bytes 1572872 | tf_op jit(solution)/shard_map/ppermute | solution.py:155
  402.8 21.3 %collective-permute-start.51 = (bf16[128,2048]{1,0:T(8,128)(2,1)S(1)}, bf16[128,2048]{1,0:T(8,128)(2,1)S(1)}, u32[]{:S(2)}, u32[]{:S(2)}) collective-permute-start(bf16[128,2048]{1,0:T(8,128)(2,1)S(1)} %get-tuple-element.148), channel_id=1, source_target_pairs={{0,1},{1,2},{2,3},{4,5},{5,6},{6,7},{8,9},{9,10},{10,11},{12,13},{... | collective-permute-start | bytes 1572872 | tf_op jit(solution)/shard_map/ppermute | solution.py:155
  413.0 20.0 %collective-permute-start.53 = (bf16[128,2048]{1,0:T(8,128)(2,1)S(1)}, bf16[128,2048]{1,0:T(8,128)(2,1)S(1)}, u32[]{:S(2)}, u32[]{:S(2)}) collective-permute-start(bf16[128,2048]{1,0:T(8,128)(2,1)S(1)} %get-tuple-element.149), channel_id=1, source_target_pairs={{3,2},{2,1},{1,0},{7,6},{6,5},{5,4},{11,10},{10,9},{9,8},{15,14},{... | collective-permute-start | bytes 1572872 | tf_op jit(solution)/shard_map/ppermute | solution.py:155
  438.2 14.9 %collective-permute-start.54 = (bf16[128,2048]{1,0:T(8,128)(2,1)}, bf16[128,2048]{1,0:T(8,128)(2,1)S(1)}, u32[]{:S(2)}, u32[]{:S(2)}) collective-permute-start(bf16[128,2048]{1,0:T(8,128)(2,1)} %get-tuple-element.120), channel_id=1, source_target_pairs={{0,8},{4,12},{8,0},{12,4},{16,24},{20,28},{24,16},{28,20},{1,9},{5... | collective-permute-start | bytes 1572872 | tf_op jit(solution)/shard_map/ppermute | solution.py:149
  445.1 112.2 %reduce-scatter.8.cloned.1.call-start = ((), (), s32[]{:S(2)}) async-start(), calls=%async_computation.14 | async-start | bytes 1310720 | tf_op jit(solution)/shard_map/reduce_scatter | solution.py:403
  445.1 21.9 %collective-permute-start.58 = (bf16[128,2048]{1,0:T(8,128)(2,1)}, bf16[128,2048]{1,0:T(8,128)(2,1)S(1)}, u32[]{:S(2)}, u32[]{:S(2)}) collective-permute-start(bf16[128,2048]{1,0:T(8,128)(2,1)} %get-tuple-element.120), channel_id=1, source_target_pairs={{0,4},{4,0},{8,12},{12,8},{16,20},{20,16},{24,28},{28,24},{1,5},{5... | collective-permute-start | bytes 1572872 | tf_op jit(solution)/shard_map/ppermute | solution.py:149
  454.3 14.4 %collective-permute-start.60 = (bf16[128,2048]{1,0:T(8,128)(2,1)S(1)}, bf16[128,2048]{1,0:T(8,128)(2,1)S(1)}, u32[]{:S(2)}, u32[]{:S(2)}) collective-permute-start(bf16[128,2048]{1,0:T(8,128)(2,1)S(1)} %collective-permute-done.55), channel_id=1, source_target_pairs={{0,4},{4,0},{8,12},{12,8},{16,20},{20,16},{24,28},{28,24},{1,5},{5... | collective-permute-start | bytes 1572872 | tf_op jit(solution)/shard_map/ppermute | solution.py:149
  498.5 130.2 %reduce-scatter.6.cloned.1.call-start = ((), (), s32[]{:S(2)}) async-start(), calls=%async_computation.13 | async-start | bytes 3932160 | tf_op jit(solution)/shard_map/reduce_scatter | solution.py:421
  548.5 80.2 %all-to-all-start.3 = ((bf16[4,2,2,64,704]{4,3,2,1,0:T(8,128)(2,1)}), bf16[4,2,2,64,704]{4,3,2,1,0:T(8,128)(2,1)S(1)}, u32[]{:S(2)}, u32[]{:S(2)}) async-start(bf16[4,2,2,64,704]{4,3,2,1,0:T(8,128)(2,1)} %copy.177), calls=%async_computation.7 | async-start | bytes 3145728 | tf_op jit(solution)/shard_map/all_to_all | solution.py:441
  560.4 65.7 %collective-permute-start.71 = (f32[2,448]{1,0:T(2,128)S(1)}, f32[2,448]{1,0:T(2,128)S(1)}, u32[]{:S(2)}, u32[]{:S(2)}) collective-permute-start(f32[2,448]{1,0:T(2,128)S(1)} %broadcast_select_fusion.14), channel_id=1, source_target_pairs={{0,2},{1,3},{2,0},{3,1},{4,6},{5,7},{6,4},{7,5},{8,10},{9,11},{10,... | collective-permute-start | bytes 10760 | tf_op jit(solution)/shard_map/ppermute | solution.py:280
  628.7 26.6 %all-to-all-start.2 = ((bf16[8,64,768]{2,1,0:T(8,128)(2,1)}), bf16[8,64,768]{2,1,0:T(8,128)(2,1)S(1)}, u32[]{:S(2)}, u32[]{:S(2)}) async-start(bf16[8,64,768]{2,1,0:T(8,128)(2,1)} %bitcast.285), calls=%async_computation.3 | async-start | bytes 1572864 | tf_op jit(solution)/shard_map/all_to_all | solution.py:423
  (116 other events, 1033.3 us)
Sparse Core Ops, SparseCore 0:
  27.7 96.1 all-gather.14
  125.5 26.4 all-gather.6
  154.4 43.4 all-gather.10
  200.2 50.9 all-gather.8
  252.9 41.6 all-gather.12
  327.8 51.0 reduce-scatter.11
  382.0 41.7 reduce-scatter.9
  445.2 49.3 reduce-scatter.13
  498.6 33.1 reduce-scatter.7
  534.1 83.9 reduce-scatter.5

commit v2 on v1

v2 whole, which is shorter than its diff:
```python
import jax
import jax.numpy as jnp
from jax import lax
from jax.experimental import pallas as pl
from jax.experimental.pallas import tpu as pltpu
from jax.sharding import PartitionSpec as P

HD = 64
ROT = 16

EPS = 1e-05
NEG = -1e30

BF = jnp.bfloat16
F4 = jnp.float32


def dot(a, b, out=F4):
    return jnp.dot(a, b, preferred_element_type=F4).astype(out)


def dot_nt(a, b):
    return lax.dot_general(a, b, (((1,), (1,)), ((), ())), preferred_element_type=F4)


def dot_tn(a, b):
    return lax.dot_general(a, b, (((0,), (0,)), ((), ())), preferred_element_type=F4)


def layer_norm(values, gain_row, shift_row):
    row_mean = jnp.mean(values, axis=1, keepdims=True)
    centred = values - row_mean
    inverse = lax.rsqrt(jnp.mean(centred * centred, axis=1, keepdims=True) + EPS)
    normed = centred * inverse
    return (normed * gain_row.astype(F4) + shift_row.astype(F4), normed, inverse)


def norm_backward(grad_rows, normed, inverse, gain_row):
    scaled = grad_rows * gain_row.astype(F4)
    inner_term = (
        scaled
        - jnp.mean(scaled, axis=1, keepdims=True)
        - normed * jnp.mean(scaled * normed, axis=1, keepdims=True)
    )
    return (inner_term * inverse, jnp.sum(grad_rows * normed, axis=0), jnp.sum(grad_rows, axis=0))


def angle_tables(places):
    half_rot = ROT // 2
    frequency = 10000.0 ** (-2.0 * jnp.arange(half_rot, dtype=F4) / ROT)
    angles = places.astype(F4)[:, None] * frequency[None, :]
    return (
        jnp.concatenate([jnp.cos(angles), jnp.cos(angles)], 1),
        jnp.concatenate([jnp.sin(angles), jnp.sin(angles)], 1),
    )


def busy(microseconds):
    return pl.CostEstimate(
        flops=int(microseconds * 1e9), bytes_accessed=0, transcendentals=0
    )


VMEM_BYTES = 56 << 20
BLOCK = 256


def kernel_dot(a, b, contract):
    return lax.dot_general(a, b, (contract, ((), ())), preferred_element_type=F4)


NN = ((1,), (0,))
NT = ((1,), (1,))


def copy_all(pairs, sems):
    copies = [pltpu.make_async_copy(a, b, sems.at[i]) for i, (a, b) in enumerate(pairs)]
    for copy in copies:
        copy.start()
    for copy in copies:
        copy.wait()


def piece_rows(place, pieces, chunk):
    return [
        0 if at is None else pl.multiple_of((place ^ at) * chunk + start, 16)
        for _, at, start in pieces
    ]


def turned(rows, tables, backward):
    plain, ahead, behind = tables
    width = rows.shape[1]
    half = ROT // 2
    moved = pltpu.roll(rows, width - half, 1) * ahead + pltpu.roll(rows, half, 1) * behind
    return rows * plain - moved if backward else rows * plain + moved


def rotary_tables(places, cols):
    half = ROT // 2
    cosine, sine = angle_tables(places)
    rows = places.shape[0]
    rest = jnp.zeros((rows, HD - ROT), F4)
    none = jnp.zeros((rows, half), F4)
    plain = jnp.concatenate([cosine, rest + 1.0], 1)
    ahead = jnp.concatenate([-sine[:, :half], none, rest], 1)
    behind = jnp.concatenate([none, sine[:, half:], rest], 1)
    return [jnp.tile(table, (1, cols // HD)) for table in (plain, ahead, behind)]


def head_lanes(shape, head):
    return lax.broadcasted_iota(jnp.int32, shape, 1) // HD == head


def attend(place, pieces, gain, shift, qkv_line, bias, tables, order, chunk):
    line, plane, shard, three = qkv_line.shape
    cols = three // 3
    width = line * plane * shard
    length = tables[0].shape[0]
    heads = cols // HD
    count = len(pieces)
    block = min(BLOCK, length)
    score_scale = HD ** (-0.5)

    def kernel(place_ref, *refs):
        piece_refs = refs[:count]
        w_ref, gain_ref, shift_ref, bias_ref, plain_ref, ahead_ref, behind_ref = refs[
            count : count + 7
        ]
        n_ref, q_ref, k_ref, v_ref, o_ref, rel_ref, lse_ref, w_held, sems = refs[count + 7 :]
        here = place_ref[0]
        starts = piece_rows(here, pieces, chunk)
        pairs = [
            (ref, n_ref.at[pl.ds(at, ref.shape[0])]) for ref, at in zip(piece_refs, starts)
        ]
        for f in range(line):
            for s in range(plane):
                pairs.append((w_ref.at[f, s], w_held.at[pl.ds((s * line + f) * shard, shard)]))
        copy_all(pairs, sems)

        def project(i, carry):
            rows = pl.ds(pl.multiple_of(i * block, block), block)
            raw = n_ref[rows, :].astype(F4)
            centred = raw - jnp.mean(raw, axis=1, keepdims=True)
            inverse = lax.rsqrt(jnp.mean(centred * centred, axis=1, keepdims=True) + EPS)
            normed = (centred * inverse * gain_ref[...] + shift_ref[...]).astype(BF)
            n_ref[rows, :] = normed
            found = kernel_dot(normed, w_held[...], NN) + bias_ref[...]
            factors = (plain_ref[rows, :], ahead_ref[rows, :], behind_ref[rows, :])
            q_ref[rows, :] = turned(found[:, :cols], factors, False).astype(BF)
            k_ref[rows, :] = turned(found[:, cols : 2 * cols], factors, False).astype(BF)
            v_ref[rows, :] = found[:, 2 * cols :].astype(BF)
            return carry

        lax.fori_loop(0, length // block, project, 0)
        for i in range(length // block):
            rows = slice(i * block, (i + 1) * block)
            seen = (i + 1) * block
            q_rows = q_ref[rows, :]
            k_rows = k_ref[:seen, :]
            v_rows = v_ref[:seen, :]
            allowed = (
                lax.broadcasted_iota(jnp.int32, (block, seen), 1)
                <= lax.broadcasted_iota(jnp.int32, (block, seen), 0) + i * block
            )
            found = jnp.zeros((block, cols), F4)
            totals = jnp.zeros((block, 128), F4)
            for h in range(heads):
                mine = head_lanes((block, cols), h)
                scores = kernel_dot(jnp.where(mine, q_rows, jnp.zeros_like(q_rows)), k_rows, NT)
                scores = jnp.where(allowed, scores * score_scale, NEG)
                peak = jnp.max(scores, axis=1, keepdims=True)
                weights = jnp.exp(scores - peak)
                total = jnp.sum(weights, axis=1, keepdims=True)
                weights = (weights * (1.0 / total)).astype(BF)
                found = jnp.where(mine, kernel_dot(weights, v_rows, NN), found)
                lane = lax.broadcasted_iota(jnp.int32, (block, 128), 1)
                totals = jnp.where(lane == h, peak + jnp.log(total), totals)
            o_ref[rows, :] = found.astype(BF)
            lse_ref[rows, :] = totals
        if order is None:
            rel_ref[...] = o_ref[...]
        else:
            for k, at in enumerate(order):
                start = pl.multiple_of((here ^ at) * chunk, chunk)
                rel_ref[pl.ds(k * chunk, chunk), :] = o_ref[pl.ds(start, chunk), :]

    anywhere = pl.BlockSpec(memory_space=pl.ANY)
    whole = pl.BlockSpec(memory_space=pltpu.VMEM)
    tall = jax.ShapeDtypeStruct((length, cols), BF)
    return pl.pallas_call(
        kernel,
        out_shape=[
            jax.ShapeDtypeStruct((length, width), BF),
            tall,
            tall,
            tall,
            tall,
            tall,
            jax.ShapeDtypeStruct((length, 128), F4),
        ],
        in_specs=[pl.BlockSpec(memory_space=pltpu.SMEM)] + [anywhere] * (count + 1) + [whole] * 6,
        out_specs=[whole] * 7,
        scratch_shapes=[
            pltpu.VMEM((width, three), BF),
            pltpu.SemaphoreType.DMA((count + line * plane,)),
        ],
        compiler_params=pltpu.CompilerParams(vmem_limit_bytes=VMEM_BYTES),
        cost_estimate=busy(17),
        name="attend",
    )(place, *[piece for piece, _, _ in pieces], qkv_line, gain, shift, bias, *tables)


def attend_back(place, pieces, out_here, q, k, v, lse, tables, order, chunk):
    length, cols = q.shape
    width = out_here.shape[1]
    heads = cols // HD
    count = len(pieces)
    block = min(BLOCK, length)
    score_scale = HD ** (-0.5)

    def kernel(place_ref, *refs):
        piece_refs = refs[:count]
        out_ref, q_ref, k_ref, v_ref, lse_ref, plain_ref, ahead_ref, behind_ref = refs[
            count : count + 8
        ]
        d_ref, all_ref, rel_ref, sum_ref, do_ref, delta_ref, dq_ref, dk_ref, sems = refs[count + 8 :]
        here = place_ref[0]
        starts = piece_rows(here, pieces, chunk)
        copy_all(
            [(ref, d_ref.at[pl.ds(at, ref.shape[0])]) for ref, at in zip(piece_refs, starts)], sems
        )

        def project(i, carry):
            rows = pl.ds(pl.multiple_of(i * block, block), block)
            do_ref[rows, :] = kernel_dot(d_ref[rows, :], out_ref[...], NT).astype(BF)
            return carry

        lax.fori_loop(0, length // block, project, 0)
        for i in range(length // block):
            rows = slice(i * block, (i + 1) * block)
            seen = (i + 1) * block
            q_rows, do_rows = q_ref[rows, :], do_ref[rows, :]
            k_rows, v_rows = k_ref[:seen, :], v_ref[:seen, :]
            allowed = (
                lax.broadcasted_iota(jnp.int32, (block, seen), 1)
                <= lax.broadcasted_iota(jnp.int32, (block, seen), 0) + i * block
            )
            found = jnp.zeros((block, cols), F4)
            deltas = jnp.zeros((block, 128), F4)
            for h in range(heads):
                mine = head_lanes((block, cols), h)
                none = jnp.zeros_like(q_rows)
                scores = kernel_dot(jnp.where(mine, q_rows, none), k_rows, NT) * score_scale
                probs = jnp.where(allowed, jnp.exp(scores - lse_ref[rows, h : h + 1]), 0.0)
                d_probs = kernel_dot(jnp.where(mine, do_rows, none), v_rows, NT)
                delta = jnp.sum(probs * d_probs, axis=1, keepdims=True)
                d_scores = (probs * (d_probs - delta)).astype(BF)
                found = jnp.where(mine, kernel_dot(d_scores, k_rows, NN), found)
                lane = lax.broadcasted_iota(jnp.int32, (block, 128), 1)
                deltas = jnp.where(lane == h, delta, deltas)
            dq_ref[rows, :] = (found * score_scale).astype(BF)
            delta_ref[rows, :] = deltas
        lse_rows = jnp.transpose(lse_ref[...])
        delta_rows = jnp.transpose(delta_ref[...])
        for j in range(length // block):
            rows = slice(j * block, (j + 1) * block)
            left = length - j * block
            k_rows, v_rows = k_ref[rows, :], v_ref[rows, :]
            q_rows, do_rows = q_ref[j * block :, :], do_ref[j * block :, :]
            allowed = lax.broadcasted_iota(jnp.int32, (block, left), 0) <= lax.broadcasted_iota(
                jnp.int32, (block, left), 1
            )
            keys = jnp.zeros((block, cols), F4)
            values = jnp.zeros((block, cols), F4)
            for h in range(heads):
                mine = head_lanes((block, cols), h)
                none = jnp.zeros_like(k_rows)
                scores = kernel_dot(jnp.where(mine, k_rows, none), q_rows, NT) * score_scale
                lse_row = lse_rows[h : h + 1, j * block :]
                probs = jnp.where(allowed, jnp.exp(scores - lse_row), 0.0)
                d_probs = kernel_dot(jnp.where(mine, v_rows, none), do_rows, NT)
                d_scores = (probs * (d_probs - delta_rows[h : h + 1, j * block :])).astype(BF)
                keys = jnp.where(mine, kernel_dot(d_scores, q_rows, NN), keys)
                values = jnp.where(mine, kernel_dot(probs.astype(BF), do_rows, NN), values)
            dk_ref[rows, :] = (keys * score_scale).astype(BF)
            all_ref[rows, 2 * cols :] = values.astype(BF)

        sum_ref[...] = jnp.zeros_like(sum_ref)

        def finish(i, carry):
            rows = pl.ds(pl.multiple_of(i * block, block), block)
            factors = (plain_ref[rows, :], ahead_ref[rows, :], behind_ref[rows, :])
            all_ref[rows, :cols] = turned(dq_ref[rows, :].astype(F4), factors, True).astype(BF)
            all_ref[rows, cols : 2 * cols] = turned(
                dk_ref[rows, :].astype(F4), factors, True
            ).astype(BF)
            sum_ref[...] += jnp.sum(all_ref[rows, :].astype(F4), axis=0, keepdims=True)
            return carry

        lax.fori_loop(0, length // block, finish, 0)
        if order is None:
            rel_ref[...] = all_ref[...]
        else:
            for n, at in enumerate(order):
                start = pl.multiple_of((here ^ at) * chunk, chunk)
                rel_ref[pl.ds(n * chunk, chunk), :] = all_ref[pl.ds(start, chunk), :]

    anywhere = pl.BlockSpec(memory_space=pl.ANY)
    whole = pl.BlockSpec(memory_space=pltpu.VMEM)
    wide = jax.ShapeDtypeStruct((length, 3 * cols), BF)
    return pl.pallas_call(
        kernel,
        out_shape=[
            jax.ShapeDtypeStruct((length, width), BF),
            wide,
            wide,
            jax.ShapeDtypeStruct((1, 3 * cols), F4),
        ],
        in_specs=[pl.BlockSpec(memory_space=pltpu.SMEM)] + [anywhere] * count + [whole] * 8,
        out_specs=[whole] * 4,
        scratch_shapes=[
            pltpu.VMEM((length, cols), BF),
            pltpu.VMEM((length, 128), F4),
            pltpu.VMEM((length, cols), BF),
            pltpu.VMEM((length, cols), BF),
            pltpu.SemaphoreType.DMA((count,)),
        ],
        compiler_params=pltpu.CompilerParams(vmem_limit_bytes=VMEM_BYTES),
        cost_estimate=busy(26),
        name="attend_back",
    )(place, *[piece for piece, _, _ in pieces], out_here, q, k, v, lse, *tables)


def outer_rows(left, pieces):
    count = len(pieces)
    starts, length = [], 0
    for piece in pieces:
        starts.append(length)
        length += piece.shape[0]
    cols, width = left.shape[1], pieces[0].shape[1]

    def kernel(left_ref, *refs):
        held, sems = refs[count + 1 :]
        copy_all(
            [(ref, held.at[pl.ds(at, ref.shape[0])]) for ref, at in zip(refs[:count], starts)], sems
        )
        refs[count][...] = kernel_dot(left_ref[...], held[...], ((0,), (0,))).astype(BF)

    anywhere = pl.BlockSpec(memory_space=pl.ANY)
    whole = pl.BlockSpec(memory_space=pltpu.VMEM)
    return pl.pallas_call(
        kernel,
        out_shape=jax.ShapeDtypeStruct((cols, width), BF),
        in_specs=[whole] + [anywhere] * count,
        out_specs=whole,
        scratch_shapes=[pltpu.VMEM((length, width), BF), pltpu.SemaphoreType.DMA((count,))],
        compiler_params=pltpu.CompilerParams(vmem_limit_bytes=VMEM_BYTES),
        cost_estimate=busy(4),
        name="outer_rows",
    )(left, *pieces)


def feed(pieces, grads, ff_line):
    line, plane, shard, both = ff_line.shape
    cols = both // 2
    width = line * plane * shard
    count = len(pieces)
    starts, length = [], 0
    for piece in pieces:
        starts.append(length)
        length += piece.shape[0]
    block = min(512, length)
    copies = 2 * count + line * plane

    def kernel(*refs):
        piece_refs, grad_refs = refs[:count], refs[count : 2 * count]
        ff_ref = refs[2 * count]
        n_ref, g_ref, a_ref, both_ref, w_held, sems = refs[2 * count + 1 :]
        pairs = []
        for f in range(line):
            for s in range(plane):
                pairs.append((ff_ref.at[f, s], w_held.at[pl.ds((s * line + f) * shard, shard)]))
        for held, found in ((n_ref, piece_refs), (g_ref, grad_refs)):
            for ref, at in zip(found, starts):
                pairs.append((ref, held.at[pl.ds(at, ref.shape[0])]))
        copy_all(pairs, sems)

        def step(i, carry):
            rows = pl.ds(pl.multiple_of(i * block, block), block)
            gate_up = kernel_dot(n_ref[rows, :], w_held[...], NN)
            both_ref[rows, :] = gate_up
            gate, up = gate_up[:, :cols], gate_up[:, cols:]
            a_ref[rows, :] = (gate / (1.0 + jnp.exp(-gate)) * up).astype(BF)
            return carry

        lax.fori_loop(0, length // block, step, 0)

    anywhere = pl.BlockSpec(memory_space=pl.ANY)
    whole = pl.BlockSpec(memory_space=pltpu.VMEM)
    return pl.pallas_call(
        kernel,
        out_shape=[
            jax.ShapeDtypeStruct((length, width), BF),
            jax.ShapeDtypeStruct((length, width), BF),
            jax.ShapeDtypeStruct((length, cols), BF),
            jax.ShapeDtypeStruct((length, both), F4),
        ],
        in_specs=[anywhere] * (2 * count + 1),
        out_specs=[whole] * 4,
        scratch_shapes=[pltpu.VMEM((width, both), BF), pltpu.SemaphoreType.DMA((copies,))],
        compiler_params=pltpu.CompilerParams(vmem_limit_bytes=VMEM_BYTES),
        cost_estimate=busy(17),
        name="feed",
    )(*pieces, *grads, ff_line)


def feed_back(grad_rows, gate_up, ff_line, down_here):
    line, plane, shard, both = ff_line.shape
    cols = both // 2
    length, width = grad_rows.shape
    half = length // 2
    block = min(512, half)

    def kernel(g_ref, both_ref, ff_ref, down_ref, d_ref, send_ref, keep_ref, w_held, sems):
        pairs = []
        for f in range(line):
            for s in range(plane):
                pairs.append((ff_ref.at[f, s], w_held.at[pl.ds((s * line + f) * shard, shard)]))
        copies = [pltpu.make_async_copy(a, b, sems.at[i]) for i, (a, b) in enumerate(pairs)]
        for copy in copies:
            copy.start()

        def step(i, carry):
            rows = pl.ds(pl.multiple_of(i * block, block), block)
            d_hidden = kernel_dot(g_ref[rows, :], down_ref[...], NT)
            gate, up = both_ref[rows, :cols], both_ref[rows, cols:]
            sigmoid = 1.0 / (1.0 + jnp.exp(-gate))
            d_gate = d_hidden * up * sigmoid * (1.0 + gate * (1.0 - sigmoid))
            d_ref[rows, :] = jnp.concatenate([d_gate, d_hidden * gate * sigmoid], 1).astype(BF)
            return carry

        lax.fori_loop(0, length // block, step, 0)
        for copy in copies:
            copy.wait()

        def back(i, carry):
            rows = pl.ds(pl.multiple_of(i * block, block), block)
            there = pl.ds(pl.multiple_of(half + i * block, block), block)
            send_ref[rows, :] = kernel_dot(d_ref[there, :], w_held[...], NT).astype(BF)
            keep_ref[rows, :] = kernel_dot(d_ref[rows, :], w_held[...], NT)
            return carry

        lax.fori_loop(0, half // block, back, 0)

    anywhere = pl.BlockSpec(memory_space=pl.ANY)
    whole = pl.BlockSpec(memory_space=pltpu.VMEM)
    return pl.pallas_call(
        kernel,
        out_shape=[
            jax.ShapeDtypeStruct((length, both), BF),
            jax.ShapeDtypeStruct((half, width), BF),
            jax.ShapeDtypeStruct((half, width), F4),
        ],
        in_specs=[whole, whole, anywhere, whole],
        out_specs=[whole] * 3,
        scratch_shapes=[
            pltpu.VMEM((width, both), BF),
            pltpu.SemaphoreType.DMA((line * plane,)),
        ],
        compiler_params=pltpu.CompilerParams(vmem_limit_bytes=VMEM_BYTES),
        cost_estimate=busy(17),
        name="feed_back",
    )(grad_rows, gate_up, ff_line, down_here)


def nothing(*refs):
    pass


def turn(values, *earlier):
    anywhere = pl.BlockSpec(memory_space=pl.ANY)
    return pl.pallas_call(
        nothing,
        out_shape=[jax.ShapeDtypeStruct(v.shape, v.dtype) for v in values],
        in_specs=[anywhere] * (len(values) + len(earlier)),
        out_specs=[anywhere] * len(values),
        input_output_aliases={i: i for i in range(len(values))},
        cost_estimate=pl.CostEstimate(flops=0, bytes_accessed=0, transcendentals=0),
        name="in_turn",
    )(*values, *earlier)


def after(values, *earlier):
    return turn([values], *earlier)[0]


def pair_columns(gate, up, lists):
    rows, width = gate.shape
    part = width // sum(len(blocks) for blocks in lists)

    def kernel(gate_ref, up_ref, blocks_ref):
        whole = [gate_ref[...].astype(F4), up_ref[...].astype(F4)]
        for i, blocks in enumerate(lists):
            columns = [w[:, at * part : (at + 1) * part] for w in whole for at in blocks]
            blocks_ref[i] = jnp.concatenate(columns, 1).astype(BF)

    held = 2 * part * len(lists[0])
    return pl.pallas_call(
        kernel,
        out_shape=jax.ShapeDtypeStruct((len(lists), rows, held), BF),
        compiler_params=pltpu.CompilerParams(vmem_limit_bytes=32 << 20),
        name="pair_columns",
    )(gate, up)


def part_columns(blocks, lists):
    parts, rows, held = blocks.shape
    count = len(lists[0])
    part = held // (2 * count)
    width = parts * count * part
    place = {at: (i, j) for i, each in enumerate(lists) for j, at in enumerate(each)}

    def kernel(blocks_ref, first_ref, second_ref):
        whole = [blocks_ref[i].astype(F4) for i in range(parts)]
        for k, ref in enumerate((first_ref, second_ref)):
            columns = []
            for at in range(parts * count):
                i, j = place[at]
                start = (k * count + j) * part
                columns.append(whole[i][:, start : start + part])
            ref[...] = jnp.concatenate(columns, 1)

    return pl.pallas_call(
        kernel,
        out_shape=[jax.ShapeDtypeStruct((rows, width), F4)] * 2,
        compiler_params=pltpu.CompilerParams(vmem_limit_bytes=32 << 20),
        name="part_columns",
    )(blocks)


class Links:
    def __init__(self):
        self.ns = lax.axis_size("seq")
        self.nz = lax.axis_size("fsdp")
        self.s = lax.axis_index("seq")
        self.z = lax.axis_index("fsdp")
        self.core = self.s % 2
        self.fast_plane = self.ns == 8
        self.order = [0, 2, 4, 6, 1, 3, 5, 7]

    def flip(self, values, bit):
        return lax.ppermute(values, "seq", [(i, i ^ bit) for i in range(self.ns)])

    def swap_core(self, values):
        return self.flip(values, 1)

    def hop(self, values, pairs):
        return lax.ppermute(values, "fsdp", pairs)

    def along_x(self, values):
        return self.flip(values, 2)

    def along_y(self, values):
        return self.flip(values, 4)

    def square_gather(self, own, one, two, codes):
        cut = own.shape[0] // 32 * 16
        first = one(own)
        second = two(own)
        return [
            (own, 0, 0),
            (first, codes[0], 0),
            (second, codes[1], 0),
            (two(first[:cut]), codes[0] | codes[1], 0),
            (one(second[cut:]), codes[0] | codes[1], cut),
        ]

    def with_core(self, found):
        return found + [(self.swap_core(part), at | 1, start) for part, at, start in found]

    def square_reduce(self, own, first, second, far, one, two):
        return self.square_reduce_end(
            self.square_reduce_start(own, first, second, far, one, two), one, two
        )

    def square_reduce_start(self, own, first, second, far, one, two):
        cut = far.shape[0] // 32 * 16
        far = far.astype(BF)
        via_one = one(far[:cut])
        via_two = two(far[cut:])
        second = jnp.concatenate([second[:cut] + via_one.astype(F4), second[cut:]], 0).astype(BF)
        first = jnp.concatenate([first[:cut], first[cut:] + via_two.astype(F4)], 0).astype(BF)
        return [own, first, second]

    def square_reduce_end(self, parts, one, two):
        own, first, second = parts
        return own + one(first).astype(F4) + two(second).astype(F4)

    def core_sum(self, keep, send, *earlier):
        other = self.swap_core(send.astype(BF))
        return keep + (after(other, *earlier) if earlier else other).astype(F4)

    def plane_gather(self, own):
        if not self.fast_plane:
            return [(lax.all_gather(own, "seq", axis=0, tiled=True), None, 0)]
        return self.with_core(self.square_gather(own, self.along_x, self.along_y, (2, 4)))

    def plane_reduce(self, keep, send):
        if not self.fast_plane:
            terms = jnp.concatenate([keep, send], 0).astype(BF)
            return lax.psum_scatter(terms, "seq", scatter_dimension=0, tiled=True).astype(F4)
        pair = self.core_sum(keep, send)
        rows = pair.shape[0] // 4
        terms = [pair[i * rows : (i + 1) * rows] for i in range(4)]
        return self.square_reduce(*terms, self.along_x, self.along_y)

    def line_gather(self, own):
        return lax.all_gather(own, "fsdp", axis=0, tiled=True)

    def line_reduce(self, terms):
        return lax.psum_scatter(terms, "fsdp", scatter_dimension=0, tiled=True)

    def swap_blocks(self, blocks):
        return lax.all_to_all(blocks, "seq", split_axis=0, concat_axis=0, tiled=True)

    def rows_sorted(self, blocks):
        return blocks.transpose(1, 0, 2, 3).reshape(-1, blocks.shape[3])

    def rows_by_line(self, rows_in, shard_rows):
        shape = (self.ns, self.nz, shard_rows, rows_in.shape[1])
        return rows_in.reshape(shape).transpose(1, 0, 2, 3)

    def ff_lists(self):
        return [[s * self.nz + f for f in range(self.nz)] for s in range(self.ns)]

    def short_gather_line(self, own):
        held = own[None, :]
        for k in range(1, self.nz):
            other = lax.ppermute(own, "fsdp", [(i, i ^ k) for i in range(self.nz)])
            held = jnp.concatenate([held, other[None, :]], 0)
        bit = 1
        while bit < self.nz:
            pairs = held.reshape(-1, 2, bit, own.shape[0])
            held = jnp.where((self.z & bit) != 0, pairs[:, ::-1], pairs).reshape(held.shape)
            bit *= 2
        return held

    def short_gather_plane(self, held):
        bit = 1
        while bit < self.ns:
            other = self.flip(held, bit)
            high = (self.s & bit) != 0
            first = jnp.where(high, other, held)
            second = jnp.where(high, held, other)
            held = jnp.concatenate([first, second], 0)
            bit *= 2
        return held

    def short_reduce(self, held):
        bit = self.ns // 2
        while bit:
            half = held.shape[0] // 2
            high = (self.s & bit) != 0
            keep = jnp.where(high, held[half:], held[:half])
            send = jnp.where(high, held[:half], held[half:])
            held = keep + self.flip(send, bit)
            bit //= 2
        total = lax.dynamic_index_in_dim(held, self.z, 0, keepdims=False)
        for k in range(1, self.nz):
            send = lax.dynamic_index_in_dim(held, self.z ^ k, 0, keepdims=False)
            total = total + lax.ppermute(send, "fsdp", [(i, i ^ k) for i in range(self.nz)])
        return total


def on_device(
    hidden_in,
    positions,
    norm1_gain,
    norm1_shift,
    w_qkv,
    b_qkv,
    w_out,
    norm2_gain,
    norm2_shift,
    w_gate,
    w_up,
    w_down,
    grad_out,
):
    links = Links()
    ns, nz = links.ns, links.nz
    devices = ns * nz
    tok_rows = hidden_in.shape[1]
    width = hidden_in.shape[2]
    shard_rows = w_qkv.shape[0]
    seq_places = positions[0]
    length = seq_places.shape[0]
    cols = width // ns
    score_scale = HD ** (-0.5)

    lists = links.ff_lists()
    out_here = links.line_gather(w_out)
    short = jnp.concatenate([norm1_gain, norm1_shift, norm2_gain, norm2_shift, b_qkv])
    short_line = links.short_gather_line(short)
    qkv_blocks = w_qkv.reshape(shard_rows, 3, ns, cols).transpose(2, 0, 1, 3)
    qkv_blocks = links.swap_blocks(qkv_blocks.reshape(ns, shard_rows, 3 * cols))
    qkv_blocks, short_line = turn([qkv_blocks, short_line], out_here)
    qkv_line = links.line_gather(qkv_blocks[None])
    ff_blocks = links.swap_blocks(pair_columns(w_gate, w_up, lists))

    short_all = links.short_gather_plane(short_line)
    short_all, w_down = turn([short_all, w_down])
    n = shard_rows
    first_gain = short_all[:, :n].reshape(-1)
    first_shift = short_all[:, n : 2 * n].reshape(-1)
    second_gain = short_all[:, 2 * n : 3 * n].reshape(-1)
    second_shift = short_all[:, 3 * n : 4 * n].reshape(-1)
    bias_all = short_all[:, 4 * n :].reshape(3, ns, cols)
    bias_here = lax.dynamic_index_in_dim(bias_all, links.s, 1, keepdims=False).reshape(3 * cols)

    place = jnp.stack([links.s, links.z]).astype(jnp.int32)
    order = links.order if links.fast_plane else None
    inputs = hidden_in.reshape(tok_rows, width).astype(F4)
    _, first_hat, first_inverse = layer_norm(inputs, first_gain, first_shift)
    first_pieces = links.plane_gather(hidden_in.reshape(tok_rows, width))
    cotangent_low = grad_out.reshape(tok_rows, width)
    tables = rotary_tables(seq_places, cols)
    half = length // 2

    def let(values, *earlier):
        flat = turn([v for group in values for v in group], *earlier)
        found = []
        for group in values:
            found.append(list(flat[: len(group)]))
            flat = flat[len(group) :]
        return found

    def arrays(pieces):
        return [piece for piece, _, _ in pieces]

    def renewed(pieces, values):
        return [(value, at, start) for value, (_, at, start) in zip(values, pieces)]

    vectors = [v.astype(F4)[None] for v in (first_gain, first_shift, bias_here)]
    found, vectors, (ff_blocks, cotangent_low) = let(
        [arrays(first_pieces), vectors, [ff_blocks, cotangent_low]]
    )
    found, vectors, (ff_blocks, w_down, cotangent_low) = let(
        [found, vectors, [ff_blocks, w_down, cotangent_low]], qkv_line
    )
    first_pieces = renewed(first_pieces, found)
    ff_line = links.line_gather(ff_blocks[None])
    down_here = links.line_gather(after(w_down, ff_line))
    cotangent_pieces = arrays(links.plane_gather(cotangent_low))
    normed_rows, queries, keys, values, mixed, mixed_rel, log_totals = attend(
        place,
        first_pieces,
        vectors[0],
        vectors[1],
        qkv_line,
        vectors[2],
        tables,
        order,
        tok_rows,
    )
    out_send = dot(mixed_rel[half:], out_here, BF)
    out_keep = dot(mixed_rel[:half], out_here)
    middle = inputs + links.plane_reduce(out_keep, out_send)

    second_normed, second_hat, second_inverse = layer_norm(middle, second_gain, second_shift)
    second_low = second_normed.astype(BF)
    second_pieces = arrays(links.plane_gather(second_low))
    second_rows, cotangent_rows, hidden_mid, gate_up = feed(
        second_pieces, cotangent_pieces, ff_line
    )
    down_grad = dot_tn(hidden_mid, cotangent_rows).astype(BF)
    down_sum = links.line_reduce(down_grad)
    grad_rows, gate_up = turn([cotangent_rows, gate_up], down_grad)
    d_ff, second_send, second_keep = feed_back(grad_rows, gate_up, ff_line, down_here)
    ff_grad = links.rows_by_line(dot_tn(second_rows, d_ff).astype(BF), shard_rows)
    ff_sum = links.line_reduce(after(ff_grad, down_sum)).reshape(ns, shard_rows, -1)
    second_send, second_keep = turn([second_send, second_keep], ff_grad)
    d_second = links.plane_reduce(second_keep, second_send)
    d_second = after(d_second, down_sum)
    d_from_norm, second_gain_grad, second_shift_grad = norm_backward(
        d_second, second_hat, second_inverse, second_gain
    )
    d_middle = cotangent_low.astype(F4) + d_from_norm
    d_middle_pieces = links.plane_gather(d_middle.astype(BF))
    out_grad = outer_rows(mixed_rel, arrays(d_middle_pieces))
    d_middle_rows, d_projected, d_projected_rel, bias_grad = attend_back(
        place,
        d_middle_pieces,
        out_here,
        queries,
        keys,
        values,
        log_totals,
        tables,
        order,
        tok_rows,
    )
    qkv_here = links.rows_sorted(qkv_line)
    first_send = dot_nt(d_projected_rel[half:], qkv_here).astype(BF)
    d_projected = after(d_projected, first_send)
    qkv_grad = links.rows_by_line(dot_tn(normed_rows, d_projected).astype(BF), shard_rows)
    qkv_sum = links.line_reduce(after(qkv_grad, ff_sum))
    out_share = links.line_reduce(after(out_grad, qkv_sum))
    qkv_sum = qkv_sum.reshape(ns, shard_rows, -1)
    bias_grad = bias_grad.reshape(3, 1, cols)

    hidden_later = after(hidden_mid, d_middle_rows)
    layer_send = dot(hidden_later[half:], down_here, BF)
    layer_keep = dot(hidden_later[:half], down_here)
    layer_out = (middle + links.plane_reduce(layer_keep, layer_send)).astype(BF)

    first_keep = dot_nt(d_projected_rel[:half], qkv_here)
    d_first = links.plane_reduce(first_keep, first_send)
    d_from_first, first_gain_grad, first_shift_grad = norm_backward(
        d_first, first_hat, first_inverse, first_gain
    )
    grad_in = (d_middle + d_from_first).astype(BF).reshape(1, tok_rows, width)

    placed = lax.dynamic_update_slice(
        jnp.zeros((3, ns, cols), F4), bias_grad, (0, links.s, 0)
    ).reshape(devices, -1)
    short_terms = jnp.concatenate(
        [
            first_gain_grad.reshape(devices, n),
            first_shift_grad.reshape(devices, n),
            second_gain_grad.reshape(devices, n),
            second_shift_grad.reshape(devices, n),
            placed,
        ],
        1,
    )
    short_sums = links.short_reduce(short_terms)

    gate_share, up_share = part_columns(links.swap_blocks(ff_sum), lists)
    qkv_share = links.swap_blocks(qkv_sum).reshape(ns, shard_rows, 3, cols).transpose(1, 2, 0, 3)
    qkv_share = qkv_share.reshape(shard_rows, 3 * width).astype(F4)
    return (
        layer_out.reshape(1, tok_rows, width),
        grad_in,
        short_sums[:n],
        short_sums[n : 2 * n],
        qkv_share,
        short_sums[4 * n :],
        out_share.astype(F4),
        short_sums[2 * n : 3 * n],
        short_sums[3 * n : 4 * n],
        gate_share,
        up_share,
        down_sum.astype(F4),
    )


def solution(mesh):
    both = ("seq", "fsdp")
    rows = P("fsdp", "seq", None)
    vector = P(both)
    matrix = P(both, None)
    return jax.shard_map(
        on_device,
        mesh=mesh,
        in_specs=(
            rows,
            P("fsdp", None),
            vector,
            vector,
            matrix,
            vector,
            matrix,
            vector,
            vector,
            matrix,
            matrix,
            matrix,
            rows,
        ),
        out_specs=(
            rows,
            rows,
            vector,
            vector,
            matrix,
            vector,
            matrix,
            vector,
            vector,
            matrix,
            matrix,
            matrix,
        ),
        check_vma=False,
    )
```

time: 675 us -> 553 us (0.82)
  Pallas kernels: 0 us -> 89.9 us
  matrix products: 110 us -> 39.2 us
  local copies, waits for them, and re-layouts: 90.8 us -> 40 us
  starting transfers between devices: 123 us -> 76.3 us
  other arithmetic: 51.3 us -> 25.9 us
  blocking collectives: 17.6 us -> 0 us
  waiting for transfers between devices: 251 us -> 262 us
    ppermute x34 -> x6, waiting for transfers between devices: 179 us -> 5.15 us  [the longest x3 5.14 us: short_gather_line(): other = lax.ppermute(own, 'fsdp', [(i, i ^ k) for i in range(self.nz)])]
    pallas_call x0 -> x20, Pallas kernels: none -> 89.9 us  [the longest x1 26 us: attend_back(): pl.pallas_call(kernel, out_shape=[jax.ShapeDtypeStruct((length, width), B...]
    ppermute x40 -> x62, waiting for transfers between devices: 52.1 us -> 133 us  [flip(): return lax.ppermute(values, 'seq', [(i, i ^ bit) for i in range(self.ns)])]
    all_gather x5 -> x4, waiting for transfers between devices: 0.04 us -> 80.3 us  [line_gather(): return lax.all_gather(own, 'fsdp', axis=0, tiled=True)]
    ppermute x34 -> x6, starting transfers between devices: 82 us -> 8.84 us  [the longest x3 4.45 us: short_reduce(): lax.ppermute(send, 'fsdp', [(i, i ^ k) for i in range(self.nz)])]
    reduce_scatter x5 -> x4, waiting for transfers between devices: 0.03 us -> 33.8 us  [line_reduce(): return lax.psum_scatter(terms, 'fsdp', scatter_dimension=0, tiled=True)]
    dot_general x8 -> x2, matrix products: 35.8 us -> 7.91 us  [dot_nt(): lax.dot_general(a, b, (((1,), (1,)), ((), ())), preferred_element_type=F4)]
    ppermute x40 -> x62, starting transfers between devices: 22.1 us -> 49.5 us  [flip(): return lax.ppermute(values, 'seq', [(i, i ^ bit) for i in range(self.ns)])]
  transfers between devices with their start and end apart: 87 -> 80, of which waited for: 32 -> 41; matrix products, arithmetic and copies ran while one was open for 33% -> 17% of each run, Pallas kernels for 0% -> 16%
where the time goes in v2:
time: 553 us; the launch traced here: 549 us
  waiting for transfers between devices  262 us (47%)
  Pallas kernels  89.9 us (16%)
  starting transfers between devices  76.3 us (14%)
  local copies, waits for them, and re-layouts  40 us (7%)
  matrix products  39.2 us (7%)
  other arithmetic  25.9 us (5%)
  between operations  15.6 us (3%)
    ppermute x62, waiting for transfers between devices, flip(): return lax.ppermute(values, 'seq', [(i, i ^ bit) for i in range(self.ns)])  133 us
    all_gather x4, waiting for transfers between devices, line_gather(): return lax.all_gather(own, 'fsdp', axis=0, tiled=True)  80.3 us
    ppermute x62, starting transfers between devices, flip(): return lax.ppermute(values, 'seq', [(i, i ^ bit) for i in range(self.ns)])  49.5 us
    reduce_scatter x4, waiting for transfers between devices, line_reduce(): return lax.psum_scatter(terms, 'fsdp', scatter_dimension=0, tiled=True)  33.8 us
    pallas_call x1, Pallas kernels, attend_back(): pl.pallas_call(kernel, out_shape=[jax.ShapeDtypeStruct((length, width), B...  26 us
    dot_general x3, matrix products, dot_tn(): lax.dot_general(a, b, (((0,), (0,)), ((), ())), preferred_element_type=F4)  20 us
    pallas_call x1, Pallas kernels, attend(): pl.pallas_call(kernel, out_shape=[jax.ShapeDtypeStruct((length, width), B...  19.9 us
    pallas_call x1, Pallas kernels, feed_back(): pl.pallas_call(kernel, out_shape=[jax.ShapeDtypeStruct((length, both), BF...  19.1 us
  transfers between devices with their start and end apart: 80, of which 41 were waited for; matrix products, arithmetic and copies ran while one was open for 17% of the time, Pallas kernels for 16%

profile of v2, /device:TPU:0, one launch (start us, length us, event | category | flops | bytes accessed | tf_op | source)
XLA Modules:
  0.0 548.5 jit_solution(8457185586598018004)
XLA Ops:
  13.6 5.2 all-to-all-start
  20.5 2.6 collective-permute-start.10
  25.0 3.5 collective-permute-done.11
  31.4 10.7 %all-gather.7.cloned.1.call-done.refs_2_.refs_10_ = bf16[256,2048]{1,0:T(8,128)(2,1)} async-done(((bf16[64,2048]{1,0:T(8,128)(2,1)}), bf16[256,2048]{1,0:T(8,128)(2,1)}) %all-gather.7.cloned.1.call-update) | async-done | bytes 1048592 | tf_op jit(solution)/shard_map/all_gather | solution.py:619
  46.6 3.6 all-to-all-start.1
  52.2 4.8 collective-permute-done.refs_1_
  60.1 3.2 collective-permute-start.3
  63.3 9.5 %collective-permute-done.13 = bf16[8,448]{1,0:T(8,128)(2,1)S(1)} collective-permute-done((bf16[8,448]{1,0:T(8,128)(2,1)S(1)}, bf16[8,448]{1,0:T(8,128)(2,1)S(1)}, u32[]{:S(2)}, u32[]{:S(2)}) %collective-permute-start.13) | collective-permute-done | bytes 7200 | tf_op jit(solution)/shard_map/ppermute | solution.py:553
  75.6 2.5 collective-permute-done.2.refs_3_
  84.2 23.0 %all-gather.11.cloned.1.call-done = bf16[32,64,768]{2,1,0:T(8,128)(2,1)} async-done(((bf16[8,64,768]{2,1,0:T(8,128)(2,1)}), bf16[32,64,768]{2,1,0:T(8,128)(2,1)}) %all-gather.11.cloned.1.call-update) | async-done | bytes 3145744 | tf_op jit(solution)/shard_map/all_gather | solution.py:619
  113.3 19.9 %attend.1 = (bf16[1024,2048]{1,0:T(8,128)(2,1)}, bf16[1024,256]{1,0:T(8,128)(2,1)}, bf16[1024,256]{1,0:T(8,128)(2,1)}, bf16[1024,256]{1,0:T(8,128)(2,1)}, bf16[1...) custom-call(s32[2]{0:T(128)} %pad_add_fusion.place_ref, ...), custom_call_target="tpu_custom_call" | custom-call | flops 16999999488 | tf_op jit(solution)/shard_map/attend/pallas_call | solution.py:191
  135.0 4.1 collective-permute-done.15
  142.9 5.5 %collective-permute-done.16 = bf16[64,2048]{1,0:T(8,128)(2,1)S(1)} collective-permute-done((bf16[64,2048]{1,0:T(8,128)(2,1)S(1)}, bf16[64,2048]{1,0:T(8,128)(2,1)S(1)}, u32[]{:S(2)}, u32[]{:S(2)}) %collective-permute-start.16) | collective-permute-done | bytes 262176 | tf_op jit(solution)/shard_map/ppermute | solution.py:553
  154.3 10.4 %collective-permute-done.17 = bf16[128,2048]{1,0:T(8,128)(2,1)S(1)} collective-permute-done((bf16[128,2048]{1,0:T(8,128)(2,1)S(1)}, bf16[128,2048]{1,0:T(8,128)(2,1)S(1)}, u32[]{:S(2)}, u32[]{:S(2)}) %collective-permute-start.17) | collective-permute-done | bytes 524320 | tf_op jit(solution)/shard_map/ppermute | solution.py:553
  168.2 46.6 %all-gather.13.cloned.1.call-done = bf16[32,64,1408]{2,1,0:T(8,128)(2,1)} async-done(((bf16[8,64,1408]{2,1,0:T(8,128)(2,1)}), bf16[32,64,1408]{2,1,0:T(8,128)(2,1)}) %all-gather.13.cloned.1.call-update) | async-done | bytes 5767184 | tf_op jit(solution)/shard_map/all_gather | solution.py:619
  221.8 15.6 %collective-permute-done.31.refs_13_ = bf16[64,2048]{1,0:T(8,128)(2,1)S(1)} collective-permute-done((bf16[64,2048]{1,0:T(8,128)(2,1)S(1)}, bf16[64,2048]{1,0:T(8,128)(2,1)S(1)}, u32[]{:S(2)}, u32[]{:S(2)}) %collective-permute-start.31) | collective-permute-done | bytes 262176 | tf_op jit(solution)/shard_map/ppermute | solution.py:553
  242.6 5.8 %collective-permute-done.22.refs_3_ = bf16[64,2048]{1,0:T(8,128)(2,1)S(1)} collective-permute-done((bf16[64,2048]{1,0:T(8,128)(2,1)S(1)}, bf16[64,2048]{1,0:T(8,128)(2,1)S(1)}, u32[]{:S(2)}, u32[]{:S(2)}) %collective-permute-start.22) | collective-permute-done | bytes 262176 | tf_op jit(solution)/shard_map/ppermute | solution.py:553
  252.9 15.5 %feed.1 = (bf16[1024,2048]{1,0:T(8,128)(2,1)}, bf16[1024,2048]{1,0:T(8,128)(2,1)}, bf16[1024,704]{1,0:T(8,128)(2,1)}, f32[1024,1408]{1,0:T(8,128)}) custom-call(bf16[128,2048]{1,0:T(8,128)(2,1)} %copy-done.22, bf16[128,2048]{1,0:T(8,128)(2,1)} %copy-done.28, bf16[128,2048]{1,0:T(8,128)(2,1)} %copy-done.29, bf16[64,2048]{1,0:T(8,128)(2,1)} %copy-done.57, ...), custom_call_target="tpu_custom_call" | custom-call | flops 16999999488 | tf_op jit(solution)/shard_map/feed/pallas_call | solution.py:401
  268.4 7.4 %convolution_convert_fusion.2.refs_2_ = bf16[704,2048]{1,0:T(8,128)(2,1)} fusion(bf16[1024,704]{1,0:T(8,128)(2,1)} %get-tuple-element.105.refs_0_, bf16[1024,2048]{1,0:T(8,128)(2,1)} %get-tuple-element.106.refs_0_), kind=kOutput, calls=%fused_computation.7 | convolution fusion | flops 2954231808 | bytes 8519680 | tf_op jit(solution)/shard_map/dot_general | solution.py:27
  276.1 19.1 %feed_back.1 = (bf16[1024,1408]{1,0:T(8,128)(2,1)}, bf16[512,2048]{1,0:T(8,128)(2,1)}, f32[512,2048]{1,0:T(8,128)}) custom-call(bf16[1024,2048]{1,0:T(8,128)(2,1)} %get-tuple-element.108.g_ref, f32[1024,1408]{1,0:T(8,128)} %get-tuple-element.109.both_ref, bf16[4,8,64,1408]{3,2,1,0:T(8,128)(2,1)} %bitcast.82, ...), custom_call_target="tpu_custom_call" | custom-call | flops 16999999488 | tf_op jit(solution)/shard_map/feed_back/pallas_call | solution.py:458
  295.3 8.8 %convolution_convert_fusion = bf16[2048,1408]{1,0:T(8,128)(2,1)S(1)} fusion(bf16[1024,2048]{1,0:T(8,128)(2,1)S(1)} %copy-done.63, bf16[1024,1408]{1,0:T(8,128)(2,1)} %get-tuple-element.114), kind=kOutput, calls=%fused_computation | convolution fusion | flops 5908463616 | bytes 12845056 | tf_op jit(solution)/shard_map/dot_general | solution.py:27
  304.1 2.9 copy.121
  307.0 23.7 %reduce-scatter.5.cloned.1.call-done.refs_1_ = bf16[176,2048]{1,0:T(8,128)(2,1)} async-done(((bf16[704,2048]{1,0:T(8,128)(2,1)}), bf16[176,2048]{1,0:T(8,128)(2,1)}) %reduce-scatter.5.cloned.1.call-update) | async-done | bytes 720912 | tf_op jit(solution)/shard_map/reduce_scatter | solution.py:622
  330.8 3.7 fusion.41
  337.6 5.0 collective-permute-done.39
  346.2 10.3 %collective-permute-done.40 = bf16[128,2048]{1,0:T(8,128)(2,1)S(1)} collective-permute-done((bf16[128,2048]{1,0:T(8,128)(2,1)S(1)}, bf16[128,2048]{1,0:T(8,128)(2,1)S(1)}, u32[]{:S(2)}, u32[]{:S(2)}) %collective-permute-start.40) | collective-permute-done | bytes 524320 | tf_op jit(solution)/shard_map/ppermute | solution.py:553
  360.7 2.9 fusion.40
  364.7 10.6 %collective-permute-done.43.refs_1_ = bf16[128,2048]{1,0:T(8,128)(2,1)S(1)} collective-permute-done((bf16[128,2048]{1,0:T(8,128)(2,1)S(1)}, bf16[128,2048]{1,0:T(8,128)(2,1)S(1)}, u32[]{:S(2)}, u32[]{:S(2)}) %collective-permute-start.43) | collective-permute-done | bytes 524320 | tf_op jit(solution)/shard_map/ppermute | solution.py:553
  379.0 2.8 collective-permute-done.45.refs_3_
  385.8 26.0 %attend_back.1 = (bf16[1024,2048]{1,0:T(8,128)(2,1)}, bf16[1024,768]{1,0:T(8,128)(2,1)}, bf16[1024,768]{1,0:T(8,128)(2,1)}, f32[1,768]{1,0:T(1,128)}) custom-call(s32[2]{0:T(128)} %pad_add_fusion.place_ref, bf16[128,2048]{1,0:T(8,128)(2,1)} %copy-done.23, bf16[128,2048]{1,0:T(8,128)(2,1)} %copy-done.26, bf16[128,2048]{1,0:T(8,128)(2,1)} %copy-done.27, ...), custom_call_target="tpu_custom_call" | custom-call | flops 25999998976 | tf_op jit(solution)/shard_map/attend_back/pallas_call | solution.py:312
  411.9 4.3 convolution_convert_fusion.4.refs_1_
  416.4 5.4 convolution_convert_fusion.5
  422.2 3.7 convolution_convert_fusion.1
  428.0 7.1 %reduce-scatter.7.cloned.1.call-done = bf16[1,8,64,1408]{3,2,1,0:T(8,128)(2,1)} async-done(((bf16[4,8,64,1408]{3,2,1,0:T(8,128)(2,1)}), bf16[1,8,64,1408]{3,2,1,0:T(8,128)(2,1)}) %reduce-scatter.7.cloned.1.call-update) | async-done | bytes 1441808 | tf_op jit(solution)/shard_map/reduce_scatter | solution.py:622
  439.7 6.0 %outer_rows.1.refs_0_ = bf16[256,2048]{1,0:T(8,128)(2,1)} custom-call(bf16[1024,256]{1,0:T(8,128)(2,1)} %get-tuple-element.102.left_ref, bf16[128,2048]{1,0:T(8,128)(2,1)} %copy-done.23, bf16[128,2048]{1,0:T(8,128)(2,1)} %copy-done.26, bf16[128,2048]{1,0:T(8,128)(2,1)} %copy-done.27, bf16[64,2048]{1,0:T(8,128)(2,1)} %copy-done.49, ...), custom_call_target="tpu_custom_call" | custom-call | flops 4000000000 | tf_op jit(solution)/shard_map/outer_rows/pallas_call | solution.py:352
  445.8 3.6 fusion.50
  452.5 3.4 fusion.49
  462.0 3.3 collective-permute-done.53
  469.7 7.4 %collective-permute-done.59 = bf16[128,2048]{1,0:T(8,128)(2,1)S(1)} collective-permute-done((bf16[128,2048]{1,0:T(8,128)(2,1)S(1)}, bf16[128,2048]{1,0:T(8,128)(2,1)S(1)}, u32[]{:S(2)}, u32[]{:S(2)}) %collective-permute-start.59) | collective-permute-done | bytes 524320 | tf_op jit(solution)/shard_map/ppermute | solution.py:553
  480.8 6.1 %collective-permute-done.54 = bf16[128,2048]{1,0:T(8,128)(2,1)S(1)} collective-permute-done((bf16[128,2048]{1,0:T(8,128)(2,1)}, bf16[128,2048]{1,0:T(8,128)(2,1)S(1)}, u32[]{:S(2)}, u32[]{:S(2)}) %collective-permute-start.54) | collective-permute-done | bytes 524320 | tf_op jit(solution)/shard_map/ppermute | solution.py:553
  486.9 2.4 fusion.22
  489.4 3.7 all-to-all-start.3
  495.1 3.0 reduce-scatter.9.cloned.1.call-done.refs_1_
  498.2 13.9 %collective-permute-done.63 = f32[8,448]{1,0:T(8,128)S(1)} collective-permute-done((f32[8,448]{1,0:T(8,128)S(1)}, f32[8,448]{1,0:T(8,128)S(1)}, u32[]{:S(2)}, u32[]{:S(2)}) %collective-permute-start.63) | collective-permute-done | bytes 14368 | tf_op jit(solution)/shard_map/ppermute | solution.py:553
  517.8 4.2 all-to-all-start.2
  522.0 2.5 fusion.23
  527.6 7.1 %all-to-all-done.2 = bf16[8,64,768]{2,1,0:T(8,128)(2,1)} async-done(((bf16[8,64,768]{2,1,0:T(8,128)(2,1)}), bf16[8,64,768]{2,1,0:T(8,128)(2,1)}, u32[]{:S(2)}, u32[]{:S(2)}) %all-to-all-start.2) | async-done | bytes 786464 | tf_op jit(solution)/shard_map/all_to_all | solution.py:625
  534.6 2.5 reshape.240
  (396 shorter events, 127.9 us)
Async XLA Ops:
  7.2 34.9 %all-gather.7.cloned.1.call-start = ((), (), s32[]{:S(2)}) async-start(), calls=%async_computation.8 | async-start | bytes 1310720 | tf_op jit(solution)/shard_map/all_gather | solution.py:619
  13.6 17.8 %all-to-all-start = ((bf16[8,64,768]{2,1,0:T(8,128)(2,1)}), bf16[8,64,768]{2,1,0:T(8,128)(2,1)S(1)}, u32[]{:S(2)}, u32[]{:S(2)}) async-start(bf16[8,64,768]{2,1,0:T(8,128)(2,1)} %reshape.215), calls=%async_computation | async-start | bytes 1572864 | tf_op jit(solution)/shard_map/all_to_all | solution.py:625
  18.8 88.4 %all-gather.11.cloned.1.call-start = ((), (), s32[]{:S(2)}) async-start(), calls=%async_computation.14 | async-start | bytes 3932160 | tf_op jit(solution)/shard_map/all_gather | solution.py:619
  42.1 14.9 %collective-permute-start = (bf16[128,2048]{1,0:T(8,128)(2,1)S(1)}, bf16[128,2048]{1,0:T(8,128)(2,1)S(1)}, u32[]{:S(2)}, u32[]{:S(2)}) collective-permute-start(bf16[128,2048]{1,0:T(8,128)(2,1)S(1)} %bitcast.70), channel_id=1, source_target_pairs={{0,8},{4,12},{8,0},{12,4},{16,24},{20,28},{24,16},{28,20},{1,9},{5... | collective-permute-start | bytes 1572872 | tf_op jit(solution)/shard_map/ppermute | solution.py:553
  43.7 15.6 %collective-permute-start.1 = (bf16[128,2048]{1,0:T(8,128)(2,1)S(1)}, bf16[128,2048]{1,0:T(8,128)(2,1)S(1)}, u32[]{:S(2)}, u32[]{:S(2)}) collective-permute-start(bf16[128,2048]{1,0:T(8,128)(2,1)S(1)} %bitcast.71), channel_id=1, source_target_pairs={{0,16},{4,20},{8,24},{12,28},{16,0},{20,4},{24,8},{28,12},{1,17},{... | collective-permute-start | bytes 1572872 | tf_op jit(solution)/shard_map/ppermute | solution.py:553
  46.6 36.5 %all-to-all-start.1 = ((bf16[8,64,1408]{2,1,0:T(8,128)(2,1)}), bf16[8,64,1408]{2,1,0:T(8,128)(2,1)S(1)}, u32[]{:S(2)}, u32[]{:S(2)}) async-start(bf16[8,64,1408]{2,1,0:T(8,128)(2,1)} %pair_columns.1), calls=%async_computation.1 | async-start | bytes 2883584 | tf_op jit(solution)/shard_map/all_to_all | solution.py:625
  50.2 164.6 %all-gather.13.cloned.1.call-start = ((), (), s32[]{:S(2)}) async-start(), calls=%async_computation.15 | async-start | bytes 7208960 | tf_op jit(solution)/shard_map/all_gather | solution.py:619
  50.3 22.5 %collective-permute-start.13 = (bf16[8,448]{1,0:T(8,128)(2,1)S(1)}, bf16[8,448]{1,0:T(8,128)(2,1)S(1)}, u32[]{:S(2)}, u32[]{:S(2)}) collective-permute-start(bf16[8,448]{1,0:T(8,128)(2,1)S(1)} %pad_maximum_fusion.10), channel_id=1, source_target_pairs={{0,8},{4,12},{8,0},{12,4},{16,24},{20,28},{24,16},{28,20},{1,9},{5... | collective-permute-start | bytes 21512 | tf_op jit(solution)/shard_map/ppermute | solution.py:553
  57.8 20.4 %collective-permute-start.2 = (bf16[64,2048]{1,0:T(8,128)(2,1)}, bf16[64,2048]{1,0:T(8,128)(2,1)S(1)}, u32[]{:S(2)}, u32[]{:S(2)}) collective-permute-start(bf16[64,2048]{1,0:T(8,128)(2,1)} %slice.286), channel_id=1, source_target_pairs={{0,16},{4,20},{8,24},{12,28},{16,0},{20,4},{24,8},{28,12},{1,17},{... | collective-permute-start | bytes 786440 | tf_op jit(solution)/shard_map/ppermute | solution.py:553
  60.1 18.1 %collective-permute-start.3 = (bf16[64,2048]{1,0:T(8,128)(2,1)}, bf16[64,2048]{1,0:T(8,128)(2,1)}, u32[]{:S(2)}, u32[]{:S(2)}) collective-permute-start(bf16[64,2048]{1,0:T(8,128)(2,1)} %slice.287), channel_id=1, source_target_pairs={{0,8},{4,12},{8,0},{12,4},{16,24},{20,28},{24,16},{28,20},{1,9},{5... | collective-permute-start | bytes 786440 | tf_op jit(solution)/shard_map/ppermute | solution.py:553
  74.3 8.7 %collective-permute-start.4 = (bf16[128,2048]{1,0:T(8,128)(2,1)S(1)}, bf16[128,2048]{1,0:T(8,128)(2,1)}, u32[]{:S(2)}, u32[]{:S(2)}) collective-permute-start(bf16[128,2048]{1,0:T(8,128)(2,1)S(1)} %bitcast.72), channel_id=1, source_target_pairs={{0,4},{4,0},{8,12},{12,8},{16,20},{20,16},{24,28},{28,24},{1,5},{5... | collective-permute-start | bytes 1572872 | tf_op jit(solution)/shard_map/ppermute | solution.py:553
  107.2 168.9 %all-gather.9.cloned.1.call-start = ((), (), s32[]{:S(2)}) async-start(), calls=%async_computation.9 | async-start | bytes 3604480 | tf_op jit(solution)/shard_map/all_gather | solution.py:619
  149.7 14.9 %collective-permute-start.17 = (bf16[128,2048]{1,0:T(8,128)(2,1)S(1)}, bf16[128,2048]{1,0:T(8,128)(2,1)S(1)}, u32[]{:S(2)}, u32[]{:S(2)}) collective-permute-start(bf16[128,2048]{1,0:T(8,128)(2,1)S(1)} %pad_maximum_fusion), channel_id=1, source_target_pairs={{0,8},{4,12},{8,0},{12,4},{16,24},{20,28},{24,16},{28,20},{1,9},{5... | collective-permute-start | bytes 1572872 | tf_op jit(solution)/shard_map/ppermute | solution.py:553
  151.3 14.9 %collective-permute-start.19 = (bf16[128,2048]{1,0:T(8,128)(2,1)S(1)}, bf16[128,2048]{1,0:T(8,128)(2,1)S(1)}, u32[]{:S(2)}, u32[]{:S(2)}) collective-permute-start(bf16[128,2048]{1,0:T(8,128)(2,1)S(1)} %pad_maximum_fusion.1), channel_id=1, source_target_pairs={{0,16},{4,20},{8,24},{12,28},{16,0},{20,4},{24,8},{28,12},{1,17},{... | collective-permute-start | bytes 1572872 | tf_op jit(solution)/shard_map/ppermute | solution.py:553
  152.2 64.9 %collective-permute-start.29 = (bf16[128,2048]{1,0:T(8,128)(2,1)S(1)}, bf16[128,2048]{1,0:T(8,128)(2,1)}, u32[]{:S(2)}, u32[]{:S(2)}) collective-permute-start(bf16[128,2048]{1,0:T(8,128)(2,1)S(1)} %copy-done.8), channel_id=1, source_target_pairs={{0,8},{4,12},{8,0},{12,4},{16,24},{20,28},{24,16},{28,20},{1,9},{5... | collective-permute-start | bytes 1572872 | tf_op jit(solution)/shard_map/ppermute | solution.py:553
  152.9 67.3 %collective-permute-start.30 = (bf16[128,2048]{1,0:T(8,128)(2,1)S(1)}, bf16[128,2048]{1,0:T(8,128)(2,1)}, u32[]{:S(2)}, u32[]{:S(2)}) collective-permute-start(bf16[128,2048]{1,0:T(8,128)(2,1)S(1)} %copy-done.8), channel_id=1, source_target_pairs={{0,16},{4,20},{8,24},{12,28},{16,0},{20,4},{24,8},{28,12},{1,17},{... | collective-permute-start | bytes 1572872 | tf_op jit(solution)/shard_map/ppermute | solution.py:553
  214.8 116.0 %reduce-scatter.5.cloned.1.call-start = ((), (), s32[]{:S(2)}) async-start(), calls=%async_computation.10 | async-start | bytes 3604480 | tf_op jit(solution)/shard_map/reduce_scatter | solution.py:622
  215.6 22.3 %collective-permute-start.20 = (bf16[128,2048]{1,0:T(8,128)(2,1)S(1)}, bf16[128,2048]{1,0:T(8,128)(2,1)S(1)}, u32[]{:S(2)}, u32[]{:S(2)}) collective-permute-start(bf16[128,2048]{1,0:T(8,128)(2,1)S(1)} %add_convert_fusion.refs_0_), channel_id=1, source_target_pairs={{0,8},{4,12},{8,0},{12,4},{16,24},{20,28},{24,16},{28,20},{1,9},{5... | collective-permute-start | bytes 1572872 | tf_op jit(solution)/shard_map/ppermute | solution.py:553
  218.1 19.9 %collective-permute-start.21 = (bf16[128,2048]{1,0:T(8,128)(2,1)S(1)}, bf16[128,2048]{1,0:T(8,128)(2,1)S(1)}, u32[]{:S(2)}, u32[]{:S(2)}) collective-permute-start(bf16[128,2048]{1,0:T(8,128)(2,1)S(1)} %add_convert_fusion.refs_0_), channel_id=1, source_target_pairs={{0,16},{4,20},{8,24},{12,28},{16,0},{20,4},{24,8},{28,12},{1,17},{... | collective-permute-start | bytes 1572872 | tf_op jit(solution)/shard_map/ppermute | solution.py:553
  219.7 17.7 %collective-permute-start.31 = (bf16[64,2048]{1,0:T(8,128)(2,1)S(1)}, bf16[64,2048]{1,0:T(8,128)(2,1)S(1)}, u32[]{:S(2)}, u32[]{:S(2)}) collective-permute-start(bf16[64,2048]{1,0:T(8,128)(2,1)S(1)} %slice.297), channel_id=1, source_target_pairs={{0,16},{4,20},{8,24},{12,28},{16,0},{20,4},{24,8},{28,12},{1,17},{... | collective-permute-start | bytes 786440 | tf_op jit(solution)/shard_map/ppermute | solution.py:553
  221.2 16.2 %collective-permute-start.32 = (bf16[64,2048]{1,0:T(8,128)(2,1)S(1)}, bf16[64,2048]{1,0:T(8,128)(2,1)S(1)}, u32[]{:S(2)}, u32[]{:S(2)}) collective-permute-start(bf16[64,2048]{1,0:T(8,128)(2,1)S(1)} %slice.298), channel_id=1, source_target_pairs={{0,8},{4,12},{8,0},{12,4},{16,24},{20,28},{24,16},{28,20},{1,9},{5... | collective-permute-start | bytes 786440 | tf_op jit(solution)/shard_map/ppermute | solution.py:553
  221.8 16.7 %collective-permute-start.33 = (bf16[128,2048]{1,0:T(8,128)(2,1)S(1)}, bf16[128,2048]{1,0:T(8,128)(2,1)S(1)}, u32[]{:S(2)}, u32[]{:S(2)}) collective-permute-start(bf16[128,2048]{1,0:T(8,128)(2,1)S(1)} %copy-done.8), channel_id=1, source_target_pairs={{0,4},{4,0},{8,12},{12,8},{16,20},{20,16},{24,28},{28,24},{1,5},{5... | collective-permute-start | bytes 1572872 | tf_op jit(solution)/shard_map/ppermute | solution.py:553
  238.5 11.1 %collective-permute-start.24 = (bf16[128,2048]{1,0:T(8,128)(2,1)S(1)}, bf16[128,2048]{1,0:T(8,128)(2,1)S(1)}, u32[]{:S(2)}, u32[]{:S(2)}) collective-permute-start(bf16[128,2048]{1,0:T(8,128)(2,1)S(1)} %add_convert_fusion.refs_0_), channel_id=1, source_target_pairs={{0,4},{4,0},{8,12},{12,8},{16,20},{20,16},{24,28},{28,24},{1,5},{5... | collective-permute-start | bytes 1572872 | tf_op jit(solution)/shard_map/ppermute | solution.py:553
  242.1 9.0 %collective-permute-start.25 = (bf16[128,2048]{1,0:T(8,128)(2,1)S(1)}, bf16[128,2048]{1,0:T(8,128)(2,1)S(1)}, u32[]{:S(2)}, u32[]{:S(2)}) collective-permute-start(bf16[128,2048]{1,0:T(8,128)(2,1)S(1)} %collective-permute-done.20.refs_1_), channel_id=1, source_target_pairs={{0,4},{4,0},{8,12},{12,8},{16,20},{20,16},{24,28},{28,24},{1,5},{5... | collective-permute-start | bytes 1572872 | tf_op jit(solution)/shard_map/ppermute | solution.py:553
  242.2 9.1 %collective-permute-start.26 = (bf16[128,2048]{1,0:T(8,128)(2,1)S(1)}, bf16[128,2048]{1,0:T(8,128)(2,1)S(1)}, u32[]{:S(2)}, u32[]{:S(2)}) collective-permute-start(bf16[128,2048]{1,0:T(8,128)(2,1)S(1)} %collective-permute-done.21.refs_2_), channel_id=1, source_target_pairs={{0,4},{4,0},{8,12},{12,8},{16,20},{20,16},{24,28},{28,24},{1,5},{5... | collective-permute-start | bytes 1572872 | tf_op jit(solution)/shard_map/ppermute | solution.py:553
  275.9 159.2 %reduce-scatter.7.cloned.1.call-start = ((), (), s32[]{:S(2)}) async-start(), calls=%async_computation.11 | async-start | bytes 7208960 | tf_op jit(solution)/shard_map/reduce_scatter | solution.py:622
  307.0 23.8 %collective-permute-start.38 = (bf16[512,2048]{1,0:T(8,128)(2,1)}, bf16[512,2048]{1,0:T(8,128)(2,1)}, u32[]{:S(2)}, u32[]{:S(2)}) collective-permute-start(bf16[512,2048]{1,0:T(8,128)(2,1)} %get-tuple-element.116), channel_id=1, source_target_pairs={{0,4},{4,0},{8,12},{12,8},{16,20},{20,16},{24,28},{28,24},{1,5},{5... | collective-permute-start | bytes 6291464 | tf_op jit(solution)/shard_map/ppermute | solution.py:553
  330.8 167.4 %reduce-scatter.9.cloned.1.call-start = ((), (), s32[]{:S(2)}) async-start(), calls=%async_computation.12 | async-start | bytes 3932160 | tf_op jit(solution)/shard_map/reduce_scatter | solution.py:622
  344.0 12.5 %collective-permute-start.40 = (bf16[128,2048]{1,0:T(8,128)(2,1)S(1)}, bf16[128,2048]{1,0:T(8,128)(2,1)S(1)}, u32[]{:S(2)}, u32[]{:S(2)}) collective-permute-start(bf16[128,2048]{1,0:T(8,128)(2,1)S(1)} %pad_maximum_fusion.2), channel_id=1, source_target_pairs={{0,8},{4,12},{8,0},{12,4},{16,24},{20,28},{24,16},{28,20},{1,9},{5... | collective-permute-start | bytes 1572872 | tf_op jit(solution)/shard_map/ppermute | solution.py:553
  345.5 12.2 %collective-permute-start.42 = (bf16[128,2048]{1,0:T(8,128)(2,1)S(1)}, bf16[128,2048]{1,0:T(8,128)(2,1)S(1)}, u32[]{:S(2)}, u32[]{:S(2)}) collective-permute-start(bf16[128,2048]{1,0:T(8,128)(2,1)S(1)} %pad_maximum_fusion.3), channel_id=1, source_target_pairs={{0,16},{4,20},{8,24},{12,28},{16,0},{20,4},{24,8},{28,12},{1,17},{... | collective-permute-start | bytes 1572872 | tf_op jit(solution)/shard_map/ppermute | solution.py:553
  363.6 11.7 %collective-permute-start.43 = (bf16[128,2048]{1,0:T(8,128)(2,1)S(1)}, bf16[128,2048]{1,0:T(8,128)(2,1)S(1)}, u32[]{:S(2)}, u32[]{:S(2)}) collective-permute-start(bf16[128,2048]{1,0:T(8,128)(2,1)S(1)} %get-tuple-element.137.refs_0_), channel_id=1, source_target_pairs={{0,8},{4,12},{8,0},{12,4},{16,24},{20,28},{24,16},{28,20},{1,9},{5... | collective-permute-start | bytes 1572872 | tf_op jit(solution)/shard_map/ppermute | solution.py:553
  364.2 11.9 %collective-permute-start.44 = (bf16[128,2048]{1,0:T(8,128)(2,1)S(1)}, bf16[128,2048]{1,0:T(8,128)(2,1)S(1)}, u32[]{:S(2)}, u32[]{:S(2)}) collective-permute-start(bf16[128,2048]{1,0:T(8,128)(2,1)S(1)} %get-tuple-element.137.refs_0_), channel_id=1, source_target_pairs={{0,16},{4,20},{8,24},{12,28},{16,0},{20,4},{24,8},{28,12},{1,17},{... | collective-permute-start | bytes 1572872 | tf_op jit(solution)/shard_map/ppermute | solution.py:553
  364.7 18.9 %collective-permute-start.47 = (bf16[128,2048]{1,0:T(8,128)(2,1)S(1)}, bf16[128,2048]{1,0:T(8,128)(2,1)S(1)}, u32[]{:S(2)}, u32[]{:S(2)}) collective-permute-start(bf16[128,2048]{1,0:T(8,128)(2,1)S(1)} %get-tuple-element.137.refs_0_), channel_id=1, source_target_pairs={{0,4},{4,0},{8,12},{12,8},{16,20},{20,16},{24,28},{28,24},{1,5},{5... | collective-permute-start | bytes 1572872 | tf_op jit(solution)/shard_map/ppermute | solution.py:553
  416.2 29.5 %collective-permute-start.57 = (bf16[512,2048]{1,0:T(8,128)(2,1)}, bf16[512,2048]{1,0:T(8,128)(2,1)}, u32[]{:S(2)}, u32[]{:S(2)}) collective-permute-start(bf16[512,2048]{1,0:T(8,128)(2,1)} %convolution_convert_fusion.4.refs_1_), channel_id=1, source_target_pairs={{0,4},{4,0},{8,12},{12,8},{16,20},{20,16},{24,28},{28,24},{1,5},{5... | collective-permute-start | bytes 6291464 | tf_op jit(solution)/shard_map/ppermute | solution.py:553
  421.8 30.6 %collective-permute-start.52 = (bf16[512,2048]{1,0:T(8,128)(2,1)}, bf16[512,2048]{1,0:T(8,128)(2,1)}, u32[]{:S(2)}, u32[]{:S(2)}) collective-permute-start(bf16[512,2048]{1,0:T(8,128)(2,1)} %convolution_convert_fusion.5), channel_id=1, source_target_pairs={{0,4},{4,0},{8,12},{12,8},{16,20},{20,16},{24,28},{28,24},{1,5},{5... | collective-permute-start | bytes 6291464 | tf_op jit(solution)/shard_map/ppermute | solution.py:553
  456.0 9.3 %collective-permute-start.53 = (bf16[64,2048]{1,0:T(8,128)(2,1)S(1)}, bf16[64,2048]{1,0:T(8,128)(2,1)S(1)}, u32[]{:S(2)}, u32[]{:S(2)}) collective-permute-start(bf16[64,2048]{1,0:T(8,128)(2,1)S(1)} %get-tuple-element.158), channel_id=1, source_target_pairs={{0,16},{4,20},{8,24},{12,28},{16,0},{20,4},{24,8},{28,12},{1,17},{... | collective-permute-start | bytes 786440 | tf_op jit(solution)/shard_map/ppermute | solution.py:553
  456.7 9.2 %collective-permute-start.55 = (bf16[64,2048]{1,0:T(8,128)(2,1)S(1)}, bf16[64,2048]{1,0:T(8,128)(2,1)S(1)}, u32[]{:S(2)}, u32[]{:S(2)}) collective-permute-start(bf16[64,2048]{1,0:T(8,128)(2,1)S(1)} %get-tuple-element.157), channel_id=1, source_target_pairs={{0,8},{4,12},{8,0},{12,4},{16,24},{20,28},{24,16},{28,20},{1,9},{5... | collective-permute-start | bytes 786440 | tf_op jit(solution)/shard_map/ppermute | solution.py:553
  459.4 17.7 %collective-permute-start.59 = (bf16[128,2048]{1,0:T(8,128)(2,1)S(1)}, bf16[128,2048]{1,0:T(8,128)(2,1)S(1)}, u32[]{:S(2)}, u32[]{:S(2)}) collective-permute-start(bf16[128,2048]{1,0:T(8,128)(2,1)S(1)} %pad_maximum_fusion.6), channel_id=1, source_target_pairs={{0,8},{4,12},{8,0},{12,4},{16,24},{20,28},{24,16},{28,20},{1,9},{5... | collective-permute-start | bytes 1572872 | tf_op jit(solution)/shard_map/ppermute | solution.py:553
  461.9 15.2 %collective-permute-start.61 = (bf16[128,2048]{1,0:T(8,128)(2,1)S(1)}, bf16[128,2048]{1,0:T(8,128)(2,1)S(1)}, u32[]{:S(2)}, u32[]{:S(2)}) collective-permute-start(bf16[128,2048]{1,0:T(8,128)(2,1)S(1)} %pad_maximum_fusion.7), channel_id=1, source_target_pairs={{0,16},{4,20},{8,24},{12,28},{16,0},{20,4},{24,8},{28,12},{1,17},{... | collective-permute-start | bytes 1572872 | tf_op jit(solution)/shard_map/ppermute | solution.py:553
  466.8 20.1 %collective-permute-start.54 = (bf16[128,2048]{1,0:T(8,128)(2,1)}, bf16[128,2048]{1,0:T(8,128)(2,1)S(1)}, u32[]{:S(2)}, u32[]{:S(2)}) collective-permute-start(bf16[128,2048]{1,0:T(8,128)(2,1)} %pad_maximum_fusion.4), channel_id=1, source_target_pairs={{0,8},{4,12},{8,0},{12,4},{16,24},{20,28},{24,16},{28,20},{1,9},{5... | collective-permute-start | bytes 1572872 | tf_op jit(solution)/shard_map/ppermute | solution.py:553
  469.0 17.9 %collective-permute-start.56 = (bf16[128,2048]{1,0:T(8,128)(2,1)}, bf16[128,2048]{1,0:T(8,128)(2,1)}, u32[]{:S(2)}, u32[]{:S(2)}) collective-permute-start(bf16[128,2048]{1,0:T(8,128)(2,1)} %pad_maximum_fusion.5), channel_id=1, source_target_pairs={{0,16},{4,20},{8,24},{12,28},{16,0},{20,4},{24,8},{28,12},{1,17},{... | collective-permute-start | bytes 1572872 | tf_op jit(solution)/shard_map/ppermute | solution.py:553
  479.3 10.0 %collective-permute-start.62 = (f32[16,448]{1,0:T(8,128)S(1)}, f32[16,448]{1,0:T(8,128)S(1)}, u32[]{:S(2)}, u32[]{:S(2)}) collective-permute-start(f32[16,448]{1,0:T(8,128)S(1)} %slice_select_fusion), channel_id=1, source_target_pairs={{0,16},{4,20},{8,24},{12,28},{16,0},{20,4},{24,8},{28,12},{1,17},{... | collective-permute-start | bytes 86024 | tf_op jit(solution)/shard_map/ppermute | solution.py:553
  489.4 28.4 %all-to-all-start.3 = ((bf16[8,64,1408]{2,1,0:T(8,128)(2,1)}), bf16[8,64,1408]{2,1,0:T(8,128)(2,1)S(1)}, u32[]{:S(2)}, u32[]{:S(2)}) async-start(bf16[8,64,1408]{2,1,0:T(8,128)(2,1)} %bitcast.25.refs_1_), calls=%async_computation.7 | async-start | bytes 2883584 | tf_op jit(solution)/shard_map/all_to_all | solution.py:625
  493.1 46.6 %reduce-scatter.11.cloned.1.call-start = ((), (), s32[]{:S(2)}) async-start(), calls=%async_computation.13 | async-start | bytes 1310720 | tf_op jit(solution)/shard_map/reduce_scatter | solution.py:622
  493.2 18.9 %collective-permute-start.63 = (f32[8,448]{1,0:T(8,128)S(1)}, f32[8,448]{1,0:T(8,128)S(1)}, u32[]{:S(2)}, u32[]{:S(2)}) collective-permute-start(f32[8,448]{1,0:T(8,128)S(1)} %slice_select_fusion.1), channel_id=1, source_target_pairs={{0,8},{4,12},{8,0},{12,4},{16,24},{20,28},{24,16},{28,20},{1,9},{5... | collective-permute-start | bytes 43016 | tf_op jit(solution)/shard_map/ppermute | solution.py:553
  513.4 11.2 %collective-permute-start.65 = (f32[448]{0:T(512)S(1)}, f32[448]{0:T(512)S(1)}, u32[]{:S(2)}, u32[]{:S(2)}) collective-permute-start(f32[448]{0:T(512)S(1)} %bitcast.101), channel_id=1, source_target_pairs={{0,1},{1,0},{2,3},{3,2},{4,5},{5,4},{6,7},{7,6},{8,9},{9,8},{10,11... | collective-permute-start | bytes 5384 | tf_op jit(solution)/shard_map/ppermute | solution.py:672
  514.8 9.8 %collective-permute-start.66 = (f32[448]{0:T(512)S(1)}, f32[448]{0:T(512)S(1)}, u32[]{:S(2)}, u32[]{:S(2)}) collective-permute-start(f32[448]{0:T(512)S(1)} %bitcast.100), channel_id=1, source_target_pairs={{0,2},{1,3},{2,0},{3,1},{4,6},{5,7},{6,4},{7,5},{8,10},{9,11},{10,... | collective-permute-start | bytes 5384 | tf_op jit(solution)/shard_map/ppermute | solution.py:672
  517.8 16.8 %all-to-all-start.2 = ((bf16[8,64,768]{2,1,0:T(8,128)(2,1)}), bf16[8,64,768]{2,1,0:T(8,128)(2,1)}, u32[]{:S(2)}, u32[]{:S(2)}) async-start(bf16[8,64,768]{2,1,0:T(8,128)(2,1)} %bitcast.92), calls=%async_computation.5 | async-start | bytes 1572864 | tf_op jit(solution)/shard_map/all_to_all | solution.py:625
  (96 other events, 786.6 us)
Sparse Core Ops, SparseCore 0:
  11.3 30.6 all-gather.6
  44.2 62.9 all-gather.10
  109.4 105.3 all-gather.12
  216.2 57.4 all-gather.8
  276.0 54.7 reduce-scatter.4
  332.9 102.1 reduce-scatter.6
  437.3 60.7 reduce-scatter.8
  500.4 27.2 reduce-scatter.10

commit v3 on v2

--- a/solution.py
+++ b/solution.py
@@ -539,6 +539,46 @@
     )(blocks)
 
 
+def pick_columns(weight, lists):
+    rows, width = weight.shape
+    part = width // sum(len(blocks) for blocks in lists)
+
+    def kernel(weight_ref, blocks_ref):
+        whole = weight_ref[...].astype(F4)
+        for i, blocks in enumerate(lists):
+            columns = [whole[:, at * part : (at + 1) * part] for at in blocks]
+            blocks_ref[i] = jnp.concatenate(columns, 1).astype(BF)
+
+    return pl.pallas_call(
+        kernel,
+        out_shape=jax.ShapeDtypeStruct((len(lists), rows, part * len(lists[0])), BF),
+        compiler_params=pltpu.CompilerParams(vmem_limit_bytes=32 << 20),
+        name="pick_columns",
+    )(weight)
+
+
+def place_columns(blocks, lists):
+    parts, rows, held = blocks.shape
+    count = len(lists[0])
+    part = held // count
+    place = {at: (i, j) for i, each in enumerate(lists) for j, at in enumerate(each)}
+
+    def kernel(blocks_ref, whole_ref):
+        whole = [blocks_ref[i].astype(F4) for i in range(parts)]
+        columns = []
+        for at in range(parts * count):
+            i, j = place[at]
+            columns.append(whole[i][:, j * part : (j + 1) * part])
+        whole_ref[...] = jnp.concatenate(columns, 1)
+
+    return pl.pallas_call(
+        kernel,
+        out_shape=jax.ShapeDtypeStruct((rows, parts * held), F4),
+        compiler_params=pltpu.CompilerParams(vmem_limit_bytes=32 << 20),
+        name="place_columns",
+    )(blocks)
+
+
 class Links:
     def __init__(self):
         self.ns = lax.axis_size("seq")
@@ -703,8 +743,8 @@
     out_here = links.line_gather(w_out)
     short = jnp.concatenate([norm1_gain, norm1_shift, norm2_gain, norm2_shift, b_qkv])
     short_line = links.short_gather_line(short)
-    qkv_blocks = w_qkv.reshape(shard_rows, 3, ns, cols).transpose(2, 0, 1, 3)
-    qkv_blocks = links.swap_blocks(qkv_blocks.reshape(ns, shard_rows, 3 * cols))
+    qkv_lists = [[s, ns + s, 2 * ns + s] for s in range(ns)]
+    qkv_blocks = links.swap_blocks(pick_columns(w_qkv, qkv_lists))
     qkv_blocks, short_line = turn([qkv_blocks, short_line], out_here)
     qkv_line = links.line_gather(qkv_blocks[None])
     ff_blocks = links.swap_blocks(pair_columns(w_gate, w_up, lists))
@@ -746,12 +786,12 @@
     found, vectors, (ff_blocks, cotangent_low) = let(
         [arrays(first_pieces), vectors, [ff_blocks, cotangent_low]]
     )
-    found, vectors, (ff_blocks, w_down, cotangent_low) = let(
-        [found, vectors, [ff_blocks, w_down, cotangent_low]], qkv_line
+    found, vectors, (ff_blocks, cotangent_low) = let(
+        [found, vectors, [ff_blocks, cotangent_low]], qkv_line
     )
     first_pieces = renewed(first_pieces, found)
     ff_line = links.line_gather(ff_blocks[None])
-    down_here = links.line_gather(after(w_down, ff_line))
+    down_here = links.line_gather(w_down)
     cotangent_pieces = arrays(links.plane_gather(cotangent_low))
     normed_rows, queries, keys, values, mixed, mixed_rel, log_totals = attend(
         place,
@@ -806,7 +846,8 @@
     d_projected = after(d_projected, first_send)
     qkv_grad = links.rows_by_line(dot_tn(normed_rows, d_projected).astype(BF), shard_rows)
     qkv_sum = links.line_reduce(after(qkv_grad, ff_sum))
-    out_share = links.line_reduce(after(out_grad, qkv_sum))
+    ff_swapped = links.swap_blocks(ff_sum)
+    out_share = links.line_reduce(after(out_grad, qkv_sum, ff_swapped))
     qkv_sum = qkv_sum.reshape(ns, shard_rows, -1)
     bias_grad = bias_grad.reshape(3, 1, cols)
 
@@ -837,9 +878,8 @@
     )
     short_sums = links.short_reduce(short_terms)
 
-    gate_share, up_share = part_columns(links.swap_blocks(ff_sum), lists)
-    qkv_share = links.swap_blocks(qkv_sum).reshape(ns, shard_rows, 3, cols).transpose(1, 2, 0, 3)
-    qkv_share = qkv_share.reshape(shard_rows, 3 * width).astype(F4)
+    gate_share, up_share = part_columns(ff_swapped, lists)
+    qkv_share = place_columns(links.swap_blocks(qkv_sum), qkv_lists)
     return (
         layer_out.reshape(1, tok_rows, width),
         grad_in,

time: 553 us -> 545 us (0.986)
  waiting for transfers between devices: 262 us -> 250 us
  other arithmetic: 25.9 us -> 33.5 us
    ppermute x62, waiting for transfers between devices: 133 us -> 125 us  [flip(): return lax.ppermute(values, 'seq', [(i, i ^ bit) for i in range(self.ns)])]
    all_gather x4, waiting for transfers between devices: 80.3 us -> 73.6 us  [line_gather(): return lax.all_gather(own, 'fsdp', axis=0, tiled=True)]
    unnamed x134 -> x150, local copies, waits for them, and re-layouts: 13.1 us -> 12.3 us
  transfers between devices with their start and end apart: 80 -> 80, of which waited for: 41 -> 46; matrix products, arithmetic and copies ran while one was open for 17% -> 18% of each run, Pallas kernels for 16% -> 17%
where the time goes in v3:
time: 545 us; the launch traced here: 541 us
  waiting for transfers between devices  250 us (46%)
  Pallas kernels  91.4 us (17%)
  starting transfers between devices  76.3 us (14%)
  matrix products  39.2 us (7%)
  local copies, waits for them, and re-layouts  34.9 us (6%)
  other arithmetic  33.5 us (6%)
  between operations  15.6 us (3%)
    ppermute x62, waiting for transfers between devices, flip(): return lax.ppermute(values, 'seq', [(i, i ^ bit) for i in range(self.ns)])  125 us
    all_gather x4, waiting for transfers between devices, line_gather(): return lax.all_gather(own, 'fsdp', axis=0, tiled=True)  73.6 us
    ppermute x62, starting transfers between devices, flip(): return lax.ppermute(values, 'seq', [(i, i ^ bit) for i in range(self.ns)])  49.6 us
    reduce_scatter x4, waiting for transfers between devices, line_reduce(): return lax.psum_scatter(terms, 'fsdp', scatter_dimension=0, tiled=True)  36.5 us
    pallas_call x1, Pallas kernels, attend_back(): pl.pallas_call(kernel, out_shape=[jax.ShapeDtypeStruct((length, width), B...  25.8 us
    dot_general x3, matrix products, dot_tn(): lax.dot_general(a, b, (((0,), (0,)), ((), ())), preferred_element_type=F4)  20 us
    pallas_call x1, Pallas kernels, attend(): pl.pallas_call(kernel, out_shape=[jax.ShapeDtypeStruct((length, width), B...  19.9 us
    pallas_call x1, Pallas kernels, feed_back(): pl.pallas_call(kernel, out_shape=[jax.ShapeDtypeStruct((length, both), BF...  18.7 us
  transfers between devices with their start and end apart: 80, of which 46 were waited for; matrix products, arithmetic and copies ran while one was open for 18% of the time, Pallas kernels for 17%

profile of v3, /device:TPU:0, one launch (start us, length us, event | category | flops | bytes accessed | tf_op | source)
XLA Modules:
  0.0 540.5 jit_solution(14646858023151589130)
XLA Ops:
  12.3 5.2 all-to-all-start
  19.2 2.6 collective-permute-start.10
  23.7 3.5 collective-permute-done.11
  30.1 12.1 %all-gather.7.cloned.1.call-done.refs_2_.refs_10_ = bf16[256,2048]{1,0:T(8,128)(2,1)} async-done(((bf16[64,2048]{1,0:T(8,128)(2,1)}), bf16[256,2048]{1,0:T(8,128)(2,1)}) %all-gather.7.cloned.1.call-update) | async-done | bytes 1048592 | tf_op jit(solution)/shard_map/all_gather | solution.py:659
  46.6 3.6 all-to-all-start.1
  52.2 4.8 collective-permute-done.refs_1_
  60.1 3.3 collective-permute-start.3
  63.4 9.4 %collective-permute-done.13 = bf16[8,448]{1,0:T(8,128)(2,1)S(1)} collective-permute-done((bf16[8,448]{1,0:T(8,128)(2,1)S(1)}, bf16[8,448]{1,0:T(8,128)(2,1)S(1)}, u32[]{:S(2)}, u32[]{:S(2)}) %collective-permute-start.13) | collective-permute-done | bytes 7200 | tf_op jit(solution)/shard_map/ppermute | solution.py:593
  89.0 18.2 %all-gather.11.cloned.1.call-done = bf16[32,64,768]{2,1,0:T(8,128)(2,1)} async-done(((bf16[8,64,768]{2,1,0:T(8,128)(2,1)}), bf16[32,64,768]{2,1,0:T(8,128)(2,1)}) %all-gather.11.cloned.1.call-update) | async-done | bytes 3145744 | tf_op jit(solution)/shard_map/all_gather | solution.py:659
  113.4 19.9 %attend.1 = (bf16[1024,2048]{1,0:T(8,128)(2,1)}, bf16[1024,256]{1,0:T(8,128)(2,1)}, bf16[1024,256]{1,0:T(8,128)(2,1)}, bf16[1024,256]{1,0:T(8,128)(2,1)}, bf16[1...) custom-call(s32[2]{0:T(128)} %pad_add_fusion.place_ref, ...), custom_call_target="tpu_custom_call" | custom-call | flops 16999999488 | tf_op jit(solution)/shard_map/attend/pallas_call | solution.py:191
  135.1 4.1 collective-permute-done.15
  143.0 5.5 %collective-permute-done.16 = bf16[64,2048]{1,0:T(8,128)(2,1)S(1)} collective-permute-done((bf16[64,2048]{1,0:T(8,128)(2,1)S(1)}, bf16[64,2048]{1,0:T(8,128)(2,1)S(1)}, u32[]{:S(2)}, u32[]{:S(2)}) %collective-permute-start.16) | collective-permute-done | bytes 262176 | tf_op jit(solution)/shard_map/ppermute | solution.py:593
  154.7 10.0 %collective-permute-done.17 = bf16[128,2048]{1,0:T(8,128)(2,1)S(1)} collective-permute-done((bf16[128,2048]{1,0:T(8,128)(2,1)S(1)}, bf16[128,2048]{1,0:T(8,128)(2,1)S(1)}, u32[]{:S(2)}, u32[]{:S(2)}) %collective-permute-start.17) | collective-permute-done | bytes 524320 | tf_op jit(solution)/shard_map/ppermute | solution.py:593
  169.2 6.8 %collective-permute-done.29.refs_11_ = bf16[128,2048]{1,0:T(8,128)(2,1)S(1)} collective-permute-done((bf16[128,2048]{1,0:T(8,128)(2,1)S(1)}, bf16[128,2048]{1,0:T(8,128)(2,1)S(1)}, u32[]{:S(2)}, u32[]{:S(2)}) %collective-permute-start.29) | collective-permute-done | bytes 524320 | tf_op jit(solution)/shard_map/ppermute | solution.py:593
  179.6 12.5 %collective-permute-done.31.refs_13_ = bf16[64,2048]{1,0:T(8,128)(2,1)S(1)} collective-permute-done((bf16[64,2048]{1,0:T(8,128)(2,1)S(1)}, bf16[64,2048]{1,0:T(8,128)(2,1)S(1)}, u32[]{:S(2)}, u32[]{:S(2)}) %collective-permute-start.31) | collective-permute-done | bytes 262176 | tf_op jit(solution)/shard_map/ppermute | solution.py:593
  197.6 6.0 %collective-permute-done.22.refs_3_ = bf16[64,2048]{1,0:T(8,128)(2,1)S(1)} collective-permute-done((bf16[64,2048]{1,0:T(8,128)(2,1)S(1)}, bf16[64,2048]{1,0:T(8,128)(2,1)S(1)}, u32[]{:S(2)}, u32[]{:S(2)}) %collective-permute-start.22) | collective-permute-done | bytes 262176 | tf_op jit(solution)/shard_map/ppermute | solution.py:593
  207.0 7.8 %all-gather.13.cloned.1.call-done = bf16[32,64,1408]{2,1,0:T(8,128)(2,1)} async-done(((bf16[8,64,1408]{2,1,0:T(8,128)(2,1)}), bf16[32,64,1408]{2,1,0:T(8,128)(2,1)}) %all-gather.13.cloned.1.call-update) | async-done | bytes 5767184 | tf_op jit(solution)/shard_map/all_gather | solution.py:659
  214.8 15.5 %feed.1 = (bf16[1024,2048]{1,0:T(8,128)(2,1)}, bf16[1024,2048]{1,0:T(8,128)(2,1)}, bf16[1024,704]{1,0:T(8,128)(2,1)}, f32[1024,1408]{1,0:T(8,128)}) custom-call(bf16[128,2048]{1,0:T(8,128)(2,1)} %copy-done.25, bf16[128,2048]{1,0:T(8,128)(2,1)} %copy-done.33, bf16[128,2048]{1,0:T(8,128)(2,1)} %copy-done.34, bf16[64,2048]{1,0:T(8,128)(2,1)} %copy-done.66, ...), custom_call_target="tpu_custom_call" | custom-call | flops 16999999488 | tf_op jit(solution)/shard_map/feed/pallas_call | solution.py:401
  230.3 7.4 %convolution_convert_fusion.2.refs_2_ = bf16[704,2048]{1,0:T(8,128)(2,1)} fusion(bf16[1024,704]{1,0:T(8,128)(2,1)} %get-tuple-element.103.refs_0_, bf16[1024,2048]{1,0:T(8,128)(2,1)} %get-tuple-element.104.refs_0_), kind=kOutput, calls=%fused_computation.7 | convolution fusion | flops 2954231808 | bytes 8519680 | tf_op jit(solution)/shard_map/dot_general | solution.py:27
  238.3 35.5 %all-gather.9.cloned.1.call-done.down_ref = bf16[704,2048]{1,0:T(8,128)(2,1)} async-done(((bf16[176,2048]{1,0:T(8,128)(2,1)}), bf16[704,2048]{1,0:T(8,128)(2,1)}) %all-gather.9.cloned.1.call-update) | async-done | bytes 2883600 | tf_op jit(solution)/shard_map/all_gather | solution.py:659
  273.8 18.7 %feed_back.1 = (bf16[1024,1408]{1,0:T(8,128)(2,1)}, bf16[512,2048]{1,0:T(8,128)(2,1)}, f32[512,2048]{1,0:T(8,128)}) custom-call(bf16[1024,2048]{1,0:T(8,128)(2,1)} %get-tuple-element.106.g_ref, f32[1024,1408]{1,0:T(8,128)} %get-tuple-element.107.both_ref, bf16[4,8,64,1408]{3,2,1,0:T(8,128)(2,1)} %bitcast.86, ...), custom_call_target="tpu_custom_call" | custom-call | flops 16999999488 | tf_op jit(solution)/shard_map/feed_back/pallas_call | solution.py:458
  292.5 8.8 %convolution_convert_fusion = bf16[2048,1408]{1,0:T(8,128)(2,1)S(1)} fusion(bf16[1024,2048]{1,0:T(8,128)(2,1)S(1)} %copy-done.72, bf16[1024,1408]{1,0:T(8,128)(2,1)} %get-tuple-element.112), kind=kOutput, calls=%fused_computation | convolution fusion | flops 5908463616 | bytes 12845056 | tf_op jit(solution)/shard_map/dot_general | solution.py:27
  301.3 2.9 copy.98
  304.3 26.5 %reduce-scatter.5.cloned.1.call-done.refs_1_ = bf16[176,2048]{1,0:T(8,128)(2,1)} async-done(((bf16[704,2048]{1,0:T(8,128)(2,1)}), bf16[176,2048]{1,0:T(8,128)(2,1)}) %reduce-scatter.5.cloned.1.call-update) | async-done | bytes 720912 | tf_op jit(solution)/shard_map/reduce_scatter | solution.py:662
  330.9 3.7 fusion.41
  337.7 4.9 collective-permute-done.39
  346.2 10.3 %collective-permute-done.40 = bf16[128,2048]{1,0:T(8,128)(2,1)S(1)} collective-permute-done((bf16[128,2048]{1,0:T(8,128)(2,1)S(1)}, bf16[128,2048]{1,0:T(8,128)(2,1)S(1)}, u32[]{:S(2)}, u32[]{:S(2)}) %collective-permute-start.40) | collective-permute-done | bytes 524320 | tf_op jit(solution)/shard_map/ppermute | solution.py:593
  360.7 2.9 fusion.40
  364.8 10.5 %collective-permute-done.43.refs_1_ = bf16[128,2048]{1,0:T(8,128)(2,1)S(1)} collective-permute-done((bf16[128,2048]{1,0:T(8,128)(2,1)S(1)}, bf16[128,2048]{1,0:T(8,128)(2,1)S(1)}, u32[]{:S(2)}, u32[]{:S(2)}) %collective-permute-start.43) | collective-permute-done | bytes 524320 | tf_op jit(solution)/shard_map/ppermute | solution.py:593
  378.9 2.9 collective-permute-done.45.refs_3_
  385.8 25.8 %attend_back.1 = (bf16[1024,2048]{1,0:T(8,128)(2,1)}, bf16[1024,768]{1,0:T(8,128)(2,1)}, bf16[1024,768]{1,0:T(8,128)(2,1)}, f32[1,768]{1,0:T(1,128)}) custom-call(s32[2]{0:T(128)} %pad_add_fusion.place_ref, bf16[128,2048]{1,0:T(8,128)(2,1)} %copy-done.26, bf16[128,2048]{1,0:T(8,128)(2,1)} %copy-done.29, bf16[128,2048]{1,0:T(8,128)(2,1)} %copy-done.30, ...), custom_call_target="tpu_custom_call" | custom-call | flops 25999998976 | tf_op jit(solution)/shard_map/attend_back/pallas_call | solution.py:312
  411.6 4.4 convolution_convert_fusion.4.refs_1_
  416.1 5.4 convolution_convert_fusion.5
  421.9 3.8 convolution_convert_fusion.1
  427.7 7.4 %reduce-scatter.7.cloned.1.call-done = bf16[1,8,64,1408]{3,2,1,0:T(8,128)(2,1)} async-done(((bf16[4,8,64,1408]{3,2,1,0:T(8,128)(2,1)}), bf16[1,8,64,1408]{3,2,1,0:T(8,128)(2,1)}) %reduce-scatter.7.cloned.1.call-update) | async-done | bytes 1441808 | tf_op jit(solution)/shard_map/reduce_scatter | solution.py:662
  439.8 6.1 %outer_rows.1.refs_0_ = bf16[256,2048]{1,0:T(8,128)(2,1)} custom-call(bf16[1024,256]{1,0:T(8,128)(2,1)} %get-tuple-element.100.left_ref, bf16[128,2048]{1,0:T(8,128)(2,1)} %copy-done.26, bf16[128,2048]{1,0:T(8,128)(2,1)} %copy-done.29, bf16[128,2048]{1,0:T(8,128)(2,1)} %copy-done.30, bf16[64,2048]{1,0:T(8,128)(2,1)} %copy-done.58, ...), custom_call_target="tpu_custom_call" | custom-call | flops 4000000000 | tf_op jit(solution)/shard_map/outer_rows/pallas_call | solution.py:352
  445.9 3.6 fusion.50
  452.6 3.4 fusion.49
  469.9 3.6 all-to-all-start.3
  473.7 3.5 collective-permute-done.59
  478.0 3.5 fusion.10
  484.0 4.6 collective-permute-done.54
  489.3 2.6 fusion.22
  491.9 8.2 %collective-permute-done.62 = f32[16,448]{1,0:T(8,128)S(1)} collective-permute-done((f32[16,448]{1,0:T(8,128)S(1)}, f32[16,448]{1,0:T(8,128)S(1)}, u32[]{:S(2)}, u32[]{:S(2)}) %collective-permute-start.62) | collective-permute-done | bytes 28704 | tf_op jit(solution)/shard_map/ppermute | solution.py:593
  500.1 3.5 collective-permute-start.63
  511.0 4.2 all-to-all-start.2
  515.3 2.8 fusion.23
  521.1 6.7 %all-to-all-done.2.blocks_ref = bf16[8,64,768]{2,1,0:T(8,128)(2,1)S(1)} async-done(((bf16[8,64,768]{2,1,0:T(8,128)(2,1)}), bf16[8,64,768]{2,1,0:T(8,128)(2,1)S(1)}, u32[]{:S(2)}, u32[]{:S(2)}) %all-to-all-start.2) | async-done | bytes 786464 | tf_op jit(solution)/shard_map/all_to_all | solution.py:665
  (409 shorter events, 136.0 us)
Async XLA Ops:
  7.2 34.9 %all-gather.7.cloned.1.call-start = ((), (), s32[]{:S(2)}) async-start(), calls=%async_computation.8 | async-start | bytes 1310720 | tf_op jit(solution)/shard_map/all_gather | solution.py:659
  12.3 17.8 %all-to-all-start = ((bf16[8,64,768]{2,1,0:T(8,128)(2,1)}), bf16[8,64,768]{2,1,0:T(8,128)(2,1)S(1)}, u32[]{:S(2)}, u32[]{:S(2)}) async-start(bf16[8,64,768]{2,1,0:T(8,128)(2,1)} %pick_columns.1), calls=%async_computation | async-start | bytes 1572864 | tf_op jit(solution)/shard_map/all_to_all | solution.py:665
  17.5 89.8 %all-gather.11.cloned.1.call-start = ((), (), s32[]{:S(2)}) async-start(), calls=%async_computation.14 | async-start | bytes 3932160 | tf_op jit(solution)/shard_map/all_gather | solution.py:659
  42.2 14.9 %collective-permute-start = (bf16[128,2048]{1,0:T(8,128)(2,1)S(1)}, bf16[128,2048]{1,0:T(8,128)(2,1)S(1)}, u32[]{:S(2)}, u32[]{:S(2)}) collective-permute-start(bf16[128,2048]{1,0:T(8,128)(2,1)S(1)} %bitcast.60), channel_id=1, source_target_pairs={{0,8},{4,12},{8,0},{12,4},{16,24},{20,28},{24,16},{28,20},{1,9},{5... | collective-permute-start | bytes 1572872 | tf_op jit(solution)/shard_map/ppermute | solution.py:593
  43.7 15.6 %collective-permute-start.1 = (bf16[128,2048]{1,0:T(8,128)(2,1)S(1)}, bf16[128,2048]{1,0:T(8,128)(2,1)S(1)}, u32[]{:S(2)}, u32[]{:S(2)}) collective-permute-start(bf16[128,2048]{1,0:T(8,128)(2,1)S(1)} %bitcast.61), channel_id=1, source_target_pairs={{0,16},{4,20},{8,24},{12,28},{16,0},{20,4},{24,8},{28,12},{1,17},{... | collective-permute-start | bytes 1572872 | tf_op jit(solution)/shard_map/ppermute | solution.py:593
  46.6 41.2 %all-to-all-start.1 = ((bf16[8,64,1408]{2,1,0:T(8,128)(2,1)}), bf16[8,64,1408]{2,1,0:T(8,128)(2,1)S(1)}, u32[]{:S(2)}, u32[]{:S(2)}) async-start(bf16[8,64,1408]{2,1,0:T(8,128)(2,1)} %pair_columns.1), calls=%async_computation.1 | async-start | bytes 2883584 | tf_op jit(solution)/shard_map/all_to_all | solution.py:665
  50.2 164.7 %all-gather.13.cloned.1.call-start = ((), (), s32[]{:S(2)}) async-start(), calls=%async_computation.15 | async-start | bytes 7208960 | tf_op jit(solution)/shard_map/all_gather | solution.py:659
  50.3 22.5 %collective-permute-start.13 = (bf16[8,448]{1,0:T(8,128)(2,1)S(1)}, bf16[8,448]{1,0:T(8,128)(2,1)S(1)}, u32[]{:S(2)}, u32[]{:S(2)}) collective-permute-start(bf16[8,448]{1,0:T(8,128)(2,1)S(1)} %pad_maximum_fusion.10), channel_id=1, source_target_pairs={{0,8},{4,12},{8,0},{12,4},{16,24},{20,28},{24,16},{28,20},{1,9},{5... | collective-permute-start | bytes 21512 | tf_op jit(solution)/shard_map/ppermute | solution.py:593
  57.8 20.5 %collective-permute-start.2 = (bf16[64,2048]{1,0:T(8,128)(2,1)}, bf16[64,2048]{1,0:T(8,128)(2,1)}, u32[]{:S(2)}, u32[]{:S(2)}) collective-permute-start(bf16[64,2048]{1,0:T(8,128)(2,1)} %slice.286), channel_id=1, source_target_pairs={{0,16},{4,20},{8,24},{12,28},{16,0},{20,4},{24,8},{28,12},{1,17},{... | collective-permute-start | bytes 786440 | tf_op jit(solution)/shard_map/ppermute | solution.py:593
  60.1 18.2 %collective-permute-start.3 = (bf16[64,2048]{1,0:T(8,128)(2,1)}, bf16[64,2048]{1,0:T(8,128)(2,1)}, u32[]{:S(2)}, u32[]{:S(2)}) collective-permute-start(bf16[64,2048]{1,0:T(8,128)(2,1)} %slice.287), channel_id=1, source_target_pairs={{0,8},{4,12},{8,0},{12,4},{16,24},{20,28},{24,16},{28,20},{1,9},{5... | collective-permute-start | bytes 786440 | tf_op jit(solution)/shard_map/ppermute | solution.py:593
  74.9 12.9 %collective-permute-start.4 = (bf16[128,2048]{1,0:T(8,128)(2,1)S(1)}, bf16[128,2048]{1,0:T(8,128)(2,1)S(1)}, u32[]{:S(2)}, u32[]{:S(2)}) collective-permute-start(bf16[128,2048]{1,0:T(8,128)(2,1)S(1)} %bitcast.62), channel_id=1, source_target_pairs={{0,4},{4,0},{8,12},{12,8},{16,20},{20,16},{24,28},{28,24},{1,5},{5... | collective-permute-start | bytes 1572872 | tf_op jit(solution)/shard_map/ppermute | solution.py:593
  75.7 12.1 %collective-permute-start.5 = (bf16[128,2048]{1,0:T(8,128)(2,1)S(1)}, bf16[128,2048]{1,0:T(8,128)(2,1)}, u32[]{:S(2)}, u32[]{:S(2)}) collective-permute-start(bf16[128,2048]{1,0:T(8,128)(2,1)S(1)} %collective-permute-done.refs_1_), channel_id=1, source_target_pairs={{0,4},{4,0},{8,12},{12,8},{16,20},{20,16},{24,28},{28,24},{1,5},{5... | collective-permute-start | bytes 1572872 | tf_op jit(solution)/shard_map/ppermute | solution.py:593
  78.3 9.5 %collective-permute-start.6 = (bf16[128,2048]{1,0:T(8,128)(2,1)S(1)}, bf16[128,2048]{1,0:T(8,128)(2,1)}, u32[]{:S(2)}, u32[]{:S(2)}) collective-permute-start(bf16[128,2048]{1,0:T(8,128)(2,1)S(1)} %collective-permute-done.1.refs_2_), channel_id=1, source_target_pairs={{0,4},{4,0},{8,12},{12,8},{16,20},{20,16},{24,28},{28,24},{1,5},{5... | collective-permute-start | bytes 1572872 | tf_op jit(solution)/shard_map/ppermute | solution.py:593
  78.3 9.5 %collective-permute-start.7 = (bf16[64,2048]{1,0:T(8,128)(2,1)}, bf16[64,2048]{1,0:T(8,128)(2,1)}, u32[]{:S(2)}, u32[]{:S(2)}) collective-permute-start(bf16[64,2048]{1,0:T(8,128)(2,1)} %collective-permute-done.2.refs_3_), channel_id=1, source_target_pairs={{0,4},{4,0},{8,12},{12,8},{16,20},{20,16},{24,28},{28,24},{1,5},{5... | collective-permute-start | bytes 786440 | tf_op jit(solution)/shard_map/ppermute | solution.py:593
  107.3 166.5 %all-gather.9.cloned.1.call-start = ((), (), s32[]{:S(2)}) async-start(), calls=%async_computation.9 | async-start | bytes 3604480 | tf_op jit(solution)/shard_map/all_gather | solution.py:659
  149.8 14.9 %collective-permute-start.17 = (bf16[128,2048]{1,0:T(8,128)(2,1)S(1)}, bf16[128,2048]{1,0:T(8,128)(2,1)S(1)}, u32[]{:S(2)}, u32[]{:S(2)}) collective-permute-start(bf16[128,2048]{1,0:T(8,128)(2,1)S(1)} %pad_maximum_fusion), channel_id=1, source_target_pairs={{0,8},{4,12},{8,0},{12,4},{16,24},{20,28},{24,16},{28,20},{1,9},{5... | collective-permute-start | bytes 1572872 | tf_op jit(solution)/shard_map/ppermute | solution.py:593
  151.4 14.9 %collective-permute-start.19 = (bf16[128,2048]{1,0:T(8,128)(2,1)S(1)}, bf16[128,2048]{1,0:T(8,128)(2,1)S(1)}, u32[]{:S(2)}, u32[]{:S(2)}) collective-permute-start(bf16[128,2048]{1,0:T(8,128)(2,1)S(1)} %pad_maximum_fusion.1), channel_id=1, source_target_pairs={{0,16},{4,20},{8,24},{12,28},{16,0},{20,4},{24,8},{28,12},{1,17},{... | collective-permute-start | bytes 1572872 | tf_op jit(solution)/shard_map/ppermute | solution.py:593
  152.3 178.5 %reduce-scatter.5.cloned.1.call-start = ((), (), s32[]{:S(2)}) async-start(), calls=%async_computation.10 | async-start | bytes 3604480 | tf_op jit(solution)/shard_map/reduce_scatter | solution.py:662
  152.6 23.3 %collective-permute-start.29 = (bf16[128,2048]{1,0:T(8,128)(2,1)S(1)}, bf16[128,2048]{1,0:T(8,128)(2,1)S(1)}, u32[]{:S(2)}, u32[]{:S(2)}) collective-permute-start(bf16[128,2048]{1,0:T(8,128)(2,1)S(1)} %copy-done.11), channel_id=1, source_target_pairs={{0,8},{4,12},{8,0},{12,4},{16,24},{20,28},{24,16},{28,20},{1,9},{5... | collective-permute-start | bytes 1572872 | tf_op jit(solution)/shard_map/ppermute | solution.py:593
  153.3 24.7 %collective-permute-start.30 = (bf16[128,2048]{1,0:T(8,128)(2,1)S(1)}, bf16[128,2048]{1,0:T(8,128)(2,1)S(1)}, u32[]{:S(2)}, u32[]{:S(2)}) collective-permute-start(bf16[128,2048]{1,0:T(8,128)(2,1)S(1)} %copy-done.11), channel_id=1, source_target_pairs={{0,16},{4,20},{8,24},{12,28},{16,0},{20,4},{24,8},{28,12},{1,17},{... | collective-permute-start | bytes 1572872 | tf_op jit(solution)/shard_map/ppermute | solution.py:593
  168.5 24.1 %collective-permute-start.20 = (bf16[128,2048]{1,0:T(8,128)(2,1)S(1)}, bf16[128,2048]{1,0:T(8,128)(2,1)S(1)}, u32[]{:S(2)}, u32[]{:S(2)}) collective-permute-start(bf16[128,2048]{1,0:T(8,128)(2,1)S(1)} %add_convert_fusion.refs_0_), channel_id=1, source_target_pairs={{0,8},{4,12},{8,0},{12,4},{16,24},{20,28},{24,16},{28,20},{1,9},{5... | collective-permute-start | bytes 1572872 | tf_op jit(solution)/shard_map/ppermute | solution.py:593
  176.0 16.8 %collective-permute-start.21 = (bf16[128,2048]{1,0:T(8,128)(2,1)S(1)}, bf16[128,2048]{1,0:T(8,128)(2,1)S(1)}, u32[]{:S(2)}, u32[]{:S(2)}) collective-permute-start(bf16[128,2048]{1,0:T(8,128)(2,1)S(1)} %add_convert_fusion.refs_0_), channel_id=1, source_target_pairs={{0,16},{4,20},{8,24},{12,28},{16,0},{20,4},{24,8},{28,12},{1,17},{... | collective-permute-start | bytes 1572872 | tf_op jit(solution)/shard_map/ppermute | solution.py:593
  176.7 15.5 %collective-permute-start.31 = (bf16[64,2048]{1,0:T(8,128)(2,1)S(1)}, bf16[64,2048]{1,0:T(8,128)(2,1)S(1)}, u32[]{:S(2)}, u32[]{:S(2)}) collective-permute-start(bf16[64,2048]{1,0:T(8,128)(2,1)S(1)} %slice.297), channel_id=1, source_target_pairs={{0,16},{4,20},{8,24},{12,28},{16,0},{20,4},{24,8},{28,12},{1,17},{... | collective-permute-start | bytes 786440 | tf_op jit(solution)/shard_map/ppermute | solution.py:593
  178.1 14.1 %collective-permute-start.32 = (bf16[64,2048]{1,0:T(8,128)(2,1)S(1)}, bf16[64,2048]{1,0:T(8,128)(2,1)S(1)}, u32[]{:S(2)}, u32[]{:S(2)}) collective-permute-start(bf16[64,2048]{1,0:T(8,128)(2,1)S(1)} %slice.298), channel_id=1, source_target_pairs={{0,8},{4,12},{8,0},{12,4},{16,24},{20,28},{24,16},{28,20},{1,9},{5... | collective-permute-start | bytes 786440 | tf_op jit(solution)/shard_map/ppermute | solution.py:593
  179.6 13.6 %collective-permute-start.33 = (bf16[128,2048]{1,0:T(8,128)(2,1)S(1)}, bf16[128,2048]{1,0:T(8,128)(2,1)S(1)}, u32[]{:S(2)}, u32[]{:S(2)}) collective-permute-start(bf16[128,2048]{1,0:T(8,128)(2,1)S(1)} %copy-done.11), channel_id=1, source_target_pairs={{0,4},{4,0},{8,12},{12,8},{16,20},{20,16},{24,28},{28,24},{1,5},{5... | collective-permute-start | bytes 1572872 | tf_op jit(solution)/shard_map/ppermute | solution.py:593
  193.3 10.8 %collective-permute-start.24 = (bf16[128,2048]{1,0:T(8,128)(2,1)S(1)}, bf16[128,2048]{1,0:T(8,128)(2,1)S(1)}, u32[]{:S(2)}, u32[]{:S(2)}) collective-permute-start(bf16[128,2048]{1,0:T(8,128)(2,1)S(1)} %add_convert_fusion.refs_0_), channel_id=1, source_target_pairs={{0,4},{4,0},{8,12},{12,8},{16,20},{20,16},{24,28},{28,24},{1,5},{5... | collective-permute-start | bytes 1572872 | tf_op jit(solution)/shard_map/ppermute | solution.py:593
  197.1 9.9 %collective-permute-start.26 = (bf16[128,2048]{1,0:T(8,128)(2,1)S(1)}, bf16[128,2048]{1,0:T(8,128)(2,1)}, u32[]{:S(2)}, u32[]{:S(2)}) collective-permute-start(bf16[128,2048]{1,0:T(8,128)(2,1)S(1)} %collective-permute-done.21.refs_2_), channel_id=1, source_target_pairs={{0,4},{4,0},{8,12},{12,8},{16,20},{20,16},{24,28},{28,24},{1,5},{5... | collective-permute-start | bytes 1572872 | tf_op jit(solution)/shard_map/ppermute | solution.py:593
  237.8 197.3 %reduce-scatter.7.cloned.1.call-start = ((), (), s32[]{:S(2)}) async-start(), calls=%async_computation.11 | async-start | bytes 7208960 | tf_op jit(solution)/shard_map/reduce_scatter | solution.py:662
  304.3 26.6 %collective-permute-start.38 = (bf16[512,2048]{1,0:T(8,128)(2,1)}, bf16[512,2048]{1,0:T(8,128)(2,1)}, u32[]{:S(2)}, u32[]{:S(2)}) collective-permute-start(bf16[512,2048]{1,0:T(8,128)(2,1)} %get-tuple-element.114), channel_id=1, source_target_pairs={{0,4},{4,0},{8,12},{12,8},{16,20},{20,16},{24,28},{28,24},{1,5},{5... | collective-permute-start | bytes 6291464 | tf_op jit(solution)/shard_map/ppermute | solution.py:593
  330.8 172.7 %reduce-scatter.9.cloned.1.call-start = ((), (), s32[]{:S(2)}) async-start(), calls=%async_computation.12 | async-start | bytes 3932160 | tf_op jit(solution)/shard_map/reduce_scatter | solution.py:662
  344.0 12.5 %collective-permute-start.40 = (bf16[128,2048]{1,0:T(8,128)(2,1)S(1)}, bf16[128,2048]{1,0:T(8,128)(2,1)S(1)}, u32[]{:S(2)}, u32[]{:S(2)}) collective-permute-start(bf16[128,2048]{1,0:T(8,128)(2,1)S(1)} %pad_maximum_fusion.2), channel_id=1, source_target_pairs={{0,8},{4,12},{8,0},{12,4},{16,24},{20,28},{24,16},{28,20},{1,9},{5... | collective-permute-start | bytes 1572872 | tf_op jit(solution)/shard_map/ppermute | solution.py:593
  345.6 12.2 %collective-permute-start.42 = (bf16[128,2048]{1,0:T(8,128)(2,1)S(1)}, bf16[128,2048]{1,0:T(8,128)(2,1)S(1)}, u32[]{:S(2)}, u32[]{:S(2)}) collective-permute-start(bf16[128,2048]{1,0:T(8,128)(2,1)S(1)} %pad_maximum_fusion.3), channel_id=1, source_target_pairs={{0,16},{4,20},{8,24},{12,28},{16,0},{20,4},{24,8},{28,12},{1,17},{... | collective-permute-start | bytes 1572872 | tf_op jit(solution)/shard_map/ppermute | solution.py:593
  363.6 11.7 %collective-permute-start.43 = (bf16[128,2048]{1,0:T(8,128)(2,1)S(1)}, bf16[128,2048]{1,0:T(8,128)(2,1)S(1)}, u32[]{:S(2)}, u32[]{:S(2)}) collective-permute-start(bf16[128,2048]{1,0:T(8,128)(2,1)S(1)} %get-tuple-element.135.refs_0_), channel_id=1, source_target_pairs={{0,8},{4,12},{8,0},{12,4},{16,24},{20,28},{24,16},{28,20},{1,9},{5... | collective-permute-start | bytes 1572872 | tf_op jit(solution)/shard_map/ppermute | solution.py:593
  364.2 12.1 %collective-permute-start.44 = (bf16[128,2048]{1,0:T(8,128)(2,1)S(1)}, bf16[128,2048]{1,0:T(8,128)(2,1)S(1)}, u32[]{:S(2)}, u32[]{:S(2)}) collective-permute-start(bf16[128,2048]{1,0:T(8,128)(2,1)S(1)} %get-tuple-element.135.refs_0_), channel_id=1, source_target_pairs={{0,16},{4,20},{8,24},{12,28},{16,0},{20,4},{24,8},{28,12},{1,17},{... | collective-permute-start | bytes 1572872 | tf_op jit(solution)/shard_map/ppermute | solution.py:593
  364.8 18.7 %collective-permute-start.47 = (bf16[128,2048]{1,0:T(8,128)(2,1)S(1)}, bf16[128,2048]{1,0:T(8,128)(2,1)S(1)}, u32[]{:S(2)}, u32[]{:S(2)}) collective-permute-start(bf16[128,2048]{1,0:T(8,128)(2,1)S(1)} %get-tuple-element.135.refs_0_), channel_id=1, source_target_pairs={{0,4},{4,0},{8,12},{12,8},{16,20},{20,16},{24,28},{28,24},{1,5},{5... | collective-permute-start | bytes 1572872 | tf_op jit(solution)/shard_map/ppermute | solution.py:593
  416.0 29.9 %collective-permute-start.57 = (bf16[512,2048]{1,0:T(8,128)(2,1)}, bf16[512,2048]{1,0:T(8,128)(2,1)}, u32[]{:S(2)}, u32[]{:S(2)}) collective-permute-start(bf16[512,2048]{1,0:T(8,128)(2,1)} %convolution_convert_fusion.4.refs_1_), channel_id=1, source_target_pairs={{0,4},{4,0},{8,12},{12,8},{16,20},{20,16},{24,28},{28,24},{1,5},{5... | collective-permute-start | bytes 6291464 | tf_op jit(solution)/shard_map/ppermute | solution.py:593
  421.5 31.1 %collective-permute-start.52 = (bf16[512,2048]{1,0:T(8,128)(2,1)}, bf16[512,2048]{1,0:T(8,128)(2,1)}, u32[]{:S(2)}, u32[]{:S(2)}) collective-permute-start(bf16[512,2048]{1,0:T(8,128)(2,1)} %convolution_convert_fusion.5), channel_id=1, source_target_pairs={{0,4},{4,0},{8,12},{12,8},{16,20},{20,16},{24,28},{28,24},{1,5},{5... | collective-permute-start | bytes 6291464 | tf_op jit(solution)/shard_map/ppermute | solution.py:593
  456.8 9.2 %collective-permute-start.55 = (bf16[64,2048]{1,0:T(8,128)(2,1)S(1)}, bf16[64,2048]{1,0:T(8,128)(2,1)S(1)}, u32[]{:S(2)}, u32[]{:S(2)}) collective-permute-start(bf16[64,2048]{1,0:T(8,128)(2,1)S(1)} %get-tuple-element.155), channel_id=1, source_target_pairs={{0,8},{4,12},{8,0},{12,4},{16,24},{20,28},{24,16},{28,20},{1,9},{5... | collective-permute-start | bytes 786440 | tf_op jit(solution)/shard_map/ppermute | solution.py:593
  460.3 16.9 %collective-permute-start.59 = (bf16[128,2048]{1,0:T(8,128)(2,1)}, bf16[128,2048]{1,0:T(8,128)(2,1)S(1)}, u32[]{:S(2)}, u32[]{:S(2)}) collective-permute-start(bf16[128,2048]{1,0:T(8,128)(2,1)} %pad_maximum_fusion.6), channel_id=1, source_target_pairs={{0,8},{4,12},{8,0},{12,4},{16,24},{20,28},{24,16},{28,20},{1,9},{5... | collective-permute-start | bytes 1572872 | tf_op jit(solution)/shard_map/ppermute | solution.py:593
  462.8 15.2 %collective-permute-start.61 = (bf16[128,2048]{1,0:T(8,128)(2,1)}, bf16[128,2048]{1,0:T(8,128)(2,1)}, u32[]{:S(2)}, u32[]{:S(2)}) collective-permute-start(bf16[128,2048]{1,0:T(8,128)(2,1)} %pad_maximum_fusion.7), channel_id=1, source_target_pairs={{0,16},{4,20},{8,24},{12,28},{16,0},{20,4},{24,8},{28,12},{1,17},{... | collective-permute-start | bytes 1572872 | tf_op jit(solution)/shard_map/ppermute | solution.py:593
  467.0 21.6 %collective-permute-start.54 = (bf16[128,2048]{1,0:T(8,128)(2,1)}, bf16[128,2048]{1,0:T(8,128)(2,1)}, u32[]{:S(2)}, u32[]{:S(2)}) collective-permute-start(bf16[128,2048]{1,0:T(8,128)(2,1)} %pad_maximum_fusion.4), channel_id=1, source_target_pairs={{0,8},{4,12},{8,0},{12,4},{16,24},{20,28},{24,16},{28,20},{1,9},{5... | collective-permute-start | bytes 1572872 | tf_op jit(solution)/shard_map/ppermute | solution.py:593
  468.5 20.8 %collective-permute-start.56 = (bf16[128,2048]{1,0:T(8,128)(2,1)}, bf16[128,2048]{1,0:T(8,128)(2,1)}, u32[]{:S(2)}, u32[]{:S(2)}) collective-permute-start(bf16[128,2048]{1,0:T(8,128)(2,1)} %pad_maximum_fusion.5), channel_id=1, source_target_pairs={{0,16},{4,20},{8,24},{12,28},{16,0},{20,4},{24,8},{28,12},{1,17},{... | collective-permute-start | bytes 1572872 | tf_op jit(solution)/shard_map/ppermute | solution.py:593
  469.9 33.7 %all-to-all-start.3 = ((bf16[8,64,1408]{2,1,0:T(8,128)(2,1)}), bf16[8,64,1408]{2,1,0:T(8,128)(2,1)S(1)}, u32[]{:S(2)}, u32[]{:S(2)}) async-start(bf16[8,64,1408]{2,1,0:T(8,128)(2,1)} %bitcast.70), calls=%async_computation.6 | async-start | bytes 2883584 | tf_op jit(solution)/shard_map/all_to_all | solution.py:665
  473.4 58.2 %reduce-scatter.11.cloned.1.call-start = ((), (), s32[]{:S(2)}) async-start(), calls=%async_computation.13 | async-start | bytes 1310720 | tf_op jit(solution)/shard_map/reduce_scatter | solution.py:662
  483.3 16.8 %collective-permute-start.62 = (f32[16,448]{1,0:T(8,128)S(1)}, f32[16,448]{1,0:T(8,128)S(1)}, u32[]{:S(2)}, u32[]{:S(2)}) collective-permute-start(f32[16,448]{1,0:T(8,128)S(1)} %slice_select_fusion), channel_id=1, source_target_pairs={{0,16},{4,20},{8,24},{12,28},{16,0},{20,4},{24,8},{28,12},{1,17},{... | collective-permute-start | bytes 86024 | tf_op jit(solution)/shard_map/ppermute | solution.py:593
  506.6 11.5 %collective-permute-start.65 = (f32[448]{0:T(512)S(1)}, f32[448]{0:T(512)S(1)}, u32[]{:S(2)}, u32[]{:S(2)}) collective-permute-start(f32[448]{0:T(512)S(1)} %bitcast.84), channel_id=1, source_target_pairs={{0,1},{1,0},{2,3},{3,2},{4,5},{5,4},{6,7},{7,6},{8,9},{9,8},{10,11... | collective-permute-start | bytes 5384 | tf_op jit(solution)/shard_map/ppermute | solution.py:712
  508.1 9.9 %collective-permute-start.66 = (f32[448]{0:T(512)S(1)}, f32[448]{0:T(512)S(1)}, u32[]{:S(2)}, u32[]{:S(2)}) collective-permute-start(f32[448]{0:T(512)S(1)} %bitcast.83), channel_id=1, source_target_pairs={{0,2},{1,3},{2,0},{3,1},{4,6},{5,7},{6,4},{7,5},{8,10},{9,11},{10,... | collective-permute-start | bytes 5384 | tf_op jit(solution)/shard_map/ppermute | solution.py:712
  511.0 16.8 %all-to-all-start.2 = ((bf16[8,64,768]{2,1,0:T(8,128)(2,1)}), bf16[8,64,768]{2,1,0:T(8,128)(2,1)S(1)}, u32[]{:S(2)}, u32[]{:S(2)}) async-start(bf16[8,64,768]{2,1,0:T(8,128)(2,1)} %bitcast.77), calls=%async_computation.5 | async-start | bytes 1572864 | tf_op jit(solution)/shard_map/all_to_all | solution.py:665
  (105 other events, 973.4 us)
Sparse Core Ops, SparseCore 0:
  11.4 30.6 all-gather.6
  44.3 62.9 all-gather.10
  109.4 105.3 all-gather.12
  216.2 57.4 all-gather.8
  275.9 54.8 reduce-scatter.4
  333.0 102.1 reduce-scatter.6
  437.4 60.7 reduce-scatter.8
  504.8 26.7 reduce-scatter.10

commit v4 on v3

--- a/solution.py
+++ b/solution.py
@@ -786,9 +786,7 @@
     found, vectors, (ff_blocks, cotangent_low) = let(
         [arrays(first_pieces), vectors, [ff_blocks, cotangent_low]]
     )
-    found, vectors, (ff_blocks, cotangent_low) = let(
-        [found, vectors, [ff_blocks, cotangent_low]], qkv_line
-    )
+    found, vectors, (cotangent_low,) = let([found, vectors, [cotangent_low]], qkv_line)
     first_pieces = renewed(first_pieces, found)
     ff_line = links.line_gather(ff_blocks[None])
     down_here = links.line_gather(w_down)
@@ -819,7 +817,7 @@
     grad_rows, gate_up = turn([cotangent_rows, gate_up], down_grad)
     d_ff, second_send, second_keep = feed_back(grad_rows, gate_up, ff_line, down_here)
     ff_grad = links.rows_by_line(dot_tn(second_rows, d_ff).astype(BF), shard_rows)
-    ff_sum = links.line_reduce(after(ff_grad, down_sum)).reshape(ns, shard_rows, -1)
+    ff_sum = links.line_reduce(ff_grad).reshape(ns, shard_rows, -1)
     second_send, second_keep = turn([second_send, second_keep], ff_grad)
     d_second = links.plane_reduce(second_keep, second_send)
     d_second = after(d_second, down_sum)
@@ -845,7 +843,7 @@
     first_send = dot_nt(d_projected_rel[half:], qkv_here).astype(BF)
     d_projected = after(d_projected, first_send)
     qkv_grad = links.rows_by_line(dot_tn(normed_rows, d_projected).astype(BF), shard_rows)
-    qkv_sum = links.line_reduce(after(qkv_grad, ff_sum))
+    qkv_sum = links.line_reduce(qkv_grad)
     ff_swapped = links.swap_blocks(ff_sum)
     out_share = links.line_reduce(after(out_grad, qkv_sum, ff_swapped))
     qkv_sum = qkv_sum.reshape(ns, shard_rows, -1)

time: 545 us -> 541 us (level)
  waiting for transfers between devices: 250 us -> 243 us
    reduce_scatter x4, waiting for transfers between devices: 36.5 us -> 28.2 us  [line_reduce(): return lax.psum_scatter(terms, 'fsdp', scatter_dimension=0, tiled=True)]
    unnamed x150 -> x148, local copies, waits for them, and re-layouts: 12.3 us -> 10.7 us
  transfers between devices with their start and end apart: 80 -> 80, of which waited for: 46 -> 42; matrix products, arithmetic and copies ran while one was open for 18% -> 18% of each run, Pallas kernels for 17% -> 17%
where the time goes in v4:
time: 541 us; the launch traced here: 537 us
  waiting for transfers between devices  243 us (45%)
  Pallas kernels  90.5 us (17%)
  starting transfers between devices  80.5 us (15%)
  matrix products  39 us (7%)
  other arithmetic  34.5 us (6%)
  local copies, waits for them, and re-layouts  33.2 us (6%)
  between operations  15.6 us (3%)
    ppermute x62, waiting for transfers between devices, flip(): return lax.ppermute(values, 'seq', [(i, i ^ bit) for i in range(self.ns)])  127 us
    all_gather x4, waiting for transfers between devices, line_gather(): return lax.all_gather(own, 'fsdp', axis=0, tiled=True)  74.3 us
    ppermute x62, starting transfers between devices, flip(): return lax.ppermute(values, 'seq', [(i, i ^ bit) for i in range(self.ns)])  54.2 us
    reduce_scatter x4, waiting for transfers between devices, line_reduce(): return lax.psum_scatter(terms, 'fsdp', scatter_dimension=0, tiled=True)  28.2 us
    pallas_call x1, Pallas kernels, attend_back(): pl.pallas_call(kernel, out_shape=[jax.ShapeDtypeStruct((length, width), B...  25.9 us
    dot_general x3, matrix products, dot_tn(): lax.dot_general(a, b, (((0,), (0,)), ((), ())), preferred_element_type=F4)  20 us
    pallas_call x1, Pallas kernels, attend(): pl.pallas_call(kernel, out_shape=[jax.ShapeDtypeStruct((length, width), B...  18.8 us
    pallas_call x1, Pallas kernels, feed_back(): pl.pallas_call(kernel, out_shape=[jax.ShapeDtypeStruct((length, both), BF...  18.7 us
  transfers between devices with their start and end apart: 80, of which 42 were waited for; matrix products, arithmetic and copies ran while one was open for 18% of the time, Pallas kernels for 17%

profile of v4, /device:TPU:0, one launch (start us, length us, event | category | flops | bytes accessed | tf_op | source)
XLA Modules:
  0.0 536.6 jit_solution(972158063591157602)
XLA Ops:
  12.3 5.2 all-to-all-start
  19.2 2.6 collective-permute-start.10
  23.7 3.5 collective-permute-done.11
  30.0 12.1 %all-gather.7.cloned.1.call-done.refs_2_.refs_10_ = bf16[256,2048]{1,0:T(8,128)(2,1)} async-done(((bf16[64,2048]{1,0:T(8,128)(2,1)}), bf16[256,2048]{1,0:T(8,128)(2,1)}) %all-gather.7.cloned.1.call-update) | async-done | bytes 1048592 | tf_op jit(solution)/shard_map/all_gather | solution.py:659
  46.6 3.6 all-to-all-start.1
  52.2 4.8 collective-permute-done.refs_1_
  60.0 3.3 collective-permute-start.3
  63.3 9.4 %collective-permute-done.13 = bf16[8,448]{1,0:T(8,128)(2,1)S(1)} collective-permute-done((bf16[8,448]{1,0:T(8,128)(2,1)S(1)}, bf16[8,448]{1,0:T(8,128)(2,1)S(1)}, u32[]{:S(2)}, u32[]{:S(2)}) %collective-permute-start.13) | collective-permute-done | bytes 7200 | tf_op jit(solution)/shard_map/ppermute | solution.py:593
  95.4 11.9 %all-gather.11.cloned.1.call-done = bf16[32,64,768]{2,1,0:T(8,128)(2,1)} async-done(((bf16[8,64,768]{2,1,0:T(8,128)(2,1)}), bf16[32,64,768]{2,1,0:T(8,128)(2,1)}) %all-gather.11.cloned.1.call-update) | async-done | bytes 3145744 | tf_op jit(solution)/shard_map/all_gather | solution.py:659
  107.3 18.8 %attend.1 = (bf16[1024,2048]{1,0:T(8,128)(2,1)}, bf16[1024,256]{1,0:T(8,128)(2,1)}, bf16[1024,256]{1,0:T(8,128)(2,1)}, bf16[1024,256]{1,0:T(8,128)(2,1)}, bf16[1...) custom-call(s32[2]{0:T(128)} %pad_add_fusion.place_ref, ...), custom_call_target="tpu_custom_call" | custom-call | flops 16999999488 | tf_op jit(solution)/shard_map/attend/pallas_call | solution.py:191
  127.9 4.1 collective-permute-done.15
  136.0 5.4 %collective-permute-done.16 = bf16[64,2048]{1,0:T(8,128)(2,1)S(1)} collective-permute-done((bf16[64,2048]{1,0:T(8,128)(2,1)S(1)}, bf16[64,2048]{1,0:T(8,128)(2,1)S(1)}, u32[]{:S(2)}, u32[]{:S(2)}) %collective-permute-start.16) | collective-permute-done | bytes 262176 | tf_op jit(solution)/shard_map/ppermute | solution.py:593
  147.7 10.0 %collective-permute-done.17 = bf16[128,2048]{1,0:T(8,128)(2,1)S(1)} collective-permute-done((bf16[128,2048]{1,0:T(8,128)(2,1)S(1)}, bf16[128,2048]{1,0:T(8,128)(2,1)S(1)}, u32[]{:S(2)}, u32[]{:S(2)}) %collective-permute-start.17) | collective-permute-done | bytes 524320 | tf_op jit(solution)/shard_map/ppermute | solution.py:593
  162.1 6.8 %collective-permute-done.29.refs_11_ = bf16[128,2048]{1,0:T(8,128)(2,1)S(1)} collective-permute-done((bf16[128,2048]{1,0:T(8,128)(2,1)S(1)}, bf16[128,2048]{1,0:T(8,128)(2,1)S(1)}, u32[]{:S(2)}, u32[]{:S(2)}) %collective-permute-start.29) | collective-permute-done | bytes 524320 | tf_op jit(solution)/shard_map/ppermute | solution.py:593
  172.6 12.5 %collective-permute-done.31.refs_13_ = bf16[64,2048]{1,0:T(8,128)(2,1)S(1)} collective-permute-done((bf16[64,2048]{1,0:T(8,128)(2,1)S(1)}, bf16[64,2048]{1,0:T(8,128)(2,1)S(1)}, u32[]{:S(2)}, u32[]{:S(2)}) %collective-permute-start.31) | collective-permute-done | bytes 262176 | tf_op jit(solution)/shard_map/ppermute | solution.py:593
  190.6 6.0 %collective-permute-done.22.refs_3_ = bf16[64,2048]{1,0:T(8,128)(2,1)S(1)} collective-permute-done((bf16[64,2048]{1,0:T(8,128)(2,1)S(1)}, bf16[64,2048]{1,0:T(8,128)(2,1)S(1)}, u32[]{:S(2)}, u32[]{:S(2)}) %collective-permute-start.22) | collective-permute-done | bytes 262176 | tf_op jit(solution)/shard_map/ppermute | solution.py:593
  199.9 14.9 %all-gather.13.cloned.1.call-done = bf16[32,64,1408]{2,1,0:T(8,128)(2,1)} async-done(((bf16[8,64,1408]{2,1,0:T(8,128)(2,1)}), bf16[32,64,1408]{2,1,0:T(8,128)(2,1)}) %all-gather.13.cloned.1.call-update) | async-done | bytes 5767184 | tf_op jit(solution)/shard_map/all_gather | solution.py:659
  214.8 15.5 %feed.1 = (bf16[1024,2048]{1,0:T(8,128)(2,1)}, bf16[1024,2048]{1,0:T(8,128)(2,1)}, bf16[1024,704]{1,0:T(8,128)(2,1)}, f32[1024,1408]{1,0:T(8,128)}) custom-call(bf16[128,2048]{1,0:T(8,128)(2,1)} %copy-done.25, bf16[128,2048]{1,0:T(8,128)(2,1)} %copy-done.33, bf16[128,2048]{1,0:T(8,128)(2,1)} %copy-done.34, bf16[64,2048]{1,0:T(8,128)(2,1)} %copy-done.65, ...), custom_call_target="tpu_custom_call" | custom-call | flops 16999999488 | tf_op jit(solution)/shard_map/feed/pallas_call | solution.py:401
  230.3 7.4 %convolution_convert_fusion.2.refs_2_ = bf16[704,2048]{1,0:T(8,128)(2,1)} fusion(bf16[1024,704]{1,0:T(8,128)(2,1)} %get-tuple-element.101.refs_0_, bf16[1024,2048]{1,0:T(8,128)(2,1)} %get-tuple-element.102.refs_0_), kind=kOutput, calls=%fused_computation.7 | convolution fusion | flops 2954231808 | bytes 8519680 | tf_op jit(solution)/shard_map/dot_general | solution.py:27
  238.2 35.5 %all-gather.9.cloned.1.call-done.down_ref = bf16[704,2048]{1,0:T(8,128)(2,1)} async-done(((bf16[176,2048]{1,0:T(8,128)(2,1)}), bf16[704,2048]{1,0:T(8,128)(2,1)}) %all-gather.9.cloned.1.call-update) | async-done | bytes 2883600 | tf_op jit(solution)/shard_map/all_gather | solution.py:659
  273.8 18.7 %feed_back.1 = (bf16[1024,1408]{1,0:T(8,128)(2,1)}, bf16[512,2048]{1,0:T(8,128)(2,1)}, f32[512,2048]{1,0:T(8,128)}) custom-call(bf16[1024,2048]{1,0:T(8,128)(2,1)} %get-tuple-element.104.g_ref, f32[1024,1408]{1,0:T(8,128)} %get-tuple-element.105.both_ref, bf16[4,8,64,1408]{3,2,1,0:T(8,128)(2,1)} %bitcast.85, ...), custom_call_target="tpu_custom_call" | custom-call | flops 16999999488 | tf_op jit(solution)/shard_map/feed_back/pallas_call | solution.py:458
  292.5 8.8 %convolution_convert_fusion = bf16[2048,1408]{1,0:T(8,128)(2,1)S(1)} fusion(bf16[1024,2048]{1,0:T(8,128)(2,1)S(1)} %copy-done.71, bf16[1024,1408]{1,0:T(8,128)(2,1)} %get-tuple-element.110), kind=kOutput, calls=%fused_computation | convolution fusion | flops 5908463616 | bytes 12845056 | tf_op jit(solution)/shard_map/dot_general | solution.py:27
  301.3 2.9 copy.95
  304.3 4.4 collective-permute-done.38
  308.8 3.7 fusion.41
  315.6 5.4 %collective-permute-done.39 = bf16[64,2048]{1,0:T(8,128)(2,1)S(1)} collective-permute-done((bf16[64,2048]{1,0:T(8,128)(2,1)S(1)}, bf16[64,2048]{1,0:T(8,128)(2,1)S(1)}, u32[]{:S(2)}, u32[]{:S(2)}) %collective-permute-start.39) | collective-permute-done | bytes 262176 | tf_op jit(solution)/shard_map/ppermute | solution.py:593
  324.6 10.8 %collective-permute-done.40 = bf16[128,2048]{1,0:T(8,128)(2,1)S(1)} collective-permute-done((bf16[128,2048]{1,0:T(8,128)(2,1)S(1)}, bf16[128,2048]{1,0:T(8,128)(2,1)S(1)}, u32[]{:S(2)}, u32[]{:S(2)}) %collective-permute-start.40) | collective-permute-done | bytes 524320 | tf_op jit(solution)/shard_map/ppermute | solution.py:593
  339.8 3.0 fusion.40
  343.7 10.5 %collective-permute-done.43.refs_1_ = bf16[128,2048]{1,0:T(8,128)(2,1)S(1)} collective-permute-done((bf16[128,2048]{1,0:T(8,128)(2,1)S(1)}, bf16[128,2048]{1,0:T(8,128)(2,1)S(1)}, u32[]{:S(2)}, u32[]{:S(2)}) %collective-permute-start.43) | collective-permute-done | bytes 524320 | tf_op jit(solution)/shard_map/ppermute | solution.py:593
  365.1 25.9 %attend_back.1 = (bf16[1024,2048]{1,0:T(8,128)(2,1)}, bf16[1024,768]{1,0:T(8,128)(2,1)}, bf16[1024,768]{1,0:T(8,128)(2,1)}, f32[1,768]{1,0:T(1,128)}) custom-call(s32[2]{0:T(128)} %pad_add_fusion.place_ref, bf16[128,2048]{1,0:T(8,128)(2,1)} %copy-done.26, bf16[128,2048]{1,0:T(8,128)(2,1)} %copy-done.29, bf16[128,2048]{1,0:T(8,128)(2,1)} %copy-done.31, ...), custom_call_target="tpu_custom_call" | custom-call | flops 25999998976 | tf_op jit(solution)/shard_map/attend_back/pallas_call | solution.py:312
  391.0 4.3 convolution_convert_fusion.4.refs_1_
  395.4 5.3 convolution_convert_fusion.5
  401.1 3.7 convolution_convert_fusion.1
  411.5 6.1 %outer_rows.1.refs_0_ = bf16[256,2048]{1,0:T(8,128)(2,1)} custom-call(bf16[1024,256]{1,0:T(8,128)(2,1)} %get-tuple-element.98.left_ref, bf16[128,2048]{1,0:T(8,128)(2,1)} %copy-done.26, bf16[128,2048]{1,0:T(8,128)(2,1)} %copy-done.29, bf16[128,2048]{1,0:T(8,128)(2,1)} %copy-done.31, bf16[64,2048]{1,0:T(8,128)(2,1)} %copy-done.57, ...), custom_call_target="tpu_custom_call" | custom-call | flops 4000000000 | tf_op jit(solution)/shard_map/outer_rows/pallas_call | solution.py:352
  417.7 3.6 fusion.50
  423.9 3.4 fusion.49
  441.6 3.7 all-to-all-start.3
  445.6 3.9 collective-permute-done.59
  449.5 3.5 fusion.10
  456.4 4.4 collective-permute-done.54
  460.8 2.6 fusion.22
  463.4 7.8 %collective-permute-done.62 = f32[16,448]{1,0:T(8,128)S(1)} collective-permute-done((f32[16,448]{1,0:T(8,128)S(1)}, f32[16,448]{1,0:T(8,128)S(1)}, u32[]{:S(2)}, u32[]{:S(2)}) %collective-permute-start.62) | collective-permute-done | bytes 28704 | tf_op jit(solution)/shard_map/ppermute | solution.py:593
  471.3 4.9 collective-permute-start.63
  476.2 22.1 %reduce-scatter.7.cloned.1.call-done.refs_1_ = bf16[1,8,64,768]{3,2,1,0:T(8,128)(2,1)} async-done(((bf16[4,8,64,768]{3,2,1,0:T(8,128)(2,1)}), bf16[1,8,64,768]{3,2,1,0:T(8,128)(2,1)}) %reduce-scatter.7.cloned.1.call-update) | async-done | bytes 786448 | tf_op jit(solution)/shard_map/reduce_scatter | solution.py:662
  504.0 3.6 all-to-all-start.2
  507.7 2.8 fusion.23
  513.5 6.7 %all-to-all-done.2.blocks_ref = bf16[8,64,768]{2,1,0:T(8,128)(2,1)S(1)} async-done(((bf16[8,64,768]{2,1,0:T(8,128)(2,1)}), bf16[8,64,768]{2,1,0:T(8,128)(2,1)S(1)}, u32[]{:S(2)}, u32[]{:S(2)}) %all-to-all-start.2) | async-done | bytes 786464 | tf_op jit(solution)/shard_map/all_to_all | solution.py:665
  521.5 6.2 %reduce-scatter.11.cloned.1.call-done = bf16[64,2048]{1,0:T(8,128)(2,1)} async-done(((bf16[256,2048]{1,0:T(8,128)(2,1)}), bf16[64,2048]{1,0:T(8,128)(2,1)}) %reduce-scatter.11.cloned.1.call-update) | async-done | bytes 262160 | tf_op jit(solution)/shard_map/reduce_scatter | solution.py:662
  (405 shorter events, 135.0 us)
Async XLA Ops:
  7.2 34.9 %all-gather.7.cloned.1.call-start = ((), (), s32[]{:S(2)}) async-start(), calls=%async_computation.8 | async-start | bytes 1310720 | tf_op jit(solution)/shard_map/all_gather | solution.py:659
  12.3 17.8 %all-to-all-start = ((bf16[8,64,768]{2,1,0:T(8,128)(2,1)}), bf16[8,64,768]{2,1,0:T(8,128)(2,1)S(1)}, u32[]{:S(2)}, u32[]{:S(2)}) async-start(bf16[8,64,768]{2,1,0:T(8,128)(2,1)} %pick_columns.1), calls=%async_computation | async-start | bytes 1572864 | tf_op jit(solution)/shard_map/all_to_all | solution.py:665
  17.4 89.8 %all-gather.11.cloned.1.call-start = ((), (), s32[]{:S(2)}) async-start(), calls=%async_computation.14 | async-start | bytes 3932160 | tf_op jit(solution)/shard_map/all_gather | solution.py:659
  42.1 14.9 %collective-permute-start = (bf16[128,2048]{1,0:T(8,128)(2,1)S(1)}, bf16[128,2048]{1,0:T(8,128)(2,1)S(1)}, u32[]{:S(2)}, u32[]{:S(2)}) collective-permute-start(bf16[128,2048]{1,0:T(8,128)(2,1)S(1)} %bitcast.59), channel_id=1, source_target_pairs={{0,8},{4,12},{8,0},{12,4},{16,24},{20,28},{24,16},{28,20},{1,9},{5... | collective-permute-start | bytes 1572872 | tf_op jit(solution)/shard_map/ppermute | solution.py:593
  43.7 15.6 %collective-permute-start.1 = (bf16[128,2048]{1,0:T(8,128)(2,1)S(1)}, bf16[128,2048]{1,0:T(8,128)(2,1)S(1)}, u32[]{:S(2)}, u32[]{:S(2)}) collective-permute-start(bf16[128,2048]{1,0:T(8,128)(2,1)S(1)} %bitcast.60), channel_id=1, source_target_pairs={{0,16},{4,20},{8,24},{12,28},{16,0},{20,4},{24,8},{28,12},{1,17},{... | collective-permute-start | bytes 1572872 | tf_op jit(solution)/shard_map/ppermute | solution.py:593
  46.6 41.2 %all-to-all-start.1 = ((bf16[8,64,1408]{2,1,0:T(8,128)(2,1)}), bf16[8,64,1408]{2,1,0:T(8,128)(2,1)S(1)}, u32[]{:S(2)}, u32[]{:S(2)}) async-start(bf16[8,64,1408]{2,1,0:T(8,128)(2,1)} %pair_columns.1), calls=%async_computation.1 | async-start | bytes 2883584 | tf_op jit(solution)/shard_map/all_to_all | solution.py:665
  50.1 164.7 %all-gather.13.cloned.1.call-start = ((), (), s32[]{:S(2)}) async-start(), calls=%async_computation.15 | async-start | bytes 7208960 | tf_op jit(solution)/shard_map/all_gather | solution.py:659
  50.3 22.5 %collective-permute-start.13 = (bf16[8,448]{1,0:T(8,128)(2,1)S(1)}, bf16[8,448]{1,0:T(8,128)(2,1)S(1)}, u32[]{:S(2)}, u32[]{:S(2)}) collective-permute-start(bf16[8,448]{1,0:T(8,128)(2,1)S(1)} %pad_maximum_fusion.10), channel_id=1, source_target_pairs={{0,8},{4,12},{8,0},{12,4},{16,24},{20,28},{24,16},{28,20},{1,9},{5... | collective-permute-start | bytes 21512 | tf_op jit(solution)/shard_map/ppermute | solution.py:593
  57.8 20.5 %collective-permute-start.2 = (bf16[64,2048]{1,0:T(8,128)(2,1)}, bf16[64,2048]{1,0:T(8,128)(2,1)}, u32[]{:S(2)}, u32[]{:S(2)}) collective-permute-start(bf16[64,2048]{1,0:T(8,128)(2,1)} %slice.286), channel_id=1, source_target_pairs={{0,16},{4,20},{8,24},{12,28},{16,0},{20,4},{24,8},{28,12},{1,17},{... | collective-permute-start | bytes 786440 | tf_op jit(solution)/shard_map/ppermute | solution.py:593
  60.0 18.2 %collective-permute-start.3 = (bf16[64,2048]{1,0:T(8,128)(2,1)}, bf16[64,2048]{1,0:T(8,128)(2,1)}, u32[]{:S(2)}, u32[]{:S(2)}) collective-permute-start(bf16[64,2048]{1,0:T(8,128)(2,1)} %slice.287), channel_id=1, source_target_pairs={{0,8},{4,12},{8,0},{12,4},{16,24},{20,28},{24,16},{28,20},{1,9},{5... | collective-permute-start | bytes 786440 | tf_op jit(solution)/shard_map/ppermute | solution.py:593
  74.8 12.9 %collective-permute-start.4 = (bf16[128,2048]{1,0:T(8,128)(2,1)S(1)}, bf16[128,2048]{1,0:T(8,128)(2,1)S(1)}, u32[]{:S(2)}, u32[]{:S(2)}) collective-permute-start(bf16[128,2048]{1,0:T(8,128)(2,1)S(1)} %bitcast.61), channel_id=1, source_target_pairs={{0,4},{4,0},{8,12},{12,8},{16,20},{20,16},{24,28},{28,24},{1,5},{5... | collective-permute-start | bytes 1572872 | tf_op jit(solution)/shard_map/ppermute | solution.py:593
  75.6 12.1 %collective-permute-start.5 = (bf16[128,2048]{1,0:T(8,128)(2,1)S(1)}, bf16[128,2048]{1,0:T(8,128)(2,1)}, u32[]{:S(2)}, u32[]{:S(2)}) collective-permute-start(bf16[128,2048]{1,0:T(8,128)(2,1)S(1)} %collective-permute-done.refs_1_), channel_id=1, source_target_pairs={{0,4},{4,0},{8,12},{12,8},{16,20},{20,16},{24,28},{28,24},{1,5},{5... | collective-permute-start | bytes 1572872 | tf_op jit(solution)/shard_map/ppermute | solution.py:593
  78.3 9.5 %collective-permute-start.6 = (bf16[128,2048]{1,0:T(8,128)(2,1)S(1)}, bf16[128,2048]{1,0:T(8,128)(2,1)}, u32[]{:S(2)}, u32[]{:S(2)}) collective-permute-start(bf16[128,2048]{1,0:T(8,128)(2,1)S(1)} %collective-permute-done.1.refs_2_), channel_id=1, source_target_pairs={{0,4},{4,0},{8,12},{12,8},{16,20},{20,16},{24,28},{28,24},{1,5},{5... | collective-permute-start | bytes 1572872 | tf_op jit(solution)/shard_map/ppermute | solution.py:593
  78.3 9.5 %collective-permute-start.7 = (bf16[64,2048]{1,0:T(8,128)(2,1)}, bf16[64,2048]{1,0:T(8,128)(2,1)}, u32[]{:S(2)}, u32[]{:S(2)}) collective-permute-start(bf16[64,2048]{1,0:T(8,128)(2,1)} %collective-permute-done.2.refs_3_), channel_id=1, source_target_pairs={{0,4},{4,0},{8,12},{12,8},{16,20},{20,16},{24,28},{28,24},{1,5},{5... | collective-permute-start | bytes 786440 | tf_op jit(solution)/shard_map/ppermute | solution.py:593
  89.1 184.7 %all-gather.9.cloned.1.call-start = ((), (), s32[]{:S(2)}) async-start(), calls=%async_computation.9 | async-start | bytes 3604480 | tf_op jit(solution)/shard_map/all_gather | solution.py:659
  142.8 14.9 %collective-permute-start.17 = (bf16[128,2048]{1,0:T(8,128)(2,1)S(1)}, bf16[128,2048]{1,0:T(8,128)(2,1)S(1)}, u32[]{:S(2)}, u32[]{:S(2)}) collective-permute-start(bf16[128,2048]{1,0:T(8,128)(2,1)S(1)} %pad_maximum_fusion), channel_id=1, source_target_pairs={{0,8},{4,12},{8,0},{12,4},{16,24},{20,28},{24,16},{28,20},{1,9},{5... | collective-permute-start | bytes 1572872 | tf_op jit(solution)/shard_map/ppermute | solution.py:593
  144.3 14.9 %collective-permute-start.19 = (bf16[128,2048]{1,0:T(8,128)(2,1)S(1)}, bf16[128,2048]{1,0:T(8,128)(2,1)S(1)}, u32[]{:S(2)}, u32[]{:S(2)}) collective-permute-start(bf16[128,2048]{1,0:T(8,128)(2,1)S(1)} %pad_maximum_fusion.1), channel_id=1, source_target_pairs={{0,16},{4,20},{8,24},{12,28},{16,0},{20,4},{24,8},{28,12},{1,17},{... | collective-permute-start | bytes 1572872 | tf_op jit(solution)/shard_map/ppermute | solution.py:593
  145.3 192.5 %reduce-scatter.5.cloned.1.call-start = ((), (), s32[]{:S(2)}) async-start(), calls=%async_computation.10 | async-start | bytes 3604480 | tf_op jit(solution)/shard_map/reduce_scatter | solution.py:662
  145.6 23.3 %collective-permute-start.29 = (bf16[128,2048]{1,0:T(8,128)(2,1)S(1)}, bf16[128,2048]{1,0:T(8,128)(2,1)S(1)}, u32[]{:S(2)}, u32[]{:S(2)}) collective-permute-start(bf16[128,2048]{1,0:T(8,128)(2,1)S(1)} %copy-done.11), channel_id=1, source_target_pairs={{0,8},{4,12},{8,0},{12,4},{16,24},{20,28},{24,16},{28,20},{1,9},{5... | collective-permute-start | bytes 1572872 | tf_op jit(solution)/shard_map/ppermute | solution.py:593
  146.2 24.8 %collective-permute-start.30 = (bf16[128,2048]{1,0:T(8,128)(2,1)S(1)}, bf16[128,2048]{1,0:T(8,128)(2,1)S(1)}, u32[]{:S(2)}, u32[]{:S(2)}) collective-permute-start(bf16[128,2048]{1,0:T(8,128)(2,1)S(1)} %copy-done.11), channel_id=1, source_target_pairs={{0,16},{4,20},{8,24},{12,28},{16,0},{20,4},{24,8},{28,12},{1,17},{... | collective-permute-start | bytes 1572872 | tf_op jit(solution)/shard_map/ppermute | solution.py:593
  161.5 24.1 %collective-permute-start.20 = (bf16[128,2048]{1,0:T(8,128)(2,1)S(1)}, bf16[128,2048]{1,0:T(8,128)(2,1)S(1)}, u32[]{:S(2)}, u32[]{:S(2)}) collective-permute-start(bf16[128,2048]{1,0:T(8,128)(2,1)S(1)} %add_convert_fusion.refs_0_), channel_id=1, source_target_pairs={{0,8},{4,12},{8,0},{12,4},{16,24},{20,28},{24,16},{28,20},{1,9},{5... | collective-permute-start | bytes 1572872 | tf_op jit(solution)/shard_map/ppermute | solution.py:593
  168.9 16.8 %collective-permute-start.21 = (bf16[128,2048]{1,0:T(8,128)(2,1)S(1)}, bf16[128,2048]{1,0:T(8,128)(2,1)S(1)}, u32[]{:S(2)}, u32[]{:S(2)}) collective-permute-start(bf16[128,2048]{1,0:T(8,128)(2,1)S(1)} %add_convert_fusion.refs_0_), channel_id=1, source_target_pairs={{0,16},{4,20},{8,24},{12,28},{16,0},{20,4},{24,8},{28,12},{1,17},{... | collective-permute-start | bytes 1572872 | tf_op jit(solution)/shard_map/ppermute | solution.py:593
  169.6 15.6 %collective-permute-start.31 = (bf16[64,2048]{1,0:T(8,128)(2,1)S(1)}, bf16[64,2048]{1,0:T(8,128)(2,1)S(1)}, u32[]{:S(2)}, u32[]{:S(2)}) collective-permute-start(bf16[64,2048]{1,0:T(8,128)(2,1)S(1)} %slice.297), channel_id=1, source_target_pairs={{0,16},{4,20},{8,24},{12,28},{16,0},{20,4},{24,8},{28,12},{1,17},{... | collective-permute-start | bytes 786440 | tf_op jit(solution)/shard_map/ppermute | solution.py:593
  171.1 14.1 %collective-permute-start.32 = (bf16[64,2048]{1,0:T(8,128)(2,1)S(1)}, bf16[64,2048]{1,0:T(8,128)(2,1)S(1)}, u32[]{:S(2)}, u32[]{:S(2)}) collective-permute-start(bf16[64,2048]{1,0:T(8,128)(2,1)S(1)} %slice.298), channel_id=1, source_target_pairs={{0,8},{4,12},{8,0},{12,4},{16,24},{20,28},{24,16},{28,20},{1,9},{5... | collective-permute-start | bytes 786440 | tf_op jit(solution)/shard_map/ppermute | solution.py:593
  172.6 13.6 %collective-permute-start.33 = (bf16[128,2048]{1,0:T(8,128)(2,1)S(1)}, bf16[128,2048]{1,0:T(8,128)(2,1)S(1)}, u32[]{:S(2)}, u32[]{:S(2)}) collective-permute-start(bf16[128,2048]{1,0:T(8,128)(2,1)S(1)} %copy-done.11), channel_id=1, source_target_pairs={{0,4},{4,0},{8,12},{12,8},{16,20},{20,16},{24,28},{28,24},{1,5},{5... | collective-permute-start | bytes 1572872 | tf_op jit(solution)/shard_map/ppermute | solution.py:593
  186.2 10.8 %collective-permute-start.24 = (bf16[128,2048]{1,0:T(8,128)(2,1)S(1)}, bf16[128,2048]{1,0:T(8,128)(2,1)S(1)}, u32[]{:S(2)}, u32[]{:S(2)}) collective-permute-start(bf16[128,2048]{1,0:T(8,128)(2,1)S(1)} %add_convert_fusion.refs_0_), channel_id=1, source_target_pairs={{0,4},{4,0},{8,12},{12,8},{16,20},{20,16},{24,28},{28,24},{1,5},{5... | collective-permute-start | bytes 1572872 | tf_op jit(solution)/shard_map/ppermute | solution.py:593
  190.1 9.9 %collective-permute-start.26 = (bf16[128,2048]{1,0:T(8,128)(2,1)S(1)}, bf16[128,2048]{1,0:T(8,128)(2,1)}, u32[]{:S(2)}, u32[]{:S(2)}) collective-permute-start(bf16[128,2048]{1,0:T(8,128)(2,1)S(1)} %collective-permute-done.21.refs_2_), channel_id=1, source_target_pairs={{0,4},{4,0},{8,12},{12,8},{16,20},{20,16},{24,28},{28,24},{1,5},{5... | collective-permute-start | bytes 1572872 | tf_op jit(solution)/shard_map/ppermute | solution.py:593
  237.8 203.8 %reduce-scatter.9.cloned.1.call-start = ((), (), s32[]{:S(2)}) async-start(), calls=%async_computation.12 | async-start | bytes 7208960 | tf_op jit(solution)/shard_map/reduce_scatter | solution.py:662
  304.3 193.9 %reduce-scatter.7.cloned.1.call-start = ((), (), s32[]{:S(2)}) async-start(), calls=%async_computation.11 | async-start | bytes 3932160 | tf_op jit(solution)/shard_map/reduce_scatter | solution.py:662
  322.4 13.0 %collective-permute-start.40 = (bf16[128,2048]{1,0:T(8,128)(2,1)S(1)}, bf16[128,2048]{1,0:T(8,128)(2,1)S(1)}, u32[]{:S(2)}, u32[]{:S(2)}) collective-permute-start(bf16[128,2048]{1,0:T(8,128)(2,1)S(1)} %pad_maximum_fusion.2), channel_id=1, source_target_pairs={{0,8},{4,12},{8,0},{12,4},{16,24},{20,28},{24,16},{28,20},{1,9},{5... | collective-permute-start | bytes 1572872 | tf_op jit(solution)/shard_map/ppermute | solution.py:593
  323.9 12.7 %collective-permute-start.42 = (bf16[128,2048]{1,0:T(8,128)(2,1)S(1)}, bf16[128,2048]{1,0:T(8,128)(2,1)S(1)}, u32[]{:S(2)}, u32[]{:S(2)}) collective-permute-start(bf16[128,2048]{1,0:T(8,128)(2,1)S(1)} %pad_maximum_fusion.3), channel_id=1, source_target_pairs={{0,16},{4,20},{8,24},{12,28},{16,0},{20,4},{24,8},{28,12},{1,17},{... | collective-permute-start | bytes 1572872 | tf_op jit(solution)/shard_map/ppermute | solution.py:593
  342.8 11.4 %collective-permute-start.43 = (bf16[128,2048]{1,0:T(8,128)(2,1)S(1)}, bf16[128,2048]{1,0:T(8,128)(2,1)S(1)}, u32[]{:S(2)}, u32[]{:S(2)}) collective-permute-start(bf16[128,2048]{1,0:T(8,128)(2,1)S(1)} %get-tuple-element.133.refs_0_), channel_id=1, source_target_pairs={{0,8},{4,12},{8,0},{12,4},{16,24},{20,28},{24,16},{28,20},{1,9},{5... | collective-permute-start | bytes 1572872 | tf_op jit(solution)/shard_map/ppermute | solution.py:593
  343.4 11.9 %collective-permute-start.44 = (bf16[128,2048]{1,0:T(8,128)(2,1)S(1)}, bf16[128,2048]{1,0:T(8,128)(2,1)S(1)}, u32[]{:S(2)}, u32[]{:S(2)}) collective-permute-start(bf16[128,2048]{1,0:T(8,128)(2,1)S(1)} %get-tuple-element.133.refs_0_), channel_id=1, source_target_pairs={{0,16},{4,20},{8,24},{12,28},{16,0},{20,4},{24,8},{28,12},{1,17},{... | collective-permute-start | bytes 1572872 | tf_op jit(solution)/shard_map/ppermute | solution.py:593
  343.7 19.1 %collective-permute-start.47 = (bf16[128,2048]{1,0:T(8,128)(2,1)S(1)}, bf16[128,2048]{1,0:T(8,128)(2,1)S(1)}, u32[]{:S(2)}, u32[]{:S(2)}) collective-permute-start(bf16[128,2048]{1,0:T(8,128)(2,1)S(1)} %get-tuple-element.133.refs_0_), channel_id=1, source_target_pairs={{0,4},{4,0},{8,12},{12,8},{16,20},{20,16},{24,28},{28,24},{1,5},{5... | collective-permute-start | bytes 1572872 | tf_op jit(solution)/shard_map/ppermute | solution.py:593
  395.3 22.4 %collective-permute-start.57 = (bf16[512,2048]{1,0:T(8,128)(2,1)}, bf16[512,2048]{1,0:T(8,128)(2,1)}, u32[]{:S(2)}, u32[]{:S(2)}) collective-permute-start(bf16[512,2048]{1,0:T(8,128)(2,1)} %convolution_convert_fusion.4.refs_1_), channel_id=1, source_target_pairs={{0,4},{4,0},{8,12},{12,8},{16,20},{20,16},{24,28},{28,24},{1,5},{5... | collective-permute-start | bytes 6291464 | tf_op jit(solution)/shard_map/ppermute | solution.py:593
  400.7 23.2 %collective-permute-start.52 = (bf16[512,2048]{1,0:T(8,128)(2,1)}, bf16[512,2048]{1,0:T(8,128)(2,1)}, u32[]{:S(2)}, u32[]{:S(2)}) collective-permute-start(bf16[512,2048]{1,0:T(8,128)(2,1)} %convolution_convert_fusion.5), channel_id=1, source_target_pairs={{0,4},{4,0},{8,12},{12,8},{16,20},{20,16},{24,28},{28,24},{1,5},{5... | collective-permute-start | bytes 6291464 | tf_op jit(solution)/shard_map/ppermute | solution.py:593
  429.0 9.2 %collective-permute-start.55 = (bf16[64,2048]{1,0:T(8,128)(2,1)S(1)}, bf16[64,2048]{1,0:T(8,128)(2,1)S(1)}, u32[]{:S(2)}, u32[]{:S(2)}) collective-permute-start(bf16[64,2048]{1,0:T(8,128)(2,1)S(1)} %get-tuple-element.153), channel_id=1, source_target_pairs={{0,8},{4,12},{8,0},{12,4},{16,24},{20,28},{24,16},{28,20},{1,9},{5... | collective-permute-start | bytes 786440 | tf_op jit(solution)/shard_map/ppermute | solution.py:593
  431.2 18.3 %collective-permute-start.59 = (bf16[128,2048]{1,0:T(8,128)(2,1)}, bf16[128,2048]{1,0:T(8,128)(2,1)S(1)}, u32[]{:S(2)}, u32[]{:S(2)}) collective-permute-start(bf16[128,2048]{1,0:T(8,128)(2,1)} %pad_maximum_fusion.6), channel_id=1, source_target_pairs={{0,8},{4,12},{8,0},{12,4},{16,24},{20,28},{24,16},{28,20},{1,9},{5... | collective-permute-start | bytes 1572872 | tf_op jit(solution)/shard_map/ppermute | solution.py:593
  434.3 15.2 %collective-permute-start.61 = (bf16[128,2048]{1,0:T(8,128)(2,1)}, bf16[128,2048]{1,0:T(8,128)(2,1)}, u32[]{:S(2)}, u32[]{:S(2)}) collective-permute-start(bf16[128,2048]{1,0:T(8,128)(2,1)} %pad_maximum_fusion.7), channel_id=1, source_target_pairs={{0,16},{4,20},{8,24},{12,28},{16,0},{20,4},{24,8},{28,12},{1,17},{... | collective-permute-start | bytes 1572872 | tf_op jit(solution)/shard_map/ppermute | solution.py:593
  439.2 21.6 %collective-permute-start.54 = (bf16[128,2048]{1,0:T(8,128)(2,1)}, bf16[128,2048]{1,0:T(8,128)(2,1)}, u32[]{:S(2)}, u32[]{:S(2)}) collective-permute-start(bf16[128,2048]{1,0:T(8,128)(2,1)} %pad_maximum_fusion.4), channel_id=1, source_target_pairs={{0,8},{4,12},{8,0},{12,4},{16,24},{20,28},{24,16},{28,20},{1,9},{5... | collective-permute-start | bytes 1572872 | tf_op jit(solution)/shard_map/ppermute | solution.py:593
  440.1 20.7 %collective-permute-start.56 = (bf16[128,2048]{1,0:T(8,128)(2,1)}, bf16[128,2048]{1,0:T(8,128)(2,1)}, u32[]{:S(2)}, u32[]{:S(2)}) collective-permute-start(bf16[128,2048]{1,0:T(8,128)(2,1)} %pad_maximum_fusion.5), channel_id=1, source_target_pairs={{0,16},{4,20},{8,24},{12,28},{16,0},{20,4},{24,8},{28,12},{1,17},{... | collective-permute-start | bytes 1572872 | tf_op jit(solution)/shard_map/ppermute | solution.py:593
  441.6 34.5 %all-to-all-start.3 = ((bf16[8,64,1408]{2,1,0:T(8,128)(2,1)}), bf16[8,64,1408]{2,1,0:T(8,128)(2,1)S(1)}, u32[]{:S(2)}, u32[]{:S(2)}) async-start(bf16[8,64,1408]{2,1,0:T(8,128)(2,1)} %bitcast.76), calls=%async_computation.6 | async-start | bytes 2883584 | tf_op jit(solution)/shard_map/all_to_all | solution.py:665
  445.3 82.4 %reduce-scatter.11.cloned.1.call-start = ((), (), s32[]{:S(2)}) async-start(), calls=%async_computation.13 | async-start | bytes 1310720 | tf_op jit(solution)/shard_map/reduce_scatter | solution.py:662
  454.7 16.5 %collective-permute-start.62 = (f32[16,448]{1,0:T(8,128)S(1)}, f32[16,448]{1,0:T(8,128)S(1)}, u32[]{:S(2)}, u32[]{:S(2)}) collective-permute-start(f32[16,448]{1,0:T(8,128)S(1)} %slice_select_fusion), channel_id=1, source_target_pairs={{0,16},{4,20},{8,24},{12,28},{16,0},{20,4},{24,8},{28,12},{1,17},{... | collective-permute-start | bytes 86024 | tf_op jit(solution)/shard_map/ppermute | solution.py:593
  471.3 27.0 %collective-permute-start.63 = (f32[8,448]{1,0:T(8,128)S(1)}, f32[8,448]{1,0:T(8,128)S(1)}, u32[]{:S(2)}, u32[]{:S(2)}) collective-permute-start(f32[8,448]{1,0:T(8,128)S(1)} %slice_select_fusion.1), channel_id=1, source_target_pairs={{0,8},{4,12},{8,0},{12,4},{16,24},{20,28},{24,16},{28,20},{1,9},{5... | collective-permute-start | bytes 43016 | tf_op jit(solution)/shard_map/ppermute | solution.py:593
  499.6 10.9 %collective-permute-start.65 = (f32[448]{0:T(512)S(1)}, f32[448]{0:T(512)S(1)}, u32[]{:S(2)}, u32[]{:S(2)}) collective-permute-start(f32[448]{0:T(512)S(1)} %bitcast.83), channel_id=1, source_target_pairs={{0,1},{1,0},{2,3},{3,2},{4,5},{5,4},{6,7},{7,6},{8,9},{9,8},{10,11... | collective-permute-start | bytes 5384 | tf_op jit(solution)/shard_map/ppermute | solution.py:712
  500.6 9.9 %collective-permute-start.66 = (f32[448]{0:T(512)S(1)}, f32[448]{0:T(512)S(1)}, u32[]{:S(2)}, u32[]{:S(2)}) collective-permute-start(f32[448]{0:T(512)S(1)} %bitcast.82), channel_id=1, source_target_pairs={{0,2},{1,3},{2,0},{3,1},{4,6},{5,7},{6,4},{7,5},{8,10},{9,11},{10,... | collective-permute-start | bytes 5384 | tf_op jit(solution)/shard_map/ppermute | solution.py:712
  504.0 16.2 %all-to-all-start.2 = ((bf16[8,64,768]{2,1,0:T(8,128)(2,1)}), bf16[8,64,768]{2,1,0:T(8,128)(2,1)S(1)}, u32[]{:S(2)}, u32[]{:S(2)}) async-start(bf16[8,64,768]{2,1,0:T(8,128)(2,1)} %bitcast.75), calls=%async_computation.4 | async-start | bytes 1572864 | tf_op jit(solution)/shard_map/all_to_all | solution.py:665
  (104 other events, 1101.4 us)
Sparse Core Ops, SparseCore 0:
  11.4 30.6 all-gather.6
  44.2 62.9 all-gather.10
  109.4 105.3 all-gather.12
  216.2 57.4 all-gather.8
  275.9 54.8 reduce-scatter.4
  333.0 102.0 reduce-scatter.8
  437.4 60.7 reduce-scatter.6
  500.5 27.1 reduce-scatter.10

commit v5 on v4

--- a/solution.py
+++ b/solution.py
@@ -783,14 +783,11 @@
         return [(value, at, start) for value, (_, at, start) in zip(values, pieces)]
 
     vectors = [v.astype(F4)[None] for v in (first_gain, first_shift, bias_here)]
-    found, vectors, (ff_blocks, cotangent_low) = let(
-        [arrays(first_pieces), vectors, [ff_blocks, cotangent_low]]
-    )
-    found, vectors, (cotangent_low,) = let([found, vectors, [cotangent_low]], qkv_line)
+    found, vectors, (ff_blocks,) = let([arrays(first_pieces), vectors, [ff_blocks]])
+    found, vectors = let([found, vectors], qkv_line)
     first_pieces = renewed(first_pieces, found)
     ff_line = links.line_gather(ff_blocks[None])
     down_here = links.line_gather(w_down)
-    cotangent_pieces = arrays(links.plane_gather(cotangent_low))
     normed_rows, queries, keys, values, mixed, mixed_rel, log_totals = attend(
         place,
         first_pieces,
@@ -802,6 +799,7 @@
         order,
         tok_rows,
     )
+    cotangent_pieces = arrays(links.plane_gather(after(cotangent_low, qkv_line)))
     out_send = dot(mixed_rel[half:], out_here, BF)
     out_keep = dot(mixed_rel[:half], out_here)
     middle = inputs + links.plane_reduce(out_keep, out_send)

time: 541 us -> 539 us (level)
  no operation moved by 1% of the time
where the time goes in v5:
time: 539 us; the launch traced here: 535 us
  waiting for transfers between devices  241 us (45%)
  Pallas kernels  90.5 us (17%)
  starting transfers between devices  80.5 us (15%)
  matrix products  39 us (7%)
  other arithmetic  34.6 us (6%)
  local copies, waits for them, and re-layouts  33.2 us (6%)
  between operations  15.6 us (3%)
    ppermute x62, waiting for transfers between devices, flip(): return lax.ppermute(values, 'seq', [(i, i ^ bit) for i in range(self.ns)])  126 us
    all_gather x4, waiting for transfers between devices, line_gather(): return lax.all_gather(own, 'fsdp', axis=0, tiled=True)  73.4 us
    ppermute x62, starting transfers between devices, flip(): return lax.ppermute(values, 'seq', [(i, i ^ bit) for i in range(self.ns)])  54.3 us
    reduce_scatter x4, waiting for transfers between devices, line_reduce(): return lax.psum_scatter(terms, 'fsdp', scatter_dimension=0, tiled=True)  28.3 us
    pallas_call x1, Pallas kernels, attend_back(): pl.pallas_call(kernel, out_shape=[jax.ShapeDtypeStruct((length, width), B...  25.9 us
    dot_general x3, matrix products, dot_tn(): lax.dot_general(a, b, (((0,), (0,)), ((), ())), preferred_element_type=F4)  20 us
    pallas_call x1, Pallas kernels, attend(): pl.pallas_call(kernel, out_shape=[jax.ShapeDtypeStruct((length, width), B...  18.9 us
    pallas_call x1, Pallas kernels, feed_back(): pl.pallas_call(kernel, out_shape=[jax.ShapeDtypeStruct((length, both), BF...  18.7 us
  transfers between devices with their start and end apart: 80, of which 42 were waited for; matrix products, arithmetic and copies ran while one was open for 18% of the time, Pallas kernels for 17%

profile of v5, /device:TPU:0, one launch (start us, length us, event | category | flops | bytes accessed | tf_op | source)
XLA Modules:
  0.0 534.8 jit_solution(13526223199857165269)
XLA Ops:
  11.4 5.2 all-to-all-start
  18.4 2.6 collective-permute-start.10
  22.8 3.5 collective-permute-done.11
  29.2 11.2 %all-gather.7.cloned.1.call-done.refs_2_.refs_10_ = bf16[256,2048]{1,0:T(8,128)(2,1)} async-done(((bf16[64,2048]{1,0:T(8,128)(2,1)}), bf16[256,2048]{1,0:T(8,128)(2,1)}) %all-gather.7.cloned.1.call-update) | async-done | bytes 1048592 | tf_op jit(solution)/shard_map/all_gather | solution.py:659
  44.8 3.6 all-to-all-start.1
  50.4 4.8 collective-permute-done.refs_1_
  58.3 3.3 collective-permute-start.3
  61.6 9.4 %collective-permute-done.13 = bf16[8,448]{1,0:T(8,128)(2,1)S(1)} collective-permute-done((bf16[8,448]{1,0:T(8,128)(2,1)S(1)}, bf16[8,448]{1,0:T(8,128)(2,1)S(1)}, u32[]{:S(2)}, u32[]{:S(2)}) %collective-permute-start.13) | collective-permute-done | bytes 7200 | tf_op jit(solution)/shard_map/ppermute | solution.py:593
  93.6 11.9 %all-gather.11.cloned.1.call-done = bf16[32,64,768]{2,1,0:T(8,128)(2,1)} async-done(((bf16[8,64,768]{2,1,0:T(8,128)(2,1)}), bf16[32,64,768]{2,1,0:T(8,128)(2,1)}) %all-gather.11.cloned.1.call-update) | async-done | bytes 3145744 | tf_op jit(solution)/shard_map/all_gather | solution.py:659
  105.5 18.9 %attend.1 = (bf16[1024,2048]{1,0:T(8,128)(2,1)}, bf16[1024,256]{1,0:T(8,128)(2,1)}, bf16[1024,256]{1,0:T(8,128)(2,1)}, bf16[1024,256]{1,0:T(8,128)(2,1)}, bf16[1...) custom-call(s32[2]{0:T(128)} %pad_add_fusion.place_ref, ...), custom_call_target="tpu_custom_call" | custom-call | flops 16999999488 | tf_op jit(solution)/shard_map/attend/pallas_call | solution.py:191
  126.2 4.1 collective-permute-done.15
  134.2 5.4 %collective-permute-done.16 = bf16[64,2048]{1,0:T(8,128)(2,1)S(1)} collective-permute-done((bf16[64,2048]{1,0:T(8,128)(2,1)S(1)}, bf16[64,2048]{1,0:T(8,128)(2,1)S(1)}, u32[]{:S(2)}, u32[]{:S(2)}) %collective-permute-start.16) | collective-permute-done | bytes 262176 | tf_op jit(solution)/shard_map/ppermute | solution.py:593
  146.7 9.2 %collective-permute-done.17 = bf16[128,2048]{1,0:T(8,128)(2,1)S(1)} collective-permute-done((bf16[128,2048]{1,0:T(8,128)(2,1)S(1)}, bf16[128,2048]{1,0:T(8,128)(2,1)S(1)}, u32[]{:S(2)}, u32[]{:S(2)}) %collective-permute-start.17) | collective-permute-done | bytes 524320 | tf_op jit(solution)/shard_map/ppermute | solution.py:593
  160.6 6.5 %collective-permute-done.29.refs_11_ = bf16[128,2048]{1,0:T(8,128)(2,1)S(1)} collective-permute-done((bf16[128,2048]{1,0:T(8,128)(2,1)}, bf16[128,2048]{1,0:T(8,128)(2,1)S(1)}, u32[]{:S(2)}, u32[]{:S(2)}) %collective-permute-start.29) | collective-permute-done | bytes 524320 | tf_op jit(solution)/shard_map/ppermute | solution.py:593
  170.8 12.5 %collective-permute-done.31.refs_13_ = bf16[64,2048]{1,0:T(8,128)(2,1)S(1)} collective-permute-done((bf16[64,2048]{1,0:T(8,128)(2,1)S(1)}, bf16[64,2048]{1,0:T(8,128)(2,1)S(1)}, u32[]{:S(2)}, u32[]{:S(2)}) %collective-permute-start.31) | collective-permute-done | bytes 262176 | tf_op jit(solution)/shard_map/ppermute | solution.py:593
  188.8 5.9 %collective-permute-done.22.refs_3_ = bf16[64,2048]{1,0:T(8,128)(2,1)S(1)} collective-permute-done((bf16[64,2048]{1,0:T(8,128)(2,1)S(1)}, bf16[64,2048]{1,0:T(8,128)(2,1)S(1)}, u32[]{:S(2)}, u32[]{:S(2)}) %collective-permute-start.22) | collective-permute-done | bytes 262176 | tf_op jit(solution)/shard_map/ppermute | solution.py:593
  198.2 14.8 %all-gather.13.cloned.1.call-done = bf16[32,64,1408]{2,1,0:T(8,128)(2,1)} async-done(((bf16[8,64,1408]{2,1,0:T(8,128)(2,1)}), bf16[32,64,1408]{2,1,0:T(8,128)(2,1)}) %all-gather.13.cloned.1.call-update) | async-done | bytes 5767184 | tf_op jit(solution)/shard_map/all_gather | solution.py:659
  213.0 15.5 %feed.1 = (bf16[1024,2048]{1,0:T(8,128)(2,1)}, bf16[1024,2048]{1,0:T(8,128)(2,1)}, bf16[1024,704]{1,0:T(8,128)(2,1)}, f32[1024,1408]{1,0:T(8,128)}) custom-call(bf16[128,2048]{1,0:T(8,128)(2,1)} %copy-done.25, bf16[128,2048]{1,0:T(8,128)(2,1)} %copy-done.33, bf16[128,2048]{1,0:T(8,128)(2,1)} %copy-done.34, bf16[64,2048]{1,0:T(8,128)(2,1)} %copy-done.65, ...), custom_call_target="tpu_custom_call" | custom-call | flops 16999999488 | tf_op jit(solution)/shard_map/feed/pallas_call | solution.py:401
  228.5 7.4 %convolution_convert_fusion.2.refs_2_ = bf16[704,2048]{1,0:T(8,128)(2,1)} fusion(bf16[1024,704]{1,0:T(8,128)(2,1)} %get-tuple-element.97.refs_0_, bf16[1024,2048]{1,0:T(8,128)(2,1)} %get-tuple-element.98.refs_0_), kind=kOutput, calls=%fused_computation.7 | convolution fusion | flops 2954231808 | bytes 8519680 | tf_op jit(solution)/shard_map/dot_general | solution.py:27
  236.5 35.5 %all-gather.9.cloned.1.call-done.down_ref = bf16[704,2048]{1,0:T(8,128)(2,1)} async-done(((bf16[176,2048]{1,0:T(8,128)(2,1)}), bf16[704,2048]{1,0:T(8,128)(2,1)}) %all-gather.9.cloned.1.call-update) | async-done | bytes 2883600 | tf_op jit(solution)/shard_map/all_gather | solution.py:659
  272.0 18.7 %feed_back.1 = (bf16[1024,1408]{1,0:T(8,128)(2,1)}, bf16[512,2048]{1,0:T(8,128)(2,1)}, f32[512,2048]{1,0:T(8,128)}) custom-call(bf16[1024,2048]{1,0:T(8,128)(2,1)} %get-tuple-element.100.g_ref, f32[1024,1408]{1,0:T(8,128)} %get-tuple-element.101.both_ref, bf16[4,8,64,1408]{3,2,1,0:T(8,128)(2,1)} %bitcast.88, ...), custom_call_target="tpu_custom_call" | custom-call | flops 16999999488 | tf_op jit(solution)/shard_map/feed_back/pallas_call | solution.py:458
  290.7 8.8 %convolution_convert_fusion = bf16[2048,1408]{1,0:T(8,128)(2,1)S(1)} fusion(bf16[1024,2048]{1,0:T(8,128)(2,1)S(1)} %copy-done.71, bf16[1024,1408]{1,0:T(8,128)(2,1)} %get-tuple-element.106), kind=kOutput, calls=%fused_computation | convolution fusion | flops 5908463616 | bytes 12845056 | tf_op jit(solution)/shard_map/dot_general | solution.py:27
  299.5 2.9 copy.94
  302.6 4.4 collective-permute-done.38
  307.0 3.7 fusion.41
  313.8 5.4 %collective-permute-done.39 = bf16[64,2048]{1,0:T(8,128)(2,1)S(1)} collective-permute-done((bf16[64,2048]{1,0:T(8,128)(2,1)S(1)}, bf16[64,2048]{1,0:T(8,128)(2,1)S(1)}, u32[]{:S(2)}, u32[]{:S(2)}) %collective-permute-start.39) | collective-permute-done | bytes 262176 | tf_op jit(solution)/shard_map/ppermute | solution.py:593
  322.8 10.8 %collective-permute-done.40 = bf16[128,2048]{1,0:T(8,128)(2,1)S(1)} collective-permute-done((bf16[128,2048]{1,0:T(8,128)(2,1)S(1)}, bf16[128,2048]{1,0:T(8,128)(2,1)S(1)}, u32[]{:S(2)}, u32[]{:S(2)}) %collective-permute-start.40) | collective-permute-done | bytes 524320 | tf_op jit(solution)/shard_map/ppermute | solution.py:593
  338.0 3.0 fusion.40
  341.8 10.5 %collective-permute-done.43.refs_1_ = bf16[128,2048]{1,0:T(8,128)(2,1)S(1)} collective-permute-done((bf16[128,2048]{1,0:T(8,128)(2,1)S(1)}, bf16[128,2048]{1,0:T(8,128)(2,1)S(1)}, u32[]{:S(2)}, u32[]{:S(2)}) %collective-permute-start.43) | collective-permute-done | bytes 524320 | tf_op jit(solution)/shard_map/ppermute | solution.py:593
  363.2 25.9 %attend_back.1 = (bf16[1024,2048]{1,0:T(8,128)(2,1)}, bf16[1024,768]{1,0:T(8,128)(2,1)}, bf16[1024,768]{1,0:T(8,128)(2,1)}, f32[1,768]{1,0:T(1,128)}) custom-call(s32[2]{0:T(128)} %pad_add_fusion.place_ref, bf16[128,2048]{1,0:T(8,128)(2,1)} %copy-done.26, bf16[128,2048]{1,0:T(8,128)(2,1)} %copy-done.29, bf16[128,2048]{1,0:T(8,128)(2,1)} %copy-done.31, ...), custom_call_target="tpu_custom_call" | custom-call | flops 25999998976 | tf_op jit(solution)/shard_map/attend_back/pallas_call | solution.py:312
  389.2 4.3 convolution_convert_fusion.4.refs_1_
  393.5 5.3 convolution_convert_fusion.5
  399.2 3.7 convolution_convert_fusion.1
  409.6 6.1 %outer_rows.1.refs_0_ = bf16[256,2048]{1,0:T(8,128)(2,1)} custom-call(bf16[1024,256]{1,0:T(8,128)(2,1)} %get-tuple-element.95.left_ref, bf16[128,2048]{1,0:T(8,128)(2,1)} %copy-done.26, bf16[128,2048]{1,0:T(8,128)(2,1)} %copy-done.29, bf16[128,2048]{1,0:T(8,128)(2,1)} %copy-done.31, bf16[64,2048]{1,0:T(8,128)(2,1)} %copy-done.57, ...), custom_call_target="tpu_custom_call" | custom-call | flops 4000000000 | tf_op jit(solution)/shard_map/outer_rows/pallas_call | solution.py:352
  415.8 3.6 fusion.50
  422.0 3.4 fusion.49
  439.8 3.6 all-to-all-start.3
  443.7 3.9 collective-permute-done.59
  447.6 3.5 fusion.10
  454.6 4.4 collective-permute-done.54
  459.0 2.6 fusion.22
  461.5 7.8 %collective-permute-done.62 = f32[16,448]{1,0:T(8,128)S(1)} collective-permute-done((f32[16,448]{1,0:T(8,128)S(1)}, f32[16,448]{1,0:T(8,128)S(1)}, u32[]{:S(2)}, u32[]{:S(2)}) %collective-permute-start.62) | collective-permute-done | bytes 28704 | tf_op jit(solution)/shard_map/ppermute | solution.py:593
  469.4 5.0 collective-permute-start.63
  474.3 22.1 %reduce-scatter.7.cloned.1.call-done.refs_1_ = bf16[1,8,64,768]{3,2,1,0:T(8,128)(2,1)} async-done(((bf16[4,8,64,768]{3,2,1,0:T(8,128)(2,1)}), bf16[1,8,64,768]{3,2,1,0:T(8,128)(2,1)}) %reduce-scatter.7.cloned.1.call-update) | async-done | bytes 786448 | tf_op jit(solution)/shard_map/reduce_scatter | solution.py:662
  502.2 3.7 all-to-all-start.2
  505.9 2.8 fusion.23
  511.8 6.7 %all-to-all-done.2.blocks_ref = bf16[8,64,768]{2,1,0:T(8,128)(2,1)S(1)} async-done(((bf16[8,64,768]{2,1,0:T(8,128)(2,1)}), bf16[8,64,768]{2,1,0:T(8,128)(2,1)S(1)}, u32[]{:S(2)}, u32[]{:S(2)}) %all-to-all-start.2) | async-done | bytes 786464 | tf_op jit(solution)/shard_map/all_to_all | solution.py:665
  519.7 6.2 %reduce-scatter.11.cloned.1.call-done = bf16[64,2048]{1,0:T(8,128)(2,1)} async-done(((bf16[256,2048]{1,0:T(8,128)(2,1)}), bf16[64,2048]{1,0:T(8,128)(2,1)}) %reduce-scatter.11.cloned.1.call-update) | async-done | bytes 262160 | tf_op jit(solution)/shard_map/reduce_scatter | solution.py:662
  (406 shorter events, 135.2 us)
Async XLA Ops:
  7.2 33.1 %all-gather.7.cloned.1.call-start = ((), (), s32[]{:S(2)}) async-start(), calls=%async_computation.8 | async-start | bytes 1310720 | tf_op jit(solution)/shard_map/all_gather | solution.py:659
  11.4 17.8 %all-to-all-start = ((bf16[8,64,768]{2,1,0:T(8,128)(2,1)}), bf16[8,64,768]{2,1,0:T(8,128)(2,1)S(1)}, u32[]{:S(2)}, u32[]{:S(2)}) async-start(bf16[8,64,768]{2,1,0:T(8,128)(2,1)} %pick_columns.1), calls=%async_computation | async-start | bytes 1572864 | tf_op jit(solution)/shard_map/all_to_all | solution.py:665
  16.6 88.9 %all-gather.11.cloned.1.call-start = ((), (), s32[]{:S(2)}) async-start(), calls=%async_computation.14 | async-start | bytes 3932160 | tf_op jit(solution)/shard_map/all_gather | solution.py:659
  40.4 14.9 %collective-permute-start = (bf16[128,2048]{1,0:T(8,128)(2,1)S(1)}, bf16[128,2048]{1,0:T(8,128)(2,1)S(1)}, u32[]{:S(2)}, u32[]{:S(2)}) collective-permute-start(bf16[128,2048]{1,0:T(8,128)(2,1)S(1)} %bitcast.65), channel_id=1, source_target_pairs={{0,8},{4,12},{8,0},{12,4},{16,24},{20,28},{24,16},{28,20},{1,9},{5... | collective-permute-start | bytes 1572872 | tf_op jit(solution)/shard_map/ppermute | solution.py:593
  41.9 15.6 %collective-permute-start.1 = (bf16[128,2048]{1,0:T(8,128)(2,1)S(1)}, bf16[128,2048]{1,0:T(8,128)(2,1)S(1)}, u32[]{:S(2)}, u32[]{:S(2)}) collective-permute-start(bf16[128,2048]{1,0:T(8,128)(2,1)S(1)} %bitcast.66), channel_id=1, source_target_pairs={{0,16},{4,20},{8,24},{12,28},{16,0},{20,4},{24,8},{28,12},{1,17},{... | collective-permute-start | bytes 1572872 | tf_op jit(solution)/shard_map/ppermute | solution.py:593
  44.8 41.2 %all-to-all-start.1 = ((bf16[8,64,1408]{2,1,0:T(8,128)(2,1)}), bf16[8,64,1408]{2,1,0:T(8,128)(2,1)S(1)}, u32[]{:S(2)}, u32[]{:S(2)}) async-start(bf16[8,64,1408]{2,1,0:T(8,128)(2,1)} %pair_columns.1), calls=%async_computation.1 | async-start | bytes 2883584 | tf_op jit(solution)/shard_map/all_to_all | solution.py:665
  48.4 164.7 %all-gather.13.cloned.1.call-start = ((), (), s32[]{:S(2)}) async-start(), calls=%async_computation.15 | async-start | bytes 7208960 | tf_op jit(solution)/shard_map/all_gather | solution.py:659
  48.5 22.5 %collective-permute-start.13 = (bf16[8,448]{1,0:T(8,128)(2,1)S(1)}, bf16[8,448]{1,0:T(8,128)(2,1)S(1)}, u32[]{:S(2)}, u32[]{:S(2)}) collective-permute-start(bf16[8,448]{1,0:T(8,128)(2,1)S(1)} %pad_maximum_fusion.10), channel_id=1, source_target_pairs={{0,8},{4,12},{8,0},{12,4},{16,24},{20,28},{24,16},{28,20},{1,9},{5... | collective-permute-start | bytes 21512 | tf_op jit(solution)/shard_map/ppermute | solution.py:593
  56.0 20.5 %collective-permute-start.2 = (bf16[64,2048]{1,0:T(8,128)(2,1)}, bf16[64,2048]{1,0:T(8,128)(2,1)}, u32[]{:S(2)}, u32[]{:S(2)}) collective-permute-start(bf16[64,2048]{1,0:T(8,128)(2,1)} %slice.286), channel_id=1, source_target_pairs={{0,16},{4,20},{8,24},{12,28},{16,0},{20,4},{24,8},{28,12},{1,17},{... | collective-permute-start | bytes 786440 | tf_op jit(solution)/shard_map/ppermute | solution.py:593
  58.3 18.2 %collective-permute-start.3 = (bf16[64,2048]{1,0:T(8,128)(2,1)}, bf16[64,2048]{1,0:T(8,128)(2,1)}, u32[]{:S(2)}, u32[]{:S(2)}) collective-permute-start(bf16[64,2048]{1,0:T(8,128)(2,1)} %slice.287), channel_id=1, source_target_pairs={{0,8},{4,12},{8,0},{12,4},{16,24},{20,28},{24,16},{28,20},{1,9},{5... | collective-permute-start | bytes 786440 | tf_op jit(solution)/shard_map/ppermute | solution.py:593
  73.1 12.9 %collective-permute-start.4 = (bf16[128,2048]{1,0:T(8,128)(2,1)S(1)}, bf16[128,2048]{1,0:T(8,128)(2,1)S(1)}, u32[]{:S(2)}, u32[]{:S(2)}) collective-permute-start(bf16[128,2048]{1,0:T(8,128)(2,1)S(1)} %bitcast.67), channel_id=1, source_target_pairs={{0,4},{4,0},{8,12},{12,8},{16,20},{20,16},{24,28},{28,24},{1,5},{5... | collective-permute-start | bytes 1572872 | tf_op jit(solution)/shard_map/ppermute | solution.py:593
  73.9 12.1 %collective-permute-start.5 = (bf16[128,2048]{1,0:T(8,128)(2,1)S(1)}, bf16[128,2048]{1,0:T(8,128)(2,1)}, u32[]{:S(2)}, u32[]{:S(2)}) collective-permute-start(bf16[128,2048]{1,0:T(8,128)(2,1)S(1)} %collective-permute-done.refs_1_), channel_id=1, source_target_pairs={{0,4},{4,0},{8,12},{12,8},{16,20},{20,16},{24,28},{28,24},{1,5},{5... | collective-permute-start | bytes 1572872 | tf_op jit(solution)/shard_map/ppermute | solution.py:593
  76.5 9.5 %collective-permute-start.6 = (bf16[128,2048]{1,0:T(8,128)(2,1)S(1)}, bf16[128,2048]{1,0:T(8,128)(2,1)}, u32[]{:S(2)}, u32[]{:S(2)}) collective-permute-start(bf16[128,2048]{1,0:T(8,128)(2,1)S(1)} %collective-permute-done.1.refs_2_), channel_id=1, source_target_pairs={{0,4},{4,0},{8,12},{12,8},{16,20},{20,16},{24,28},{28,24},{1,5},{5... | collective-permute-start | bytes 1572872 | tf_op jit(solution)/shard_map/ppermute | solution.py:593
  76.5 9.5 %collective-permute-start.7 = (bf16[64,2048]{1,0:T(8,128)(2,1)}, bf16[64,2048]{1,0:T(8,128)(2,1)}, u32[]{:S(2)}, u32[]{:S(2)}) collective-permute-start(bf16[64,2048]{1,0:T(8,128)(2,1)} %collective-permute-done.2.refs_3_), channel_id=1, source_target_pairs={{0,4},{4,0},{8,12},{12,8},{16,20},{20,16},{24,28},{28,24},{1,5},{5... | collective-permute-start | bytes 786440 | tf_op jit(solution)/shard_map/ppermute | solution.py:593
  87.3 184.7 %all-gather.9.cloned.1.call-start = ((), (), s32[]{:S(2)}) async-start(), calls=%async_computation.9 | async-start | bytes 3604480 | tf_op jit(solution)/shard_map/all_gather | solution.py:659
  141.0 14.9 %collective-permute-start.17 = (bf16[128,2048]{1,0:T(8,128)(2,1)S(1)}, bf16[128,2048]{1,0:T(8,128)(2,1)S(1)}, u32[]{:S(2)}, u32[]{:S(2)}) collective-permute-start(bf16[128,2048]{1,0:T(8,128)(2,1)S(1)} %pad_maximum_fusion), channel_id=1, source_target_pairs={{0,8},{4,12},{8,0},{12,4},{16,24},{20,28},{24,16},{28,20},{1,9},{5... | collective-permute-start | bytes 1572872 | tf_op jit(solution)/shard_map/ppermute | solution.py:593
  142.6 15.0 %collective-permute-start.19 = (bf16[128,2048]{1,0:T(8,128)(2,1)S(1)}, bf16[128,2048]{1,0:T(8,128)(2,1)}, u32[]{:S(2)}, u32[]{:S(2)}) collective-permute-start(bf16[128,2048]{1,0:T(8,128)(2,1)S(1)} %pad_maximum_fusion.1), channel_id=1, source_target_pairs={{0,16},{4,20},{8,24},{12,28},{16,0},{20,4},{24,8},{28,12},{1,17},{... | collective-permute-start | bytes 1572872 | tf_op jit(solution)/shard_map/ppermute | solution.py:593
  144.3 191.7 %reduce-scatter.5.cloned.1.call-start = ((), (), s32[]{:S(2)}) async-start(), calls=%async_computation.10 | async-start | bytes 3604480 | tf_op jit(solution)/shard_map/reduce_scatter | solution.py:662
  144.6 22.5 %collective-permute-start.29 = (bf16[128,2048]{1,0:T(8,128)(2,1)}, bf16[128,2048]{1,0:T(8,128)(2,1)S(1)}, u32[]{:S(2)}, u32[]{:S(2)}) collective-permute-start(bf16[128,2048]{1,0:T(8,128)(2,1)} %in_turn.15.refs_10_), channel_id=1, source_target_pairs={{0,8},{4,12},{8,0},{12,4},{16,24},{20,28},{24,16},{28,20},{1,9},{5... | collective-permute-start | bytes 1572872 | tf_op jit(solution)/shard_map/ppermute | solution.py:593
  145.2 24.0 %collective-permute-start.30 = (bf16[128,2048]{1,0:T(8,128)(2,1)}, bf16[128,2048]{1,0:T(8,128)(2,1)S(1)}, u32[]{:S(2)}, u32[]{:S(2)}) collective-permute-start(bf16[128,2048]{1,0:T(8,128)(2,1)} %in_turn.15.refs_10_), channel_id=1, source_target_pairs={{0,16},{4,20},{8,24},{12,28},{16,0},{20,4},{24,8},{28,12},{1,17},{... | collective-permute-start | bytes 1572872 | tf_op jit(solution)/shard_map/ppermute | solution.py:593
  160.0 23.9 %collective-permute-start.20 = (bf16[128,2048]{1,0:T(8,128)(2,1)S(1)}, bf16[128,2048]{1,0:T(8,128)(2,1)S(1)}, u32[]{:S(2)}, u32[]{:S(2)}) collective-permute-start(bf16[128,2048]{1,0:T(8,128)(2,1)S(1)} %add_convert_fusion.refs_0_), channel_id=1, source_target_pairs={{0,8},{4,12},{8,0},{12,4},{16,24},{20,28},{24,16},{28,20},{1,9},{5... | collective-permute-start | bytes 1572872 | tf_op jit(solution)/shard_map/ppermute | solution.py:593
  167.2 16.8 %collective-permute-start.21 = (bf16[128,2048]{1,0:T(8,128)(2,1)S(1)}, bf16[128,2048]{1,0:T(8,128)(2,1)S(1)}, u32[]{:S(2)}, u32[]{:S(2)}) collective-permute-start(bf16[128,2048]{1,0:T(8,128)(2,1)S(1)} %add_convert_fusion.refs_0_), channel_id=1, source_target_pairs={{0,16},{4,20},{8,24},{12,28},{16,0},{20,4},{24,8},{28,12},{1,17},{... | collective-permute-start | bytes 1572872 | tf_op jit(solution)/shard_map/ppermute | solution.py:593
  167.8 15.6 %collective-permute-start.31 = (bf16[64,2048]{1,0:T(8,128)(2,1)S(1)}, bf16[64,2048]{1,0:T(8,128)(2,1)S(1)}, u32[]{:S(2)}, u32[]{:S(2)}) collective-permute-start(bf16[64,2048]{1,0:T(8,128)(2,1)S(1)} %slice.297), channel_id=1, source_target_pairs={{0,16},{4,20},{8,24},{12,28},{16,0},{20,4},{24,8},{28,12},{1,17},{... | collective-permute-start | bytes 786440 | tf_op jit(solution)/shard_map/ppermute | solution.py:593
  169.3 14.1 %collective-permute-start.32 = (bf16[64,2048]{1,0:T(8,128)(2,1)S(1)}, bf16[64,2048]{1,0:T(8,128)(2,1)S(1)}, u32[]{:S(2)}, u32[]{:S(2)}) collective-permute-start(bf16[64,2048]{1,0:T(8,128)(2,1)S(1)} %slice.298), channel_id=1, source_target_pairs={{0,8},{4,12},{8,0},{12,4},{16,24},{20,28},{24,16},{28,20},{1,9},{5... | collective-permute-start | bytes 786440 | tf_op jit(solution)/shard_map/ppermute | solution.py:593
  170.8 13.6 %collective-permute-start.33 = (bf16[128,2048]{1,0:T(8,128)(2,1)S(1)}, bf16[128,2048]{1,0:T(8,128)(2,1)S(1)}, u32[]{:S(2)}, u32[]{:S(2)}) collective-permute-start(bf16[128,2048]{1,0:T(8,128)(2,1)S(1)} %copy-done.21), channel_id=1, source_target_pairs={{0,4},{4,0},{8,12},{12,8},{16,20},{20,16},{24,28},{28,24},{1,5},{5... | collective-permute-start | bytes 1572872 | tf_op jit(solution)/shard_map/ppermute | solution.py:593
  184.5 10.8 %collective-permute-start.24 = (bf16[128,2048]{1,0:T(8,128)(2,1)S(1)}, bf16[128,2048]{1,0:T(8,128)(2,1)S(1)}, u32[]{:S(2)}, u32[]{:S(2)}) collective-permute-start(bf16[128,2048]{1,0:T(8,128)(2,1)S(1)} %add_convert_fusion.refs_0_), channel_id=1, source_target_pairs={{0,4},{4,0},{8,12},{12,8},{16,20},{20,16},{24,28},{28,24},{1,5},{5... | collective-permute-start | bytes 1572872 | tf_op jit(solution)/shard_map/ppermute | solution.py:593
  188.3 9.9 %collective-permute-start.26 = (bf16[128,2048]{1,0:T(8,128)(2,1)S(1)}, bf16[128,2048]{1,0:T(8,128)(2,1)}, u32[]{:S(2)}, u32[]{:S(2)}) collective-permute-start(bf16[128,2048]{1,0:T(8,128)(2,1)S(1)} %collective-permute-done.21.refs_2_), channel_id=1, source_target_pairs={{0,4},{4,0},{8,12},{12,8},{16,20},{20,16},{24,28},{28,24},{1,5},{5... | collective-permute-start | bytes 1572872 | tf_op jit(solution)/shard_map/ppermute | solution.py:593
  236.0 203.8 %reduce-scatter.9.cloned.1.call-start = ((), (), s32[]{:S(2)}) async-start(), calls=%async_computation.12 | async-start | bytes 7208960 | tf_op jit(solution)/shard_map/reduce_scatter | solution.py:662
  302.5 193.9 %reduce-scatter.7.cloned.1.call-start = ((), (), s32[]{:S(2)}) async-start(), calls=%async_computation.11 | async-start | bytes 3932160 | tf_op jit(solution)/shard_map/reduce_scatter | solution.py:662
  320.6 13.0 %collective-permute-start.40 = (bf16[128,2048]{1,0:T(8,128)(2,1)S(1)}, bf16[128,2048]{1,0:T(8,128)(2,1)S(1)}, u32[]{:S(2)}, u32[]{:S(2)}) collective-permute-start(bf16[128,2048]{1,0:T(8,128)(2,1)S(1)} %pad_maximum_fusion.2), channel_id=1, source_target_pairs={{0,8},{4,12},{8,0},{12,4},{16,24},{20,28},{24,16},{28,20},{1,9},{5... | collective-permute-start | bytes 1572872 | tf_op jit(solution)/shard_map/ppermute | solution.py:593
  322.2 12.7 %collective-permute-start.42 = (bf16[128,2048]{1,0:T(8,128)(2,1)S(1)}, bf16[128,2048]{1,0:T(8,128)(2,1)S(1)}, u32[]{:S(2)}, u32[]{:S(2)}) collective-permute-start(bf16[128,2048]{1,0:T(8,128)(2,1)S(1)} %pad_maximum_fusion.3), channel_id=1, source_target_pairs={{0,16},{4,20},{8,24},{12,28},{16,0},{20,4},{24,8},{28,12},{1,17},{... | collective-permute-start | bytes 1572872 | tf_op jit(solution)/shard_map/ppermute | solution.py:593
  340.9 11.4 %collective-permute-start.43 = (bf16[128,2048]{1,0:T(8,128)(2,1)S(1)}, bf16[128,2048]{1,0:T(8,128)(2,1)S(1)}, u32[]{:S(2)}, u32[]{:S(2)}) collective-permute-start(bf16[128,2048]{1,0:T(8,128)(2,1)S(1)} %get-tuple-element.129.refs_0_), channel_id=1, source_target_pairs={{0,8},{4,12},{8,0},{12,4},{16,24},{20,28},{24,16},{28,20},{1,9},{5... | collective-permute-start | bytes 1572872 | tf_op jit(solution)/shard_map/ppermute | solution.py:593
  341.5 11.9 %collective-permute-start.44 = (bf16[128,2048]{1,0:T(8,128)(2,1)S(1)}, bf16[128,2048]{1,0:T(8,128)(2,1)S(1)}, u32[]{:S(2)}, u32[]{:S(2)}) collective-permute-start(bf16[128,2048]{1,0:T(8,128)(2,1)S(1)} %get-tuple-element.129.refs_0_), channel_id=1, source_target_pairs={{0,16},{4,20},{8,24},{12,28},{16,0},{20,4},{24,8},{28,12},{1,17},{... | collective-permute-start | bytes 1572872 | tf_op jit(solution)/shard_map/ppermute | solution.py:593
  341.8 19.1 %collective-permute-start.47 = (bf16[128,2048]{1,0:T(8,128)(2,1)S(1)}, bf16[128,2048]{1,0:T(8,128)(2,1)S(1)}, u32[]{:S(2)}, u32[]{:S(2)}) collective-permute-start(bf16[128,2048]{1,0:T(8,128)(2,1)S(1)} %get-tuple-element.129.refs_0_), channel_id=1, source_target_pairs={{0,4},{4,0},{8,12},{12,8},{16,20},{20,16},{24,28},{28,24},{1,5},{5... | collective-permute-start | bytes 1572872 | tf_op jit(solution)/shard_map/ppermute | solution.py:593
  393.4 22.4 %collective-permute-start.57 = (bf16[512,2048]{1,0:T(8,128)(2,1)}, bf16[512,2048]{1,0:T(8,128)(2,1)}, u32[]{:S(2)}, u32[]{:S(2)}) collective-permute-start(bf16[512,2048]{1,0:T(8,128)(2,1)} %convolution_convert_fusion.4.refs_1_), channel_id=1, source_target_pairs={{0,4},{4,0},{8,12},{12,8},{16,20},{20,16},{24,28},{28,24},{1,5},{5... | collective-permute-start | bytes 6291464 | tf_op jit(solution)/shard_map/ppermute | solution.py:593
  398.8 23.2 %collective-permute-start.52 = (bf16[512,2048]{1,0:T(8,128)(2,1)}, bf16[512,2048]{1,0:T(8,128)(2,1)}, u32[]{:S(2)}, u32[]{:S(2)}) collective-permute-start(bf16[512,2048]{1,0:T(8,128)(2,1)} %convolution_convert_fusion.5), channel_id=1, source_target_pairs={{0,4},{4,0},{8,12},{12,8},{16,20},{20,16},{24,28},{28,24},{1,5},{5... | collective-permute-start | bytes 6291464 | tf_op jit(solution)/shard_map/ppermute | solution.py:593
  427.1 9.2 %collective-permute-start.55 = (bf16[64,2048]{1,0:T(8,128)(2,1)S(1)}, bf16[64,2048]{1,0:T(8,128)(2,1)S(1)}, u32[]{:S(2)}, u32[]{:S(2)}) collective-permute-start(bf16[64,2048]{1,0:T(8,128)(2,1)S(1)} %get-tuple-element.149), channel_id=1, source_target_pairs={{0,8},{4,12},{8,0},{12,4},{16,24},{20,28},{24,16},{28,20},{1,9},{5... | collective-permute-start | bytes 786440 | tf_op jit(solution)/shard_map/ppermute | solution.py:593
  429.4 18.3 %collective-permute-start.59 = (bf16[128,2048]{1,0:T(8,128)(2,1)}, bf16[128,2048]{1,0:T(8,128)(2,1)S(1)}, u32[]{:S(2)}, u32[]{:S(2)}) collective-permute-start(bf16[128,2048]{1,0:T(8,128)(2,1)} %pad_maximum_fusion.6), channel_id=1, source_target_pairs={{0,8},{4,12},{8,0},{12,4},{16,24},{20,28},{24,16},{28,20},{1,9},{5... | collective-permute-start | bytes 1572872 | tf_op jit(solution)/shard_map/ppermute | solution.py:593
  432.4 15.2 %collective-permute-start.61 = (bf16[128,2048]{1,0:T(8,128)(2,1)}, bf16[128,2048]{1,0:T(8,128)(2,1)}, u32[]{:S(2)}, u32[]{:S(2)}) collective-permute-start(bf16[128,2048]{1,0:T(8,128)(2,1)} %pad_maximum_fusion.7), channel_id=1, source_target_pairs={{0,16},{4,20},{8,24},{12,28},{16,0},{20,4},{24,8},{28,12},{1,17},{... | collective-permute-start | bytes 1572872 | tf_op jit(solution)/shard_map/ppermute | solution.py:593
  437.4 21.6 %collective-permute-start.54 = (bf16[128,2048]{1,0:T(8,128)(2,1)}, bf16[128,2048]{1,0:T(8,128)(2,1)}, u32[]{:S(2)}, u32[]{:S(2)}) collective-permute-start(bf16[128,2048]{1,0:T(8,128)(2,1)} %pad_maximum_fusion.4), channel_id=1, source_target_pairs={{0,8},{4,12},{8,0},{12,4},{16,24},{20,28},{24,16},{28,20},{1,9},{5... | collective-permute-start | bytes 1572872 | tf_op jit(solution)/shard_map/ppermute | solution.py:593
  438.3 20.7 %collective-permute-start.56 = (bf16[128,2048]{1,0:T(8,128)(2,1)}, bf16[128,2048]{1,0:T(8,128)(2,1)}, u32[]{:S(2)}, u32[]{:S(2)}) collective-permute-start(bf16[128,2048]{1,0:T(8,128)(2,1)} %pad_maximum_fusion.5), channel_id=1, source_target_pairs={{0,16},{4,20},{8,24},{12,28},{16,0},{20,4},{24,8},{28,12},{1,17},{... | collective-permute-start | bytes 1572872 | tf_op jit(solution)/shard_map/ppermute | solution.py:593
  439.8 34.5 %all-to-all-start.3 = ((bf16[8,64,1408]{2,1,0:T(8,128)(2,1)}), bf16[8,64,1408]{2,1,0:T(8,128)(2,1)S(1)}, u32[]{:S(2)}, u32[]{:S(2)}) async-start(bf16[8,64,1408]{2,1,0:T(8,128)(2,1)} %bitcast.79), calls=%async_computation.6 | async-start | bytes 2883584 | tf_op jit(solution)/shard_map/all_to_all | solution.py:665
  443.4 82.5 %reduce-scatter.11.cloned.1.call-start = ((), (), s32[]{:S(2)}) async-start(), calls=%async_computation.13 | async-start | bytes 1310720 | tf_op jit(solution)/shard_map/reduce_scatter | solution.py:662
  452.8 16.5 %collective-permute-start.62 = (f32[16,448]{1,0:T(8,128)S(1)}, f32[16,448]{1,0:T(8,128)S(1)}, u32[]{:S(2)}, u32[]{:S(2)}) collective-permute-start(f32[16,448]{1,0:T(8,128)S(1)} %slice_select_fusion), channel_id=1, source_target_pairs={{0,16},{4,20},{8,24},{12,28},{16,0},{20,4},{24,8},{28,12},{1,17},{... | collective-permute-start | bytes 86024 | tf_op jit(solution)/shard_map/ppermute | solution.py:593
  469.4 27.1 %collective-permute-start.63 = (f32[8,448]{1,0:T(8,128)S(1)}, f32[8,448]{1,0:T(8,128)S(1)}, u32[]{:S(2)}, u32[]{:S(2)}) collective-permute-start(f32[8,448]{1,0:T(8,128)S(1)} %slice_select_fusion.1), channel_id=1, source_target_pairs={{0,8},{4,12},{8,0},{12,4},{16,24},{20,28},{24,16},{28,20},{1,9},{5... | collective-permute-start | bytes 43016 | tf_op jit(solution)/shard_map/ppermute | solution.py:593
  497.8 10.9 %collective-permute-start.65 = (f32[448]{0:T(512)S(1)}, f32[448]{0:T(512)S(1)}, u32[]{:S(2)}, u32[]{:S(2)}) collective-permute-start(f32[448]{0:T(512)S(1)} %bitcast.86), channel_id=1, source_target_pairs={{0,1},{1,0},{2,3},{3,2},{4,5},{5,4},{6,7},{7,6},{8,9},{9,8},{10,11... | collective-permute-start | bytes 5384 | tf_op jit(solution)/shard_map/ppermute | solution.py:712
  498.9 9.9 %collective-permute-start.66 = (f32[448]{0:T(512)S(1)}, f32[448]{0:T(512)S(1)}, u32[]{:S(2)}, u32[]{:S(2)}) collective-permute-start(f32[448]{0:T(512)S(1)} %bitcast.85), channel_id=1, source_target_pairs={{0,2},{1,3},{2,0},{3,1},{4,6},{5,7},{6,4},{7,5},{8,10},{9,11},{10,... | collective-permute-start | bytes 5384 | tf_op jit(solution)/shard_map/ppermute | solution.py:712
  502.2 16.3 %all-to-all-start.2 = ((bf16[8,64,768]{2,1,0:T(8,128)(2,1)}), bf16[8,64,768]{2,1,0:T(8,128)(2,1)S(1)}, u32[]{:S(2)}, u32[]{:S(2)}) async-start(bf16[8,64,768]{2,1,0:T(8,128)(2,1)} %bitcast.77), calls=%async_computation.4 | async-start | bytes 1572864 | tf_op jit(solution)/shard_map/all_to_all | solution.py:665
  (104 other events, 1079.4 us)
Sparse Core Ops, SparseCore 0:
  9.6 30.6 all-gather.6
  42.5 62.9 all-gather.10
  107.6 105.3 all-gather.12
  214.5 57.4 all-gather.8
  274.1 54.8 reduce-scatter.4
  331.2 102.1 reduce-scatter.8
  435.6 60.7 reduce-scatter.6
  498.7 27.1 reduce-scatter.10
